TPU v7x, 1024 devices: a whole 4x4x32 slice. The times are simulated.
1024 devices in a mesh: dp: 64 (over z, core), expert: 16 (over y, x).
Axes of the slice: x: 4, y: 4, z: 32, core: 2. Of those that a mesh axis runs over, the one named last changes fastest.
Arguments:
- tokens: bfloat16 [131072, 1024], P(('dp', 'expert')), may hold values from -24 to 24
- gate_weight: bfloat16 [16, 1024, 768], P('expert'), may hold values from -0.1875 to 0.1875
- up_weight: bfloat16 [16, 1024, 768], P('expert'), may hold values from -0.1875 to 0.1875
- hidden_grad: bfloat16 [64, 16, 256, 768], P('dp', 'expert'), may hold values from -6 to 6
- chosen: int32 [64, 16, 256], P('dp', 'expert'), may hold values from 0 to 2047, as said below
- routes: int32 [131072, 4], P(('dp', 'expert')), may hold values from 0 to 4095, as said below
- route_count: int32 [131072], P(('dp', 'expert')), may hold values from 0 to 4, as said below
Outputs:
- token_grad: bfloat16 [131072, 1024], P(('dp', 'expert'))
- grad_gate: float32 [16, 1024, 768], P('expert', 'dp')
- grad_up: float32 [16, 1024, 768], P('expert', 'dp')
Inputs may be any that keep to these rules, and one draw needn't show every extreme that they name: Each row chosen[g, e] lists 256 different tokens of the group in increasing order; at most 32 of them lie among the 128 tokens of one device, and in every group one device's tokens give exactly 32 to every expert. `routes`: the first route_count[t] entries of token t are the codes e * 256 + k with chosen[g, e, k] = t, in increasing order, each slot once; the other entries are 0. `route_count`: among the tokens of one device the counts differ by at most one; some token has 4.
All inputs are finite; a program needn't handle non-finite values.
Results may differ from a plain program's by a relative error of at most 0.01.
Values may be sent and summed in bfloat16 or wider, within the bound.
No kernel may reach another device: no remote copies, remote signals or barrier semaphores. Data moves between devices by JAX's collectives and lax.ppermute only.
A program may use at most 32 MiB of HBM per device.

v0:
```python
import jax
import jax.numpy as jnp
from jax import lax
from jax.sharding import PartitionSpec as P


def silu_parts(pre_gate):
    squash = jax.nn.sigmoid(pre_gate)
    return (pre_gate * squash, squash * (1.0 + pre_gate * (1.0 - squash)))


def on_device(tokens, gate_weight, up_weight, hidden_grad, chosen, routes, route_count):
    tok_dev, width = tokens.shape
    slot_count = hidden_grad.shape[2]
    hidden = hidden_grad.shape[3]
    route_depth = routes.shape[1]
    peer_count = lax.axis_size("expert")
    groups = lax.axis_size("dp")
    peer_cap = min(tok_dev, 2 * slot_count // peer_count)
    sentinel = peer_count * peer_cap
    route_codes = routes.reshape(-1)
    is_live = (jnp.arange(route_depth, dtype=jnp.int32)[None, :] < route_count[:, None]).reshape(-1)
    owner_expert = route_codes // slot_count
    same_owner = (
        (owner_expert[:, None] == owner_expert[None, :])
        & (route_codes[None, :] < route_codes[:, None])
        & is_live[None, :]
    )
    place_index = jnp.sum(same_owner.astype(jnp.int32), axis=1)
    target = jnp.where(is_live, owner_expert * peer_cap + place_index, sentinel)
    token_index = jnp.arange(tok_dev * route_depth, dtype=jnp.int32) // route_depth
    source_row = jnp.full((sentinel,), tok_dev, jnp.int32).at[target].set(token_index, mode="drop")
    outgoing = jnp.take(tokens, source_row, axis=0, mode="fill", fill_value=0).reshape(
        peer_count, peer_cap, width
    )
    arrived = lax.all_to_all(outgoing, "expert", split_axis=0, concat_axis=0, tiled=True).reshape(
        sentinel, width
    )
    slot_tokens = chosen[0, 0]
    source = slot_tokens // tok_dev
    source_match = (source[:, None] == jnp.arange(peer_count, dtype=jnp.int32)[None, :]).astype(
        jnp.int32
    )
    per_source = jnp.sum(source_match, axis=0)
    source_start = jnp.cumsum(per_source) - per_source
    first_slot = jnp.sum(source_match * source_start[None, :], axis=1)
    slot_row = source * peer_cap + jnp.arange(slot_count, dtype=jnp.int32) - first_slot
    slot_rows = jnp.take(arrived, slot_row, axis=0)
    gate_matrix = gate_weight[0]
    up_matrix = up_weight[0]
    gate_value = jnp.dot(slot_rows, gate_matrix, preferred_element_type=jnp.float32)
    up_value = jnp.dot(slot_rows, up_matrix, preferred_element_type=jnp.float32)
    activated, slope_value = silu_parts(gate_value)
    upstream = hidden_grad[0, 0].astype(jnp.float32)
    gate_delta = (upstream * up_value * slope_value).astype(jnp.bfloat16)
    up_delta = (upstream * activated).astype(jnp.bfloat16)
    combined = jnp.concatenate([gate_delta, up_delta], axis=1)
    contraction = (((1,), (1,)), ((), ()))
    by_slots = (((0,), (0,)), ((), ()))
    slot_grad = (
        lax.dot_general(gate_delta, gate_matrix, contraction, preferred_element_type=jnp.float32)
        + lax.dot_general(up_delta, up_matrix, contraction, preferred_element_type=jnp.float32)
    ).astype(jnp.bfloat16)
    back_rows = jnp.zeros((sentinel, width), jnp.bfloat16).at[slot_row].set(slot_grad)
    returned = lax.all_to_all(
        back_rows.reshape(peer_count, peer_cap, width),
        "expert",
        split_axis=0,
        concat_axis=0,
        tiled=True,
    ).reshape(sentinel, width)
    selected = jnp.take(returned, target, axis=0, mode="fill", fill_value=0).reshape(
        tok_dev, route_depth, width
    )
    token_grad = jnp.sum(selected.astype(jnp.float32), axis=1).astype(jnp.bfloat16)
    norm_factor = jnp.sqrt(jnp.float32(groups * slot_count))
    weight_part = (
        lax.dot_general(slot_rows, combined, by_slots, preferred_element_type=jnp.float32)
        / norm_factor
    )
    summed = lax.psum_scatter(weight_part, "dp", scatter_dimension=0, tiled=True)
    return (token_grad, summed[None, :, :hidden], summed[None, :, hidden:])


def solution(mesh):
    return jax.shard_map(
        on_device,
        mesh=mesh,
        in_specs=(
            P(("dp", "expert"), None),
            P("expert", None, None),
            P("expert", None, None),
            P("dp", "expert", None, None),
            P("dp", "expert", None),
            P(("dp", "expert"), None),
            P(("dp", "expert")),
        ),
        out_specs=(P(("dp", "expert"), None), P("expert", "dp", None), P("expert", "dp", None)),
        check_vma=False,
    )
```

profile of v0, /device:TPU:1, one launch (start us, length us, event | category | flops | bytes accessed | tf_op | source)
XLA Modules:
  0.0 275.9 jit_solution(18158461334494238644)
XLA Ops:
  7.2 0.0 copy-start
  7.2 0.0 copy-start.1
  7.2 0.9 copy.32
  8.1 0.1 reshape.361
  8.2 0.1 reshape.364
  8.3 0.7 iota_compare_fusion.1
  9.0 0.1 copy.33
  9.1 0.1 lt.98
  9.3 0.1 lt.102
  9.4 0.4 convert_reduce_fusion
  9.8 2.4 scatter_custom_fusion
  12.3 0.1 broadcast_in_dim.67
  12.4 0.0 copy-done.1
  12.4 2.1 gather_fusion
  14.5 1.1 broadcast_select_fusion
  15.6 7.7 %all-to-all-start = ((bf16[16,32,1024]{2,1,0:T(8,128)(2,1)}), bf16[16,32,1024]{2,1,0:T(8,128)(2,1)S(1)}, u32[]{:S(2)}, u32[]{:S(2)}) async-start(bf16[16,32,1024]{2,1,0:T(8,128)(2,1)} %broadcast_select_fusion), calls=%async_computation | async-start | bytes 2097152 | tf_op jit(solution)/shard_map/all_to_all | solution.py:36
  23.3 0.0 reduce-scatter.2.cloned.1.call-start
  23.4 0.0 copy-done.4
  23.4 0.1 convert_reduce_fusion.1
  23.5 0.1 copy.36
  23.6 0.1 reduce.1
  23.8 0.1 select_reduce_fusion.1
  23.9 11.6 %all-to-all-done = bf16[16,32,1024]{2,1,0:T(8,128)(2,1)S(1)} async-done(((bf16[16,32,1024]{2,1,0:T(8,128)(2,1)}), bf16[16,32,1024]{2,1,0:T(8,128)(2,1)S(1)}, u32[]{:S(2)}, u32[]{:S(2)}) %all-to-all-start) | async-done | bytes 1048608 | tf_op jit(solution)/shard_map/all_to_all | solution.py:36
  35.5 1.2 gather_fusion.1
  36.7 0.0 copy-done
  36.7 0.0 copy-start.2
  36.7 0.0 copy-start.7
  36.7 1.8 fusion.23
  38.6 0.7 fusion.20
  39.3 3.8 %convolution_multiply_fusion = f32[1024,1536]{1,0:T(8,128)} fusion(bf16[256,768]{1,0:T(8,128)(2,1)S(1)} %get-tuple-element.5, bf16[256,768]{1,0:T(8,128)(2,1)S(1)} %fusion.20, bf16[256,1024]{1,0:T(8,128)(2,1)S(1)} %gather_fusion.1, pred[256]{0:T(512)(128)(4,1)S(1)} %compare_and_fusion.1), kind=kOutput, calls=%fused_computation.5 | convolution fusion | flops 808714240 | bytes 7602432 | tf_op jit(solution)/shard_map/dot_general | solution.py:78
  43.1 0.0 reduce-scatter.2.cloned.1.call-update
  43.1 0.0 copy-start.3
  43.1 0.6 fusion
  43.7 0.8 copy-done.3
  44.5 0.6 fusion.11
  45.1 0.0 copy-start.5
  45.1 0.0 copy-start.6
  45.2 2.7 scatter_custom_fusion.1
  47.8 3.7 %all-to-all-start.1 = ((bf16[16,32,1024]{2,1,0:T(8,128)(2,1)}), bf16[16,32,1024]{2,1,0:T(8,128)(2,1)S(1)}, u32[]{:S(2)}, u32[]{:S(2)}) async-start(bf16[16,32,1024]{2,1,0:T(8,128)(2,1)} %bitcast.55), calls=%async_computation.1 | async-start | bytes 2097152 | tf_op jit(solution)/shard_map/all_to_all | solution.py:65
  51.5 0.1 reduce_sum.46
  51.6 0.1 copy.34
  51.7 0.1 copy.35
  51.9 11.8 %all-to-all-done.1 = bf16[16,32,1024]{2,1,0:T(8,128)(2,1)S(1)} async-done(((bf16[16,32,1024]{2,1,0:T(8,128)(2,1)}), bf16[16,32,1024]{2,1,0:T(8,128)(2,1)S(1)}, u32[]{:S(2)}, u32[]{:S(2)}) %all-to-all-start.1) | async-done | bytes 1048608 | tf_op jit(solution)/shard_map/all_to_all | solution.py:65
  63.6 2.8 %gather_fusion.2 = bf16[512,1024]{1,0:T(8,128)(2,1)} fusion(bf16[512,1024]{1,0:T(8,128)(2,1)S(1)} %bitcast.52, s32[1024]{0:T(1024)S(1)} %pad_clamp_fusion), kind=kCustom, calls=%fused_computation.2 | custom fusion | bytes 2099200 | tf_op jit(solution)/shard_map/jit(_take)/gather | solution.py:72
  66.4 1.5 gather.20
  67.9 1.9 select_reduce_fusion
  69.8 197.8 %reduce-scatter.2.cloned.1.call-done = f32[16,1536]{1,0:T(8,128)} async-done(((f32[1024,1536]{1,0:T(8,128)}), f32[16,1536]{1,0:T(8,128)}) %reduce-scatter.2.cloned.1.call-update) | async-done | bytes 98320 | tf_op jit(solution)/shard_map/reduce_scatter | solution.py:81
  267.6 1.5 slice_bitcast_fusion
  (19 shorter events, 0.2 us)
Async XLA Ops:
  7.2 29.5 %copy-start = (bf16[1,1024,768]{2,1,0:T(8,128)(2,1)S(1)}, bf16[1,1024,768]{2,1,0:T(8,128)(2,1)}, u32[]{:S(2)}) copy-start(bf16[1,1024,768]{2,1,0:T(8,128)(2,1)} %param.8) | copy-start | bytes 4718596
  7.2 5.2 %copy-start.1 = (bf16[128,1024]{1,0:T(8,128)(2,1)S(1)}, bf16[128,1024]{1,0:T(8,128)(2,1)}, u32[]{:S(2)}) copy-start(bf16[128,1024]{1,0:T(8,128)(2,1)} %param.7) | copy-start | bytes 786436
  15.6 7.8 %copy-start.4 = (s32[1,1,256]{2,1,0:T(1,128)S(1)}, s32[1,1,256]{2,1,0:T(1,128)}, u32[]{:S(2)}) copy-start(s32[1,1,256]{2,1,0:T(1,128)} %param.11) | copy-start | bytes 3076
  15.6 19.9 %all-to-all-start = ((bf16[16,32,1024]{2,1,0:T(8,128)(2,1)}), bf16[16,32,1024]{2,1,0:T(8,128)(2,1)S(1)}, u32[]{:S(2)}, u32[]{:S(2)}) async-start(bf16[16,32,1024]{2,1,0:T(8,128)(2,1)} %broadcast_select_fusion), calls=%async_computation | async-start | bytes 2097152 | tf_op jit(solution)/shard_map/all_to_all | solution.py:36
  23.3 244.3 %reduce-scatter.2.cloned.1.call-start = ((), (), s32[]{:S(2)}) async-start(), calls=%async_computation.3 | async-start | bytes 6389760 | tf_op jit(solution)/shard_map/reduce_scatter | solution.py:81
  36.7 1.9 copy-start.2
  36.7 1.9 copy-start.7
  43.1 1.4 copy-start.3
  45.1 6.5 %copy-start.5 = (s32[128,4]{0,1:T(4,128)S(1)}, s32[128,4]{0,1:T(4,128)}, u32[]{:S(2)}) copy-start(s32[128,4]{0,1:T(4,128)} %param.12) | copy-start | bytes 6148
  45.1 6.5 %copy-start.6 = (s32[128]{0:T(128)S(1)}, s32[128]{0:T(128)}, u32[]{:S(2)}) copy-start(s32[128]{0:T(128)} %param.13) | copy-start | bytes 1540
  47.8 15.8 %all-to-all-start.1 = ((bf16[16,32,1024]{2,1,0:T(8,128)(2,1)}), bf16[16,32,1024]{2,1,0:T(8,128)(2,1)S(1)}, u32[]{:S(2)}, u32[]{:S(2)}) async-start(bf16[16,32,1024]{2,1,0:T(8,128)(2,1)} %bitcast.55), calls=%async_computation.1 | async-start | bytes 2097152 | tf_op jit(solution)/shard_map/all_to_all | solution.py:65
Sparse Core Ops, SparseCore 0:
  43.2 224.3 reduce-scatter.1
where the time goes:
time: 279 us; the launch traced here: 276 us
  waiting for transfers between devices  221 us (79%)
  local copies, waits for them, and re-layouts  16.9 us (6%)
  between operations  14.3 us (5%)
  starting transfers between devices  11.4 us (4%)
  matrix products  7.54 us (3%)
  other arithmetic  4.56 us (2%)
    reduce_scatter x1, waiting for transfers between devices, on_device(): lax.psum_scatter(weight_part, 'dp', scatter_dimension=0, tiled=True)  198 us
    all_to_all x1, waiting for transfers between devices, on_device(): lax.all_to_all(back_rows.reshape(peer_count, peer_cap, width), 'expert',...  11.8 us
    all_to_all x1, waiting for transfers between devices, on_device(): lax.all_to_all(outgoing, 'expert', split_axis=0, concat_axis=0, tiled=True)  11.6 us
    all_to_all x1, starting transfers between devices, on_device(): lax.all_to_all(outgoing, 'expert', split_axis=0, concat_axis=0, tiled=True)  7.72 us
  transfers between devices with their start and end apart: 3, of which 3 were waited for; matrix products, arithmetic and copies ran while one was open for 4% of the time, Pallas kernels for 0%

commit v1 on v0

v1 whole, which is shorter than its diff:
```python
import functools

import jax
import jax.numpy as jnp
from jax import lax
from jax.experimental import pallas as pl
from jax.experimental.pallas import tpu as pltpu
from jax.sharding import PartitionSpec as P

FAN = 4


def iota(shape, dim):
    return lax.broadcasted_iota(jnp.int32, shape, dim)


def place_rows(member, cap):
    n, m = member.shape
    ones = member.astype(jnp.float32).astype(jnp.bfloat16)
    before = (iota((m, m), 0) < iota((m, m), 1)).astype(jnp.float32).astype(jnp.bfloat16)
    rank = jnp.dot(ones, before, preferred_element_type=jnp.float32)
    rank = jnp.where(member, rank, -1.0).astype(jnp.int32)
    marks = rank[:, None, :] == iota((n, cap, m), 1)
    return marks.astype(jnp.float32).reshape(n * cap, m).astype(jnp.bfloat16)


def token_marks(routes, count, experts, cap, slots):
    depth, tokens = routes.shape
    rows = iota((experts, tokens), 0)
    member = jnp.zeros((experts, tokens), jnp.int32)
    for r in range(depth):
        owner = jnp.where(count > r, lax.div(routes[r : r + 1], jnp.int32(slots)), -1)
        member = member + (owner == rows).astype(jnp.int32)
    return place_rows(member > 0, cap)


def slot_marks(chosen, sources, cap, tokens):
    source = lax.div(chosen, jnp.int32(tokens))
    return place_rows(source == iota((sources, chosen.shape[1]), 0), cap)


def contract(a, b, dims):
    return lax.dot_general(a, b, (dims, ((), ())), preferred_element_type=jnp.float32)


def dispatch_kernel(experts, cap, slots, tokens_ref, routes_ref, count_ref, out_ref):
    marks = token_marks(routes_ref[...], count_ref[...], experts, cap, slots)
    out_ref[...] = jnp.dot(marks, tokens_ref[...], preferred_element_type=jnp.float32).astype(jnp.bfloat16)


def combine_kernel(experts, cap, slots, back_ref, routes_ref, count_ref, out_ref):
    marks = token_marks(routes_ref[...], count_ref[...], experts, cap, slots)
    out_ref[...] = contract(marks, back_ref[...], ((0,), (0,))).astype(jnp.bfloat16)


def delta_kernel(sources, cap, tokens, arrived_ref, chosen_ref, order_ref, gate_ref, up_ref, grad_ref, mine_ref, send_ref):
    ff = gate_ref.shape[1]
    width = arrived_ref.shape[1]
    half = width // 2
    marks = slot_marks(chosen_ref[...], sources, cap, tokens)
    rows = contract(marks, arrived_ref[...], ((0,), (0,))).astype(jnp.bfloat16)
    gate = jnp.dot(rows, gate_ref[...], preferred_element_type=jnp.float32)
    up = jnp.dot(rows, up_ref[...], preferred_element_type=jnp.float32)
    squash = jax.nn.sigmoid(gate)
    upstream = grad_ref[...].astype(jnp.float32)
    send_ref[:, half : half + ff] = (upstream * up * (squash * (1.0 + gate * (1.0 - squash)))).astype(jnp.bfloat16)
    send_ref[:, half + ff :] = (upstream * (gate * squash)).astype(jnp.bfloat16)
    pick = (iota((width, width), 0) == order_ref[...]).astype(jnp.float32).astype(jnp.bfloat16)
    ordered = jnp.dot(rows, pick, preferred_element_type=jnp.float32).astype(jnp.bfloat16)
    mine_ref[...] = ordered[:, :half]
    send_ref[:, :half] = ordered[:, half:]


def back_kernel(sources, cap, tokens, half, send_ref, chosen_ref, gate_ref, up_ref, out_ref):
    ff = gate_ref.shape[1]
    grad = contract(send_ref[:, half : half + ff], gate_ref[...], ((1,), (1,)))
    grad = grad + contract(send_ref[:, half + ff :], up_ref[...], ((1,), (1,)))
    marks = slot_marks(chosen_ref[...], sources, cap, tokens)
    out_ref[...] = jnp.dot(marks, grad.astype(jnp.bfloat16), preferred_element_type=jnp.float32).astype(jnp.bfloat16)


def weight_kernel(rows, mine_ref, send_ref, got_ref, keep_ref, next_ref, past_ref, far_ref, near_ref):
    half = mine_ref.shape[1]
    block = half // FAN
    ff = (send_ref.shape[1] - half) // 2

    def part(q):
        cols = slice(q * block, (q + 1) * block)
        own = contract(mine_ref[:, cols], send_ref[:, half:], ((0,), (0,)))
        return own + contract(got_ref[:, cols], got_ref[:, half:], ((0,), (0,)))

    two = part(2).astype(jnp.bfloat16)
    far_ref[...] = two[:, :ff]
    near_ref[:rows] = two[block - rows :, ff:]
    near_ref[rows:] = two[: block - rows, ff:]
    next_ref[...] = part(1).astype(jnp.bfloat16)
    past_ref[...] = part(3).astype(jnp.bfloat16)
    keep_ref[...] = part(0)


def call(kernel, outs, *args):
    shapes = [jax.ShapeDtypeStruct(*o) for o in outs]
    return pl.pallas_call(
        kernel,
        out_shape=shapes if len(shapes) > 1 else shapes[0],
        compiler_params=pltpu.CompilerParams(vmem_limit_bytes=40 * 2**20),
    )(*args)


def on_device(tokens, gate_weight, up_weight, hidden_grad, chosen, routes, route_count):
    tok_dev, width = tokens.shape
    slots, ff = hidden_grad.shape[2:]
    peers = lax.axis_size("expert")
    groups = lax.axis_size("dp")
    cap = min(tok_dev, 2 * slots // peers)
    chips = groups // 2
    rows = width // groups
    half = width // 2
    bf16, f32 = jnp.bfloat16, jnp.float32
    place = lax.axis_index("dp")
    z, core = place // 2, place % 2

    def along(value, hops):
        return lax.ppermute(value, "dp", [(i, (i + 2 * hops) % groups) for i in range(groups)])

    routes_t = routes.T
    count = route_count[None, :]
    picked = chosen[0]
    gate, up = gate_weight[0], up_weight[0]

    outgoing = call(functools.partial(dispatch_kernel, peers, cap, slots), [((peers * cap, width), bf16)], tokens, routes_t, count)
    arrived = lax.all_to_all(
        outgoing.reshape(peers, cap, width), "expert", split_axis=0, concat_axis=0, tiled=True
    ).reshape(peers * cap, width)

    m = jnp.arange(width, dtype=jnp.int32)
    block = half // FAN
    which, q, i = m // half, (m % half) // block, (m % block) // rows
    ahead = FAN * i + jnp.where(q == FAN - 1, -1, q)
    owner = (z + ahead + chips) % chips * 2 + jnp.where(which == 0, core, 1 - core)
    order = (owner * rows + m % rows)[None, :]

    mine, send = call(
        functools.partial(delta_kernel, peers, cap, tok_dev),
        [((slots, half), bf16), ((slots, half + 2 * ff), bf16)],
        arrived, picked, order, gate, up, hidden_grad[0, 0],
    )
    got = lax.ppermute(send, "dp", [(d, d ^ 1) for d in range(groups)])
    back = call(
        functools.partial(back_kernel, peers, cap, tok_dev, half), [((peers * cap, width), bf16)], send, picked, gate, up
    )
    keep, ahead_1, past_1, ahead_2, past_2 = call(
        functools.partial(weight_kernel, rows),
        [((block, 2 * ff), f32), ((block, 2 * ff), bf16), ((block, 2 * ff), bf16), ((block, ff), bf16), ((block, ff), bf16)],
        mine, send, got,
    )
    from_far = along(ahead_2, 2)
    from_near = along(past_2, -2)
    from_1 = along(ahead_1, 1)
    from_past = along(past_1, -1)
    part = keep + from_1.astype(f32) + from_past.astype(f32)
    part = part + jnp.concatenate([from_far, from_near], axis=1).astype(f32)

    returned = lax.all_to_all(
        back.reshape(peers, cap, width), "expert", split_axis=0, concat_axis=0, tiled=True
    ).reshape(peers * cap, width)

    part = part.reshape(chips // FAN, rows, 2 * ff)
    n = chips // FAN
    h = n // 2
    right = part[h].astype(bf16)
    left = part[n - h + 1].astype(bf16)
    for t in range(1, h + 1):
        right = along(right, FAN)
        if t < h:
            right = (right.astype(f32) + part[h - t]).astype(bf16)
            left = along(left, -FAN)
            if t < h - 1:
                left = (left.astype(f32) + part[n - h + 1 + t]).astype(bf16)
    summed = (part[0] + right.astype(f32) + left.astype(f32)) / jnp.sqrt(f32(groups * slots))

    token_grad = call(
        functools.partial(combine_kernel, peers, cap, slots), [((tok_dev, width), bf16)], returned, routes_t, count
    )
    return token_grad, summed[None, :, :ff], summed[None, :, ff:]


def solution(mesh):
    return jax.shard_map(
        on_device,
        mesh=mesh,
        in_specs=(
            P(("dp", "expert"), None),
            P("expert", None, None),
            P("expert", None, None),
            P("dp", "expert", None, None),
            P("dp", "expert", None),
            P(("dp", "expert"), None),
            P(("dp", "expert")),
        ),
        out_specs=(P(("dp", "expert"), None), P("expert", "dp", None), P("expert", "dp", None)),
        check_vma=False,
    )
```

time: 279 us -> 130 us (0.47)
  the two profiles are of different devices: /device:TPU:1 before, /device:TPU:2 now
where the time goes in v1:
time: 130 us; the launch traced here: 129 us
  starting transfers between devices  78.6 us (60%)
  waiting for transfers between devices  35.8 us (28%)
  Pallas kernels  7.54 us (6%)
  local copies, waits for them, and re-layouts  5.89 us (5%)
    ppermute x11, starting transfers between devices, along(): lax.ppermute(value, 'dp', [(i, (i + 2 * hops) % groups) for i in range(gr...  53.9 us
    ppermute x11, waiting for transfers between devices, along(): lax.ppermute(value, 'dp', [(i, (i + 2 * hops) % groups) for i in range(gr...  21.1 us
    all_to_all x1, starting transfers between devices, on_device(): lax.all_to_all(outgoing.reshape(peers, cap, width), 'expert', split_axis=...  17.2 us
    all_to_all x1, waiting for transfers between devices, on_device(): lax.all_to_all(outgoing.reshape(peers, cap, width), 'expert', split_axis=...  12.1 us
    pallas_call x5, Pallas kernels, call(): pl.pallas_call(kernel, out_shape=shapes if len(shapes) > 1 else shapes[0]...  7.54 us
    all_to_all x1, starting transfers between devices, on_device(): lax.all_to_all(back.reshape(peers, cap, width), 'expert', split_axis=0, c...  5.52 us
    unnamed x26, local copies, waits for them, and re-layouts  5.23 us
    ppermute x1, waiting for transfers between devices, on_device(): got = lax.ppermute(send, 'dp', [(d, d ^ 1) for d in range(groups)])  2.63 us
  transfers between devices with their start and end apart: 14, of which 8 were waited for; matrix products, arithmetic and copies ran while one was open for 0% of the time, Pallas kernels for 2%

profile of v1, /device:TPU:2, one launch (start us, length us, event | category | flops | bytes accessed | tf_op | source)
XLA Modules:
  0.0 129.0 jit_solution(10195874215612529871)
XLA Ops:
  0.6 0.0 copy-start.5
  0.6 0.9 copy-done.5
  1.6 0.7 copy-done.6
  2.3 0.7 copy-done.9
  2.9 0.5 shard_map.94
  3.5 0.0 copy-start.2
  3.5 1.0 copy-done.2
  4.4 17.2 %all-to-all-start = ((bf16[16,32,1024]{2,1,0:T(8,128)(2,1)}), bf16[16,32,1024]{2,1,0:T(8,128)(2,1)}, u32[]{:S(2)}, u32[]{:S(2)}) async-start(bf16[16,32,1024]{2,1,0:T(8,128)(2,1)} %bitcast.18), calls=%async_computation | async-start | bytes 2097152 | tf_op jit(solution)/shard_map/all_to_all | solution.py:132
  21.7 0.1 fusion.7.order_ref
  21.7 12.1 %all-to-all-done = bf16[16,32,1024]{2,1,0:T(8,128)(2,1)} async-done(((bf16[16,32,1024]{2,1,0:T(8,128)(2,1)}), bf16[16,32,1024]{2,1,0:T(8,128)(2,1)}, u32[]{:S(2)}, u32[]{:S(2)}) %all-to-all-start) | async-done | bytes 1048608 | tf_op jit(solution)/shard_map/all_to_all | solution.py:132
  33.8 0.0 copy-done
  33.8 0.0 copy-done.8
  33.8 0.0 copy-start.4
  33.9 1.0 copy-done.4
  34.8 3.3 %shard_map.95 = (bf16[256,512]{1,0:T(8,128)(2,1)S(1)}, bf16[256,2048]{1,0:T(8,128)(2,1)S(1)}) custom-call(bf16[512,1024]{1,0:T(8,128)(2,1)} %bitcast.3.arrived_ref, s32[1,256]{1,0:T(1,128)S(1)} %bitcast.24, s32[1,1024]{1,0:T(1,128)S(1)} %fusion.7.order_ref, bf16[1024,768]{1,0:T(8,128)(2,1)S(1)} %bitcast.14, bf16[1024,768]{1,0:T(8,128)(2,1)S(1)} %bitcast.16, ...), custom_call_target="tpu_custom_call" | custom-call | tf_op jit(solution)/shard_map/pallas_call | solution.py:103
  38.2 1.9 %collective-permute-start = (bf16[256,2048]{1,0:T(8,128)(2,1)S(1)}, bf16[256,2048]{1,0:T(8,128)(2,1)S(1)}, u32[]{:S(2)}, u32[]{:S(2)}) collective-permute-start(bf16[256,2048]{1,0:T(8,128)(2,1)S(1)} %get-tuple-element.10.send_ref), channel_id=1, source_target_pairs={{0,16},{16,0},{32,48},{48,32},{64,80},{80,64},{96,112},{112,96},{1... | collective-permute-start | bytes 3145736 | tf_op jit(solution)/shard_map/ppermute | solution.py:148
  40.1 2.6 %collective-permute-done.got_ref = bf16[256,2048]{1,0:T(8,128)(2,1)S(1)} collective-permute-done((bf16[256,2048]{1,0:T(8,128)(2,1)S(1)}, bf16[256,2048]{1,0:T(8,128)(2,1)S(1)}, u32[]{:S(2)}, u32[]{:S(2)}) %collective-permute-start) | collective-permute-done | bytes 1048608 | tf_op jit(solution)/shard_map/ppermute | solution.py:148
  42.7 1.0 shard_map.98
  43.8 1.9 %collective-permute-start.1 = (bf16[128,1536]{1,0:T(8,128)(2,1)S(1)}, bf16[128,1536]{1,0:T(8,128)(2,1)S(1)}, u32[]{:S(2)}, u32[]{:S(2)}) collective-permute-start(bf16[128,1536]{1,0:T(8,128)(2,1)S(1)} %get-tuple-element.13), channel_id=1, source_target_pairs={{0,32},{16,48},{32,64},{48,80},{64,96},{80,112},{96,128},{112,144}... | collective-permute-start | bytes 1179656 | tf_op jit(solution)/shard_map/ppermute | solution.py:124
  45.7 12.7 %collective-permute-start.2 = (bf16[128,1536]{1,0:T(8,128)(2,1)S(1)}, bf16[128,1536]{1,0:T(8,128)(2,1)S(1)}, u32[]{:S(2)}, u32[]{:S(2)}) collective-permute-start(bf16[128,1536]{1,0:T(8,128)(2,1)S(1)} %get-tuple-element.14), channel_id=1, source_target_pairs={{0,992},{16,1008},{32,0},{48,16},{64,32},{80,48},{96,64},{112,80},... | collective-permute-start | bytes 1179656 | tf_op jit(solution)/shard_map/ppermute | solution.py:124
  58.4 1.9 %collective-permute-start.3 = (bf16[128,768]{1,0:T(8,128)(2,1)S(1)}, bf16[128,768]{1,0:T(8,128)(2,1)S(1)}, u32[]{:S(2)}, u32[]{:S(2)}) collective-permute-start(bf16[128,768]{1,0:T(8,128)(2,1)S(1)} %get-tuple-element.15), channel_id=1, source_target_pairs={{0,64},{16,80},{32,96},{48,112},{64,128},{80,144},{96,160},{112,17... | collective-permute-start | bytes 589832 | tf_op jit(solution)/shard_map/ppermute | solution.py:124
  60.3 6.0 %collective-permute-start.4 = (bf16[128,768]{1,0:T(8,128)(2,1)S(1)}, bf16[128,768]{1,0:T(8,128)(2,1)S(1)}, u32[]{:S(2)}, u32[]{:S(2)}) collective-permute-start(bf16[128,768]{1,0:T(8,128)(2,1)S(1)} %get-tuple-element.16), channel_id=1, source_target_pairs={{0,960},{16,976},{32,992},{48,1008},{64,0},{80,16},{96,32},{112,48... | collective-permute-start | bytes 589832 | tf_op jit(solution)/shard_map/ppermute | solution.py:124
  66.3 6.7 %collective-permute-done.3 = bf16[128,768]{1,0:T(8,128)(2,1)S(1)} collective-permute-done((bf16[128,768]{1,0:T(8,128)(2,1)S(1)}, bf16[128,768]{1,0:T(8,128)(2,1)S(1)}, u32[]{:S(2)}, u32[]{:S(2)}) %collective-permute-start.3) | collective-permute-done | bytes 196640 | tf_op jit(solution)/shard_map/ppermute | solution.py:124
  73.0 2.4 %collective-permute-done.4 = bf16[128,768]{1,0:T(8,128)(2,1)S(1)} collective-permute-done((bf16[128,768]{1,0:T(8,128)(2,1)S(1)}, bf16[128,768]{1,0:T(8,128)(2,1)S(1)}, u32[]{:S(2)}, u32[]{:S(2)}) %collective-permute-start.4) | collective-permute-done | bytes 196640 | tf_op jit(solution)/shard_map/ppermute | solution.py:124
  75.4 0.0 collective-permute-done.1
  75.4 0.0 collective-permute-done.2
  75.5 0.2 fusion.13
  75.7 1.9 %collective-permute-start.5 = (bf16[16,1536]{1,0:T(8,128)(2,1)S(1)}, bf16[16,1536]{1,0:T(8,128)(2,1)S(1)}, u32[]{:S(2)}, u32[]{:S(2)}) collective-permute-start(bf16[16,1536]{1,0:T(8,128)(2,1)S(1)} %get-tuple-element.21), channel_id=1, source_target_pairs={{0,128},{16,144},{32,160},{48,176},{64,192},{80,208},{96,224},{112... | collective-permute-start | bytes 147464 | tf_op jit(solution)/shard_map/ppermute | solution.py:124
  77.6 8.2 %collective-permute-done.5 = bf16[16,1536]{1,0:T(8,128)(2,1)S(1)} collective-permute-done((bf16[16,1536]{1,0:T(8,128)(2,1)S(1)}, bf16[16,1536]{1,0:T(8,128)(2,1)S(1)}, u32[]{:S(2)}, u32[]{:S(2)}) %collective-permute-start.5) | collective-permute-done | bytes 49184 | tf_op jit(solution)/shard_map/ppermute | solution.py:124
  85.8 2.7 %collective-permute-start.6 = (bf16[16,1536]{1,0:T(8,128)(2,1)S(1)}, bf16[16,1536]{1,0:T(8,128)(2,1)S(1)}, u32[]{:S(2)}, u32[]{:S(2)}) collective-permute-start(bf16[16,1536]{1,0:T(8,128)(2,1)S(1)} %fusion.4), channel_id=1, source_target_pairs={{0,128},{16,144},{32,160},{48,176},{64,192},{80,208},{96,224},{112... | collective-permute-start | bytes 147464 | tf_op jit(solution)/shard_map/ppermute | solution.py:124
  88.5 7.0 %collective-permute-start.9 = (bf16[16,1536]{1,0:T(8,128)(2,1)S(1)}, bf16[16,1536]{1,0:T(8,128)(2,1)S(1)}, u32[]{:S(2)}, u32[]{:S(2)}) collective-permute-start(bf16[16,1536]{1,0:T(8,128)(2,1)S(1)} %get-tuple-element.22), channel_id=1, source_target_pairs={{0,896},{16,912},{32,928},{48,944},{64,960},{80,976},{96,992},{112... | collective-permute-start | bytes 147464 | tf_op jit(solution)/shard_map/ppermute | solution.py:124
  95.6 0.3 collective-permute-done.6
  95.9 3.6 %collective-permute-start.7 = (bf16[16,1536]{1,0:T(8,128)(2,1)S(1)}, bf16[16,1536]{1,0:T(8,128)(2,1)S(1)}, u32[]{:S(2)}, u32[]{:S(2)}) collective-permute-start(bf16[16,1536]{1,0:T(8,128)(2,1)S(1)} %fusion.3), channel_id=1, source_target_pairs={{0,128},{16,144},{32,160},{48,176},{64,192},{80,208},{96,224},{112... | collective-permute-start | bytes 147464 | tf_op jit(solution)/shard_map/ppermute | solution.py:124
  99.5 1.4 %shard_map.96 = bf16[512,1024]{1,0:T(8,128)(2,1)S(1)} custom-call(bf16[256,2048]{1,0:T(8,128)(2,1)S(1)} %get-tuple-element.10.send_ref, s32[1,256]{1,0:T(1,128)S(1)} %bitcast.25, bf16[1024,768]{1,0:T(8,128)(2,1)S(1)} %bitcast.15, bf16[1024,768]{1,0:T(8,128)(2,1)S(1)} %bitcast.17), custom_call_target="tpu_custom_call" | custom-call | tf_op jit(solution)/shard_map/pallas_call | solution.py:103
  101.0 0.0 copy-start.3
  101.0 1.0 copy-done.3
  102.0 5.5 %all-to-all-start.1 = ((bf16[16,32,1024]{2,1,0:T(8,128)(2,1)}), bf16[16,32,1024]{2,1,0:T(8,128)(2,1)S(1)}, u32[]{:S(2)}, u32[]{:S(2)}) async-start(bf16[16,32,1024]{2,1,0:T(8,128)(2,1)} %bitcast.20), calls=%async_computation.1 | async-start | bytes 2097152 | tf_op jit(solution)/shard_map/all_to_all | solution.py:164
  107.5 0.0 collective-permute-done.9
  107.5 0.0 collective-permute-done.7
  107.5 6.9 %collective-permute-start.10 = (bf16[16,1536]{1,0:T(8,128)(2,1)S(1)}, bf16[16,1536]{1,0:T(8,128)(2,1)S(1)}, u32[]{:S(2)}, u32[]{:S(2)}) collective-permute-start(bf16[16,1536]{1,0:T(8,128)(2,1)S(1)} %get-tuple-element.20), channel_id=1, source_target_pairs={{0,896},{16,912},{32,928},{48,944},{64,960},{80,976},{96,992},{112... | collective-permute-start | bytes 147464 | tf_op jit(solution)/shard_map/ppermute | solution.py:124
  114.5 2.8 %collective-permute-start.8 = (bf16[16,1536]{1,0:T(8,128)(2,1)S(1)}, bf16[16,1536]{1,0:T(8,128)(2,1)S(1)}, u32[]{:S(2)}, u32[]{:S(2)}) collective-permute-start(bf16[16,1536]{1,0:T(8,128)(2,1)S(1)} %get-tuple-element.19), channel_id=1, source_target_pairs={{0,128},{16,144},{32,160},{48,176},{64,192},{80,208},{96,224},{112... | collective-permute-start | bytes 147464 | tf_op jit(solution)/shard_map/ppermute | solution.py:124
  117.3 0.7 collective-permute-done.10
  118.0 6.4 %collective-permute-start.11 = (bf16[16,1536]{1,0:T(8,128)(2,1)S(1)}, bf16[16,1536]{1,0:T(8,128)(2,1)S(1)}, u32[]{:S(2)}, u32[]{:S(2)}) collective-permute-start(bf16[16,1536]{1,0:T(8,128)(2,1)S(1)} %fusion), channel_id=1, source_target_pairs={{0,896},{16,912},{32,928},{48,944},{64,960},{80,976},{96,992},{112... | collective-permute-start | bytes 147464 | tf_op jit(solution)/shard_map/ppermute | solution.py:124
  124.4 0.0 all-to-all-done.1
  124.4 1.2 shard_map.97
  125.6 0.0 collective-permute-done.8
  125.6 2.8 %collective-permute-done.11 = bf16[16,1536]{1,0:T(8,128)(2,1)S(1)} collective-permute-done((bf16[16,1536]{1,0:T(8,128)(2,1)S(1)}, bf16[16,1536]{1,0:T(8,128)(2,1)S(1)}, u32[]{:S(2)}, u32[]{:S(2)}) %collective-permute-start.11) | collective-permute-done | bytes 49184 | tf_op jit(solution)/shard_map/ppermute | solution.py:124
  128.4 0.6 slice_bitcast_fusion
  (20 shorter events, 0.1 us)
Async XLA Ops:
  0.6 1.0 copy-start.5
  1.6 0.7 copy-start.6
  2.3 0.7 copy-start.9
  2.9 30.9 %copy-start = (bf16[1,1024,768]{2,1,0:T(8,128)(2,1)S(1)}, bf16[1,1024,768]{2,1,0:T(8,128)(2,1)}, u32[]{:S(2)}) copy-start(bf16[1,1024,768]{2,1,0:T(8,128)(2,1)} %param.8) | copy-start | bytes 4718596
  2.9 30.9 %copy-start.1 = (bf16[1,1024,768]{2,1,0:T(8,128)(2,1)S(1)}, bf16[1,1024,768]{2,1,0:T(8,128)(2,1)}, u32[]{:S(2)}) copy-start(bf16[1,1024,768]{2,1,0:T(8,128)(2,1)} %param.9) | copy-start | bytes 4718596
  2.9 30.9 %copy-start.8 = (s32[1,1,256]{2,1,0:T(1,128)S(1)}, s32[1,1,256]{2,1,0:T(1,128)}, u32[]{:S(2)}) copy-start(s32[1,1,256]{2,1,0:T(1,128)} %param.11) | copy-start | bytes 3076
  3.5 1.0 copy-start.2
  4.4 29.4 %all-to-all-start = ((bf16[16,32,1024]{2,1,0:T(8,128)(2,1)}), bf16[16,32,1024]{2,1,0:T(8,128)(2,1)}, u32[]{:S(2)}, u32[]{:S(2)}) async-start(bf16[16,32,1024]{2,1,0:T(8,128)(2,1)} %bitcast.18), calls=%async_computation | async-start | bytes 2097152 | tf_op jit(solution)/shard_map/all_to_all | solution.py:132
  33.8 1.0 copy-start.4
  38.2 4.6 %collective-permute-start = (bf16[256,2048]{1,0:T(8,128)(2,1)S(1)}, bf16[256,2048]{1,0:T(8,128)(2,1)S(1)}, u32[]{:S(2)}, u32[]{:S(2)}) collective-permute-start(bf16[256,2048]{1,0:T(8,128)(2,1)S(1)} %get-tuple-element.10.send_ref), channel_id=1, source_target_pairs={{0,16},{16,0},{32,48},{48,32},{64,80},{80,64},{96,112},{112,96},{1... | collective-permute-start | bytes 3145736 | tf_op jit(solution)/shard_map/ppermute | solution.py:148
  43.8 31.7 %collective-permute-start.1 = (bf16[128,1536]{1,0:T(8,128)(2,1)S(1)}, bf16[128,1536]{1,0:T(8,128)(2,1)S(1)}, u32[]{:S(2)}, u32[]{:S(2)}) collective-permute-start(bf16[128,1536]{1,0:T(8,128)(2,1)S(1)} %get-tuple-element.13), channel_id=1, source_target_pairs={{0,32},{16,48},{32,64},{48,80},{64,96},{80,112},{96,128},{112,144}... | collective-permute-start | bytes 1179656 | tf_op jit(solution)/shard_map/ppermute | solution.py:124
  45.7 29.8 %collective-permute-start.2 = (bf16[128,1536]{1,0:T(8,128)(2,1)S(1)}, bf16[128,1536]{1,0:T(8,128)(2,1)S(1)}, u32[]{:S(2)}, u32[]{:S(2)}) collective-permute-start(bf16[128,1536]{1,0:T(8,128)(2,1)S(1)} %get-tuple-element.14), channel_id=1, source_target_pairs={{0,992},{16,1008},{32,0},{48,16},{64,32},{80,48},{96,64},{112,80},... | collective-permute-start | bytes 1179656 | tf_op jit(solution)/shard_map/ppermute | solution.py:124
  58.4 14.7 %collective-permute-start.3 = (bf16[128,768]{1,0:T(8,128)(2,1)S(1)}, bf16[128,768]{1,0:T(8,128)(2,1)S(1)}, u32[]{:S(2)}, u32[]{:S(2)}) collective-permute-start(bf16[128,768]{1,0:T(8,128)(2,1)S(1)} %get-tuple-element.15), channel_id=1, source_target_pairs={{0,64},{16,80},{32,96},{48,112},{64,128},{80,144},{96,160},{112,17... | collective-permute-start | bytes 589832 | tf_op jit(solution)/shard_map/ppermute | solution.py:124
  60.3 15.2 %collective-permute-start.4 = (bf16[128,768]{1,0:T(8,128)(2,1)S(1)}, bf16[128,768]{1,0:T(8,128)(2,1)S(1)}, u32[]{:S(2)}, u32[]{:S(2)}) collective-permute-start(bf16[128,768]{1,0:T(8,128)(2,1)S(1)} %get-tuple-element.16), channel_id=1, source_target_pairs={{0,960},{16,976},{32,992},{48,1008},{64,0},{80,16},{96,32},{112,48... | collective-permute-start | bytes 589832 | tf_op jit(solution)/shard_map/ppermute | solution.py:124
  75.6 20.3 %copy-start.11 = (f32[128,1536]{1,0:T(8,128)}, f32[128,1536]{1,0:T(8,128)S(1)}, u32[]{:S(2)}) copy-start(f32[128,1536]{1,0:T(8,128)S(1)} %get-tuple-element.18) | copy-start | bytes 2359300
  75.7 10.2 %collective-permute-start.5 = (bf16[16,1536]{1,0:T(8,128)(2,1)S(1)}, bf16[16,1536]{1,0:T(8,128)(2,1)S(1)}, u32[]{:S(2)}, u32[]{:S(2)}) collective-permute-start(bf16[16,1536]{1,0:T(8,128)(2,1)S(1)} %get-tuple-element.21), channel_id=1, source_target_pairs={{0,128},{16,144},{32,160},{48,176},{64,192},{80,208},{96,224},{112... | collective-permute-start | bytes 147464 | tf_op jit(solution)/shard_map/ppermute | solution.py:124
  85.8 10.1 %collective-permute-start.6 = (bf16[16,1536]{1,0:T(8,128)(2,1)S(1)}, bf16[16,1536]{1,0:T(8,128)(2,1)S(1)}, u32[]{:S(2)}, u32[]{:S(2)}) collective-permute-start(bf16[16,1536]{1,0:T(8,128)(2,1)S(1)} %fusion.4), channel_id=1, source_target_pairs={{0,128},{16,144},{32,160},{48,176},{64,192},{80,208},{96,224},{112... | collective-permute-start | bytes 147464 | tf_op jit(solution)/shard_map/ppermute | solution.py:124
  88.5 18.9 %collective-permute-start.9 = (bf16[16,1536]{1,0:T(8,128)(2,1)S(1)}, bf16[16,1536]{1,0:T(8,128)(2,1)S(1)}, u32[]{:S(2)}, u32[]{:S(2)}) collective-permute-start(bf16[16,1536]{1,0:T(8,128)(2,1)S(1)} %get-tuple-element.22), channel_id=1, source_target_pairs={{0,896},{16,912},{32,928},{48,944},{64,960},{80,976},{96,992},{112... | collective-permute-start | bytes 147464 | tf_op jit(solution)/shard_map/ppermute | solution.py:124
  95.9 11.6 %collective-permute-start.7 = (bf16[16,1536]{1,0:T(8,128)(2,1)S(1)}, bf16[16,1536]{1,0:T(8,128)(2,1)S(1)}, u32[]{:S(2)}, u32[]{:S(2)}) collective-permute-start(bf16[16,1536]{1,0:T(8,128)(2,1)S(1)} %fusion.3), channel_id=1, source_target_pairs={{0,128},{16,144},{32,160},{48,176},{64,192},{80,208},{96,224},{112... | collective-permute-start | bytes 147464 | tf_op jit(solution)/shard_map/ppermute | solution.py:124
  101.0 1.0 copy-start.3
  102.0 5.5 %copy-start.12 = (f32[128,1536]{1,0:T(8,128)S(1)}, f32[128,1536]{1,0:T(8,128)}, u32[]{:S(2)}) copy-start(f32[128,1536]{1,0:T(8,128)} %copy-done.11) | copy-start | bytes 2359300
  102.0 22.4 %copy-start.7 = (s32[128,4]{0,1:T(4,128)S(1)}, s32[128,4]{0,1:T(4,128)}, u32[]{:S(2)}) copy-start(s32[128,4]{0,1:T(4,128)} %param.12) | copy-start | bytes 6148
  102.0 22.4 %copy-start.10 = (s32[128]{0:T(128)S(1)}, s32[128]{0:T(128)}, u32[]{:S(2)}) copy-start(s32[128]{0:T(128)} %param.13) | copy-start | bytes 1540
  102.0 22.4 %all-to-all-start.1 = ((bf16[16,32,1024]{2,1,0:T(8,128)(2,1)}), bf16[16,32,1024]{2,1,0:T(8,128)(2,1)S(1)}, u32[]{:S(2)}, u32[]{:S(2)}) async-start(bf16[16,32,1024]{2,1,0:T(8,128)(2,1)} %bitcast.20), calls=%async_computation.1 | async-start | bytes 2097152 | tf_op jit(solution)/shard_map/all_to_all | solution.py:164
  107.5 10.4 %collective-permute-start.10 = (bf16[16,1536]{1,0:T(8,128)(2,1)S(1)}, bf16[16,1536]{1,0:T(8,128)(2,1)S(1)}, u32[]{:S(2)}, u32[]{:S(2)}) collective-permute-start(bf16[16,1536]{1,0:T(8,128)(2,1)S(1)} %get-tuple-element.20), channel_id=1, source_target_pairs={{0,896},{16,912},{32,928},{48,944},{64,960},{80,976},{96,992},{112... | collective-permute-start | bytes 147464 | tf_op jit(solution)/shard_map/ppermute | solution.py:124
  114.5 11.1 %collective-permute-start.8 = (bf16[16,1536]{1,0:T(8,128)(2,1)S(1)}, bf16[16,1536]{1,0:T(8,128)(2,1)S(1)}, u32[]{:S(2)}, u32[]{:S(2)}) collective-permute-start(bf16[16,1536]{1,0:T(8,128)(2,1)S(1)} %get-tuple-element.19), channel_id=1, source_target_pairs={{0,128},{16,144},{32,160},{48,176},{64,192},{80,208},{96,224},{112... | collective-permute-start | bytes 147464 | tf_op jit(solution)/shard_map/ppermute | solution.py:124
  118.0 10.4 %collective-permute-start.11 = (bf16[16,1536]{1,0:T(8,128)(2,1)S(1)}, bf16[16,1536]{1,0:T(8,128)(2,1)S(1)}, u32[]{:S(2)}, u32[]{:S(2)}) collective-permute-start(bf16[16,1536]{1,0:T(8,128)(2,1)S(1)} %fusion), channel_id=1, source_target_pairs={{0,896},{16,912},{32,928},{48,944},{64,960},{80,976},{96,992},{112... | collective-permute-start | bytes 147464 | tf_op jit(solution)/shard_map/ppermute | solution.py:124

commit v2 on v1

v2 whole, which is shorter than its diff:
```python
import functools

import jax
import jax.numpy as jnp
from jax import lax
from jax.experimental import pallas as pl
from jax.experimental.pallas import tpu as pltpu
from jax.sharding import PartitionSpec as P

FAN = 4
TIE = 2
BLOCKS = 4


def iota(shape, dim):
    return lax.broadcasted_iota(jnp.int32, shape, dim)


def place_rows(member, cap):
    n, m = member.shape
    ones = member.astype(jnp.float32).astype(jnp.bfloat16)
    before = (iota((m, m), 0) < iota((m, m), 1)).astype(jnp.float32).astype(jnp.bfloat16)
    rank = jnp.dot(ones, before, preferred_element_type=jnp.float32)
    rank = jnp.where(member, rank, -1.0).astype(jnp.int32)
    marks = rank[:, None, :] == iota((n, cap, m), 1)
    return marks.astype(jnp.float32).reshape(n * cap, m).astype(jnp.bfloat16)


def token_marks(routes, count, experts, cap, slots):
    depth, tokens = routes.shape
    rows = iota((experts, tokens), 0)
    member = jnp.zeros((experts, tokens), jnp.int32)
    for r in range(depth):
        owner = jnp.where(count > r, lax.div(routes[r : r + 1], jnp.int32(slots)), -1)
        member = member + (owner == rows).astype(jnp.int32)
    return place_rows(member > 0, cap)


def slot_marks(chosen, sources, cap, tokens):
    source = lax.div(chosen, jnp.int32(tokens))
    return place_rows(source == iota((sources, chosen.shape[1]), 0), cap)


def contract(a, b, dims):
    return lax.dot_general(a, b, (dims, ((), ())), preferred_element_type=jnp.float32)


def fetch(pairs, sems):
    copies = [pltpu.make_async_copy(src, dst, sems.at[i]) for i, (src, dst) in enumerate(pairs)]
    for copy in copies:
        copy.start()
    return copies


def marked_rows(marks, rows, out_ref, stage_ref, sems):
    size = marks.shape[0] // BLOCKS
    copies = []
    for i in range(BLOCKS):
        span = pl.ds(i * size, size)
        block = jnp.dot(marks[i * size : (i + 1) * size], rows, preferred_element_type=jnp.float32)
        stage_ref[span] = block.astype(jnp.bfloat16)
        copies.append(pltpu.make_async_copy(stage_ref.at[span], out_ref.at[span], sems.at[i]))
        copies[-1].start()
    for copy in copies:
        copy.wait()


def dispatch_kernel(experts, cap, slots, tokens_hbm, routes_hbm, count_hbm, out_ref, tokens_ref, routes_ref, count_ref, stage_ref, in_sems, out_sems):
    tokens_in, routes_in, count_in = fetch(
        [(tokens_hbm, tokens_ref), (routes_hbm, routes_ref), (count_hbm, count_ref)], in_sems
    )
    routes_in.wait()
    count_in.wait()
    marks = token_marks(routes_ref[...], count_ref[...], experts, cap, slots)
    tokens_in.wait()
    marked_rows(marks, tokens_ref[...], out_ref, stage_ref, out_sems)


def combine_kernel(experts, cap, slots, back_ref, routes_ref, count_ref, out_ref):
    marks = token_marks(routes_ref[...], count_ref[...], experts, cap, slots)
    out_ref[...] = contract(marks, back_ref[...], ((0,), (0,))).astype(jnp.bfloat16)


def delta_kernel(sources, cap, tokens, arrived_ref, chosen_ref, order_ref, gate_hbm, up_hbm, grad_hbm, mine_ref, send_ref, gate_ref, up_ref, grad_ref, sems):
    ff = gate_ref.shape[1]
    width = arrived_ref.shape[1]
    half = width // 2
    gate_in, up_in, grad_in = fetch([(gate_hbm, gate_ref), (up_hbm, up_ref), (grad_hbm, grad_ref)], sems)
    marks = slot_marks(chosen_ref[...], sources, cap, tokens)
    rows = contract(marks, arrived_ref[...], ((0,), (0,))).astype(jnp.bfloat16)
    pick = (iota((width, width), 0) == order_ref[...]).astype(jnp.float32).astype(jnp.bfloat16)
    gate_in.wait()
    gate = jnp.dot(rows, gate_ref[...], preferred_element_type=jnp.float32)
    up_in.wait()
    up = jnp.dot(rows, up_ref[...], preferred_element_type=jnp.float32)
    squash = jax.nn.sigmoid(gate)
    grad_in.wait()
    upstream = grad_ref[...].astype(jnp.float32)
    send_ref[:, half : half + ff] = (upstream * up * (squash * (1.0 + gate * (1.0 - squash)))).astype(jnp.bfloat16)
    send_ref[:, half + ff :] = (upstream * (gate * squash)).astype(jnp.bfloat16)
    ordered = jnp.dot(rows, pick, preferred_element_type=jnp.float32).astype(jnp.bfloat16)
    mine_ref[...] = ordered[:, :half]
    send_ref[:, :half] = ordered[:, half:]


def back_kernel(sources, cap, tokens, half, send_ref, chosen_ref, gate_ref, up_ref, after_ref, out_ref, stage_ref, sems):
    del after_ref
    ff = gate_ref.shape[1]
    grad = contract(send_ref[:, half : half + ff], gate_ref[...], ((1,), (1,)))
    grad = grad + contract(send_ref[:, half + ff :], up_ref[...], ((1,), (1,)))
    marks = slot_marks(chosen_ref[...], sources, cap, tokens)
    marked_rows(marks, grad.astype(jnp.bfloat16), out_ref, stage_ref, sems)


def weight_kernel(mine_ref, send_ref, got_ref, keep_ref, next_ref, past_ref, far_ref):
    half = mine_ref.shape[1]
    block = half // FAN

    def part(q):
        cols = slice(q * block, (q + 1) * block)
        own = contract(mine_ref[:, cols], send_ref[:, half:], ((0,), (0,)))
        return own + contract(got_ref[:, cols], got_ref[:, half:], ((0,), (0,)))

    far_ref[...] = part(2).astype(jnp.bfloat16)
    next_ref[...] = part(1).astype(jnp.bfloat16)
    past_ref[...] = part(3).astype(jnp.bfloat16)
    keep_ref[...] = part(0)


def call(kernel, outs, *args, ins=None, out_space=None, scratch=(), mib=40):
    shapes = [jax.ShapeDtypeStruct(*o) for o in outs]
    spaces = [s or pltpu.VMEM for s in (ins or [None] * len(args))]
    out_specs = [pl.BlockSpec(memory_space=out_space or pltpu.VMEM) for _ in shapes]
    return pl.pallas_call(
        kernel,
        in_specs=[pl.BlockSpec(memory_space=s) for s in spaces],
        out_specs=out_specs if len(shapes) > 1 else out_specs[0],
        out_shape=shapes if len(shapes) > 1 else shapes[0],
        scratch_shapes=list(scratch),
        compiler_params=pltpu.CompilerParams(vmem_limit_bytes=mib * 2**20),
    )(*args)


def on_device(tokens, gate_weight, up_weight, hidden_grad, chosen, routes, route_count):
    tok_dev, width = tokens.shape
    slots, ff = hidden_grad.shape[2:]
    peers = lax.axis_size("expert")
    groups = lax.axis_size("dp")
    cap = min(tok_dev, 2 * slots // peers)
    chips = groups // 2
    rows = width // groups
    half = width // 2
    bf16, f32 = jnp.bfloat16, jnp.float32
    place = lax.axis_index("dp")
    z, core = place // 2, place % 2

    def along(value, hops):
        pairs = [(d, ((d // 2 + (hops if d % 2 == 0 else -hops)) % chips) * 2 + d % 2) for d in range(groups)]
        return lax.ppermute(value, "dp", pairs)

    routes_t = routes.T
    count = route_count[None, :]
    picked = chosen[0]
    gate, up = gate_weight[0], up_weight[0]
    hbm, vmem, dma = pltpu.HBM, pltpu.VMEM, pltpu.SemaphoreType.DMA
    padded = peers * cap

    outgoing = call(
        functools.partial(dispatch_kernel, peers, cap, slots),
        [((padded, width), bf16)],
        tokens, routes_t, count,
        ins=[hbm] * 3,
        out_space=hbm,
        scratch=[
            vmem(tokens.shape, bf16), vmem(routes_t.shape, jnp.int32), vmem(count.shape, jnp.int32),
            vmem((padded, width), bf16), dma((3,)), dma((BLOCKS,)),
        ],
        mib=61,
    )
    arrived = lax.all_to_all(
        outgoing.reshape(peers, cap, width), "expert", split_axis=0, concat_axis=0, tiled=True
    ).reshape(padded, width)

    m = jnp.arange(width, dtype=jnp.int32)
    block = half // FAN
    which, q, i = m // half, (m % half) // block, (m % block) // rows
    ahead = FAN * i + jnp.where(q == FAN - 1, -1, q)
    to_core = jnp.where(which == 0, core, 1 - core)
    owner = (z + jnp.where(to_core == 0, ahead, -ahead) + 2 * chips) % chips * 2 + to_core
    order = (owner * rows + m % rows)[None, :]

    mine, send = call(
        functools.partial(delta_kernel, peers, cap, tok_dev),
        [((slots, half), bf16), ((slots, half + 2 * ff), bf16)],
        arrived, picked, order, gate, up, hidden_grad[0, 0],
        ins=[None] * 3 + [hbm] * 3,
        scratch=[vmem(gate.shape, bf16), vmem(up.shape, bf16), vmem((slots, ff), bf16), dma((3,))],
        mib=50,
    )
    got = lax.ppermute(send, "dp", [(d, d ^ 1) for d in range(groups)])
    keep, ahead_1, past_1, ahead_2 = call(
        weight_kernel,
        [((block, 2 * ff), f32)] + [((block, 2 * ff), bf16)] * 3,
        mine, send, got,
    )
    back = call(
        functools.partial(back_kernel, peers, cap, tok_dev, half),
        [((padded, width), bf16)],
        send, picked, gate, up, keep,
        ins=[None] * 4 + [pl.ANY],
        out_space=hbm,
        scratch=[vmem((padded, width), bf16), dma((BLOCKS,))],
        mib=40,
    )
    from_2 = along(ahead_2, 2)
    from_1 = along(ahead_1, 1)
    from_past = along(past_1, -1)
    returned = lax.all_to_all(
        back.reshape(peers, cap, width), "expert", split_axis=0, concat_axis=0, tiled=True
    )
    part = keep + from_1.astype(f32) + from_past.astype(f32) + from_2.astype(f32)
    part = part.reshape(chips // FAN, rows, 2 * ff)
    n = chips // FAN
    h = n // 2
    right = part[h].astype(bf16)
    left = part[n - h + 1].astype(bf16)
    for t in range(1, h + 1):
        right = along(right, FAN)
        if t < h:
            left = along(left, -FAN)
            if t == TIE:
                right, left, returned = lax.optimization_barrier((right, left, returned))
            else:
                right, left = lax.optimization_barrier((right, left))
            right = (right.astype(f32) + part[h - t]).astype(bf16)
            if t < h - 1:
                left = (left.astype(f32) + part[n - h + 1 + t]).astype(bf16)
    summed = (part[0] + right.astype(f32) + left.astype(f32)) / jnp.sqrt(f32(groups * slots))

    token_grad = call(
        functools.partial(combine_kernel, peers, cap, slots),
        [((tok_dev, width), bf16)],
        returned.reshape(padded, width), routes_t, count,
    )
    return token_grad, summed[None, :, :ff], summed[None, :, ff:]


def solution(mesh):
    return jax.shard_map(
        on_device,
        mesh=mesh,
        in_specs=(
            P(("dp", "expert"), None),
            P("expert", None, None),
            P("expert", None, None),
            P("dp", "expert", None, None),
            P("dp", "expert", None),
            P(("dp", "expert"), None),
            P(("dp", "expert")),
        ),
        out_specs=(P(("dp", "expert"), None), P("expert", "dp", None), P("expert", "dp", None)),
        check_vma=False,
    )
```

time: 130 us -> 134 us (1.031)
  the two profiles are of different devices: /device:TPU:2 before, /device:TPU:32 now
where the time goes in v2:
time: 134 us
  waiting for transfers between devices  61 us (46%)
  starting transfers between devices  58.5 us (44%)
  Pallas kernels  11.1 us (8%)
  other arithmetic  1.46 us (1%)
    ppermute x10, starting transfers between devices, along(): return lax.ppermute(value, 'dp', pairs)  45.7 us
    ppermute x10, waiting for transfers between devices, along(): return lax.ppermute(value, 'dp', pairs)  40.8 us
    all_to_all x1, waiting for transfers between devices, on_device(): lax.all_to_all(outgoing.reshape(peers, cap, width), 'expert', split_axis=...  17.6 us
    pallas_call x5, Pallas kernels, call(): pl.pallas_call(kernel, in_specs=[pl.BlockSpec(memory_space=s) for s in sp...  11.1 us
    all_to_all x1, starting transfers between devices, on_device(): lax.all_to_all(outgoing.reshape(peers, cap, width), 'expert', split_axis=...  7.05 us
    all_to_all x1, starting transfers between devices, on_device(): lax.all_to_all(back.reshape(peers, cap, width), 'expert', split_axis=0, c...  3.66 us
  transfers between devices with their start and end apart: 13, of which 10 were waited for; matrix products, arithmetic and copies ran while one was open for 1% of the time, Pallas kernels for 3%

profile of v2, /device:TPU:32, one launch (start us, length us, event | category | flops | bytes accessed | tf_op | source)
XLA Modules:
  0.0 133.6 jit_solution(6882191213741772731)
XLA Ops:
  0.6 0.0 copy-start.2
  0.6 0.0 copy-start.4
  0.7 2.3 %shard_map.94 = bf16[512,1024]{1,0:T(8,128)(2,1)} custom-call(bf16[128,1024]{1,0:T(8,128)(2,1)} %tokens_hbm.1, s32[4,128]{1,0:T(4,128)} %bitcast.21, s32[1,128]{1,0:T(1,128)} %bitcast.25), custom_call_target="tpu_custom_call" | custom-call | tf_op jit(solution)/shard_map/pallas_call | solution.py:134
  3.0 7.0 %all-to-all-start = ((bf16[16,32,1024]{2,1,0:T(8,128)(2,1)}), bf16[16,32,1024]{2,1,0:T(8,128)(2,1)S(1)}, u32[]{:S(2)}, u32[]{:S(2)}) async-start(bf16[16,32,1024]{2,1,0:T(8,128)(2,1)} %bitcast.27), calls=%async_computation | async-start | bytes 2097152 | tf_op jit(solution)/shard_map/all_to_all | solution.py:180
  10.0 0.1 fusion.7.order_ref
  10.1 17.6 %all-to-all-done = bf16[16,32,1024]{2,1,0:T(8,128)(2,1)S(1)} async-done(((bf16[16,32,1024]{2,1,0:T(8,128)(2,1)}), bf16[16,32,1024]{2,1,0:T(8,128)(2,1)S(1)}, u32[]{:S(2)}, u32[]{:S(2)}) %all-to-all-start) | async-done | bytes 1048608 | tf_op jit(solution)/shard_map/all_to_all | solution.py:180
  27.6 0.0 copy-done.2
  27.7 0.0 copy-done.4
  27.7 0.0 copy-start.1
  27.7 4.3 %shard_map.95 = (bf16[256,512]{1,0:T(8,128)(2,1)S(1)}, bf16[256,2048]{1,0:T(8,128)(2,1)S(1)}) custom-call(bf16[512,1024]{1,0:T(8,128)(2,1)S(1)} %bitcast.19, s32[1,256]{1,0:T(1,128)S(1)} %bitcast.23, s32[1,1024]{1,0:T(1,128)S(1)} %fusion.7.order_ref, bf16[1024,768]{1,0:T(8,128)(2,1)} %bitcast.14, bf16[1024,768]{1,0:T(8,128)(2,1)} %bitcast.16, ...), custom_call_target="tpu_custom_call" | custom-call | tf_op jit(solution)/shard_map/pallas_call | solution.py:134
  32.0 0.0 copy-start
  32.0 2.1 %collective-permute-start = (bf16[256,2048]{1,0:T(8,128)(2,1)S(1)}, bf16[256,2048]{1,0:T(8,128)(2,1)S(1)}, u32[]{:S(2)}, u32[]{:S(2)}) collective-permute-start(bf16[256,2048]{1,0:T(8,128)(2,1)S(1)} %get-tuple-element.17.send_ref), channel_id=1, source_target_pairs={{0,16},{16,0},{32,48},{48,32},{64,80},{80,64},{96,112},{112,96},{1... | collective-permute-start | bytes 3145736 | tf_op jit(solution)/shard_map/ppermute | solution.py:200
  34.0 2.6 %collective-permute-done.got_ref = bf16[256,2048]{1,0:T(8,128)(2,1)S(1)} collective-permute-done((bf16[256,2048]{1,0:T(8,128)(2,1)S(1)}, bf16[256,2048]{1,0:T(8,128)(2,1)S(1)}, u32[]{:S(2)}, u32[]{:S(2)}) %collective-permute-start) | collective-permute-done | bytes 1048608 | tf_op jit(solution)/shard_map/ppermute | solution.py:200
  36.7 1.0 shard_map.96
  37.7 3.8 %collective-permute-start.1 = (bf16[128,1536]{1,0:T(8,128)(2,1)S(1)}, bf16[128,1536]{1,0:T(8,128)(2,1)S(1)}, u32[]{:S(2)}, u32[]{:S(2)}) collective-permute-start(bf16[128,1536]{1,0:T(8,128)(2,1)S(1)} %get-tuple-element.19), channel_id=1, source_target_pairs={{0,32},{16,1008},{32,64},{48,16},{64,96},{80,48},{96,128},{112,80}... | collective-permute-start | bytes 1179656 | tf_op jit(solution)/shard_map/ppermute | solution.py:159
  41.5 5.0 %collective-permute-start.2 = (bf16[128,1536]{1,0:T(8,128)(2,1)S(1)}, bf16[128,1536]{1,0:T(8,128)(2,1)}, u32[]{:S(2)}, u32[]{:S(2)}) collective-permute-start(bf16[128,1536]{1,0:T(8,128)(2,1)S(1)} %get-tuple-element.20), channel_id=1, source_target_pairs={{0,992},{16,48},{32,0},{48,80},{64,32},{80,112},{96,64},{112,144},... | collective-permute-start | bytes 1179656 | tf_op jit(solution)/shard_map/ppermute | solution.py:159
  46.6 3.3 %collective-permute-start.3 = (bf16[128,1536]{1,0:T(8,128)(2,1)S(1)}, bf16[128,1536]{1,0:T(8,128)(2,1)}, u32[]{:S(2)}, u32[]{:S(2)}) collective-permute-start(bf16[128,1536]{1,0:T(8,128)(2,1)S(1)} %get-tuple-element.21), channel_id=1, source_target_pairs={{0,64},{16,976},{32,96},{48,1008},{64,128},{80,16},{96,160},{112,4... | collective-permute-start | bytes 1179656 | tf_op jit(solution)/shard_map/ppermute | solution.py:159
  49.9 0.0 copy-done.1
  49.9 0.0 copy-done
  49.9 2.3 %shard_map.97 = bf16[512,1024]{1,0:T(8,128)(2,1)} custom-call(bf16[256,2048]{1,0:T(8,128)(2,1)S(1)} %get-tuple-element.17.send_ref, s32[1,256]{1,0:T(1,128)S(1)} %bitcast.24, bf16[1024,768]{1,0:T(8,128)(2,1)S(1)} %bitcast.15, bf16[1024,768]{1,0:T(8,128)(2,1)S(1)} %bitcast.17, f32[128,1536]{1,0:T(8,128)S(1)} %get-tuple-element.18.after_ref), custom_call_target="tpu_custom_call" | custom-call | tf_op jit(solution)/shard_map/pallas_call | solution.py:134
  52.2 3.7 %all-to-all-start.1 = ((bf16[16,32,1024]{2,1,0:T(8,128)(2,1)}), bf16[16,32,1024]{2,1,0:T(8,128)(2,1)S(1)}, u32[]{:S(2)}, u32[]{:S(2)}) async-start(bf16[16,32,1024]{2,1,0:T(8,128)(2,1)} %bitcast.8), calls=%async_computation.1 | async-start | bytes 2097152 | tf_op jit(solution)/shard_map/all_to_all | solution.py:218
  55.8 0.0 copy-start.3
  55.9 0.0 copy-start.5
  55.9 0.0 collective-permute-done.1
  55.9 0.0 collective-permute-done.2
  55.9 18.5 %collective-permute-done.3 = bf16[128,1536]{1,0:T(8,128)(2,1)} collective-permute-done((bf16[128,1536]{1,0:T(8,128)(2,1)S(1)}, bf16[128,1536]{1,0:T(8,128)(2,1)}, u32[]{:S(2)}, u32[]{:S(2)}) %collective-permute-start.3) | collective-permute-done | bytes 393248 | tf_op jit(solution)/shard_map/ppermute | solution.py:159
  74.4 1.3 fusion.12
  75.7 6.5 %collective-permute-start.5 = (bf16[16,1536]{1,0:T(8,128)(2,1)S(1)}, bf16[16,1536]{1,0:T(8,128)(2,1)S(1)}, u32[]{:S(2)}, u32[]{:S(2)}) collective-permute-start(bf16[16,1536]{1,0:T(8,128)(2,1)S(1)} %get-tuple-element.35), channel_id=1, source_target_pairs={{0,896},{16,144},{32,928},{48,176},{64,960},{80,208},{96,992},{112... | collective-permute-start | bytes 147464 | tf_op jit(solution)/shard_map/ppermute | solution.py:159
  82.2 3.3 %collective-permute-start.4 = (bf16[16,1536]{1,0:T(8,128)(2,1)S(1)}, bf16[16,1536]{1,0:T(8,128)(2,1)S(1)}, u32[]{:S(2)}, u32[]{:S(2)}) collective-permute-start(bf16[16,1536]{1,0:T(8,128)(2,1)S(1)} %get-tuple-element.36), channel_id=1, source_target_pairs={{0,128},{16,912},{32,160},{48,944},{64,192},{80,976},{96,224},{112... | collective-permute-start | bytes 147464 | tf_op jit(solution)/shard_map/ppermute | solution.py:159
  85.5 0.8 collective-permute-done.5
  86.3 7.0 %collective-permute-done.4 = bf16[16,1536]{1,0:T(8,128)(2,1)S(1)} collective-permute-done((bf16[16,1536]{1,0:T(8,128)(2,1)S(1)}, bf16[16,1536]{1,0:T(8,128)(2,1)S(1)}, u32[]{:S(2)}, u32[]{:S(2)}) %collective-permute-start.4) | collective-permute-done | bytes 49184 | tf_op jit(solution)/shard_map/ppermute | solution.py:159
  93.3 4.4 %collective-permute-start.7 = (bf16[16,1536]{1,0:T(8,128)(2,1)S(1)}, bf16[16,1536]{1,0:T(8,128)(2,1)S(1)}, u32[]{:S(2)}, u32[]{:S(2)}) collective-permute-start(bf16[16,1536]{1,0:T(8,128)(2,1)S(1)} %get-tuple-element.33), channel_id=1, source_target_pairs={{0,896},{16,144},{32,928},{48,176},{64,960},{80,208},{96,992},{112... | collective-permute-start | bytes 147464 | tf_op jit(solution)/shard_map/ppermute | solution.py:159
  97.7 5.4 %collective-permute-start.6 = (bf16[16,1536]{1,0:T(8,128)(2,1)S(1)}, bf16[16,1536]{1,0:T(8,128)(2,1)S(1)}, u32[]{:S(2)}, u32[]{:S(2)}) collective-permute-start(bf16[16,1536]{1,0:T(8,128)(2,1)S(1)} %get-tuple-element.34), channel_id=1, source_target_pairs={{0,128},{16,912},{32,160},{48,944},{64,192},{80,976},{96,224},{112... | collective-permute-start | bytes 147464 | tf_op jit(solution)/shard_map/ppermute | solution.py:159
  103.1 0.7 collective-permute-done.7
  103.8 3.8 %collective-permute-done.6 = bf16[16,1536]{1,0:T(8,128)(2,1)S(1)} collective-permute-done((bf16[16,1536]{1,0:T(8,128)(2,1)S(1)}, bf16[16,1536]{1,0:T(8,128)(2,1)S(1)}, u32[]{:S(2)}, u32[]{:S(2)}) %collective-permute-start.6) | collective-permute-done | bytes 49184 | tf_op jit(solution)/shard_map/ppermute | solution.py:159
  107.6 0.0 all-to-all-done.1
  107.6 5.4 %collective-permute-start.9 = (bf16[16,1536]{1,0:T(8,128)(2,1)S(1)}, bf16[16,1536]{1,0:T(8,128)(2,1)S(1)}, u32[]{:S(2)}, u32[]{:S(2)}) collective-permute-start(bf16[16,1536]{1,0:T(8,128)(2,1)S(1)} %get-tuple-element.31), channel_id=1, source_target_pairs={{0,896},{16,144},{32,928},{48,176},{64,960},{80,208},{96,992},{112... | collective-permute-start | bytes 147464 | tf_op jit(solution)/shard_map/ppermute | solution.py:159
  113.1 4.3 %collective-permute-start.8 = (bf16[16,1536]{1,0:T(8,128)(2,1)S(1)}, bf16[16,1536]{1,0:T(8,128)(2,1)S(1)}, u32[]{:S(2)}, u32[]{:S(2)}) collective-permute-start(bf16[16,1536]{1,0:T(8,128)(2,1)S(1)} %get-tuple-element.32), channel_id=1, source_target_pairs={{0,128},{16,912},{32,160},{48,944},{64,192},{80,976},{96,224},{112... | collective-permute-start | bytes 147464 | tf_op jit(solution)/shard_map/ppermute | solution.py:159
  117.4 0.7 collective-permute-done.9
  118.1 4.9 %collective-permute-done.8 = bf16[16,1536]{1,0:T(8,128)(2,1)S(1)} collective-permute-done((bf16[16,1536]{1,0:T(8,128)(2,1)S(1)}, bf16[16,1536]{1,0:T(8,128)(2,1)S(1)}, u32[]{:S(2)}, u32[]{:S(2)}) %collective-permute-start.8) | collective-permute-done | bytes 49184 | tf_op jit(solution)/shard_map/ppermute | solution.py:159
  123.0 4.3 %collective-permute-start.10 = (bf16[16,1536]{1,0:T(8,128)(2,1)S(1)}, bf16[16,1536]{1,0:T(8,128)(2,1)S(1)}, u32[]{:S(2)}, u32[]{:S(2)}) collective-permute-start(bf16[16,1536]{1,0:T(8,128)(2,1)S(1)} %fusion), channel_id=1, source_target_pairs={{0,128},{16,912},{32,160},{48,944},{64,192},{80,976},{96,224},{112... | collective-permute-start | bytes 147464 | tf_op jit(solution)/shard_map/ppermute | solution.py:159
  127.3 0.0 copy-done.3
  127.3 0.0 copy-done.5
  127.3 1.2 shard_map.98
  128.5 4.4 %collective-permute-done.10 = bf16[16,1536]{1,0:T(8,128)(2,1)S(1)} collective-permute-done((bf16[16,1536]{1,0:T(8,128)(2,1)S(1)}, bf16[16,1536]{1,0:T(8,128)(2,1)S(1)}, u32[]{:S(2)}, u32[]{:S(2)}) %collective-permute-start.10) | collective-permute-done | bytes 49184 | tf_op jit(solution)/shard_map/ppermute | solution.py:159
  132.9 0.6 slice_bitcast_fusion
  (5 shorter events, 0.1 us)
Async XLA Ops:
  0.6 27.0 %copy-start.2 = (bf16[1,1,256,768]{3,2,1,0:T(8,128)(2,1)S(1)}, bf16[1,1,256,768]{3,2,1,0:T(8,128)(2,1)}, u32[]{:S(2)}) copy-start(bf16[1,1,256,768]{3,2,1,0:T(8,128)(2,1)} %param.10) | copy-start | bytes 1179652
  0.6 27.0 %copy-start.4 = (s32[1,1,256]{2,1,0:T(1,128)S(1)}, s32[1,1,256]{2,1,0:T(1,128)}, u32[]{:S(2)}) copy-start(s32[1,1,256]{2,1,0:T(1,128)} %param.11) | copy-start | bytes 3076
  3.0 24.7 %all-to-all-start = ((bf16[16,32,1024]{2,1,0:T(8,128)(2,1)}), bf16[16,32,1024]{2,1,0:T(8,128)(2,1)S(1)}, u32[]{:S(2)}, u32[]{:S(2)}) async-start(bf16[16,32,1024]{2,1,0:T(8,128)(2,1)} %bitcast.27), calls=%async_computation | async-start | bytes 2097152 | tf_op jit(solution)/shard_map/all_to_all | solution.py:180
  27.7 22.2 %copy-start.1 = (bf16[1,1024,768]{2,1,0:T(8,128)(2,1)S(1)}, bf16[1,1024,768]{2,1,0:T(8,128)(2,1)}, u32[]{:S(2)}) copy-start(bf16[1,1024,768]{2,1,0:T(8,128)(2,1)} %param.9) | copy-start | bytes 4718596
  32.0 17.9 %copy-start = (bf16[1,1024,768]{2,1,0:T(8,128)(2,1)S(1)}, bf16[1,1024,768]{2,1,0:T(8,128)(2,1)}, u32[]{:S(2)}) copy-start(bf16[1,1024,768]{2,1,0:T(8,128)(2,1)} %param.8) | copy-start | bytes 4718596
  32.0 4.7 %collective-permute-start = (bf16[256,2048]{1,0:T(8,128)(2,1)S(1)}, bf16[256,2048]{1,0:T(8,128)(2,1)S(1)}, u32[]{:S(2)}, u32[]{:S(2)}) collective-permute-start(bf16[256,2048]{1,0:T(8,128)(2,1)S(1)} %get-tuple-element.17.send_ref), channel_id=1, source_target_pairs={{0,16},{16,0},{32,48},{48,32},{64,80},{80,64},{96,112},{112,96},{1... | collective-permute-start | bytes 3145736 | tf_op jit(solution)/shard_map/ppermute | solution.py:200
  37.7 18.2 %collective-permute-start.1 = (bf16[128,1536]{1,0:T(8,128)(2,1)S(1)}, bf16[128,1536]{1,0:T(8,128)(2,1)S(1)}, u32[]{:S(2)}, u32[]{:S(2)}) collective-permute-start(bf16[128,1536]{1,0:T(8,128)(2,1)S(1)} %get-tuple-element.19), channel_id=1, source_target_pairs={{0,32},{16,1008},{32,64},{48,16},{64,96},{80,48},{96,128},{112,80}... | collective-permute-start | bytes 1179656 | tf_op jit(solution)/shard_map/ppermute | solution.py:159
  41.5 14.4 %collective-permute-start.2 = (bf16[128,1536]{1,0:T(8,128)(2,1)S(1)}, bf16[128,1536]{1,0:T(8,128)(2,1)}, u32[]{:S(2)}, u32[]{:S(2)}) collective-permute-start(bf16[128,1536]{1,0:T(8,128)(2,1)S(1)} %get-tuple-element.20), channel_id=1, source_target_pairs={{0,992},{16,48},{32,0},{48,80},{64,32},{80,112},{96,64},{112,144},... | collective-permute-start | bytes 1179656 | tf_op jit(solution)/shard_map/ppermute | solution.py:159
  46.6 27.8 %collective-permute-start.3 = (bf16[128,1536]{1,0:T(8,128)(2,1)S(1)}, bf16[128,1536]{1,0:T(8,128)(2,1)}, u32[]{:S(2)}, u32[]{:S(2)}) collective-permute-start(bf16[128,1536]{1,0:T(8,128)(2,1)S(1)} %get-tuple-element.21), channel_id=1, source_target_pairs={{0,64},{16,976},{32,96},{48,1008},{64,128},{80,16},{96,160},{112,4... | collective-permute-start | bytes 1179656 | tf_op jit(solution)/shard_map/ppermute | solution.py:159
  52.2 55.4 %all-to-all-start.1 = ((bf16[16,32,1024]{2,1,0:T(8,128)(2,1)}), bf16[16,32,1024]{2,1,0:T(8,128)(2,1)S(1)}, u32[]{:S(2)}, u32[]{:S(2)}) async-start(bf16[16,32,1024]{2,1,0:T(8,128)(2,1)} %bitcast.8), calls=%async_computation.1 | async-start | bytes 2097152 | tf_op jit(solution)/shard_map/all_to_all | solution.py:218
  55.8 71.5 %copy-start.3 = (s32[128,4]{0,1:T(4,128)S(1)}, s32[128,4]{0,1:T(4,128)}, u32[]{:S(2)}) copy-start(s32[128,4]{0,1:T(4,128)} %param.12) | copy-start | bytes 6148
  55.9 71.5 %copy-start.5 = (s32[128]{0:T(128)S(1)}, s32[128]{0:T(128)}, u32[]{:S(2)}) copy-start(s32[128]{0:T(128)} %param.13) | copy-start | bytes 1540
  75.7 10.5 %collective-permute-start.5 = (bf16[16,1536]{1,0:T(8,128)(2,1)S(1)}, bf16[16,1536]{1,0:T(8,128)(2,1)S(1)}, u32[]{:S(2)}, u32[]{:S(2)}) collective-permute-start(bf16[16,1536]{1,0:T(8,128)(2,1)S(1)} %get-tuple-element.35), channel_id=1, source_target_pairs={{0,896},{16,144},{32,928},{48,176},{64,960},{80,208},{96,992},{112... | collective-permute-start | bytes 147464 | tf_op jit(solution)/shard_map/ppermute | solution.py:159
  82.2 11.1 %collective-permute-start.4 = (bf16[16,1536]{1,0:T(8,128)(2,1)S(1)}, bf16[16,1536]{1,0:T(8,128)(2,1)S(1)}, u32[]{:S(2)}, u32[]{:S(2)}) collective-permute-start(bf16[16,1536]{1,0:T(8,128)(2,1)S(1)} %get-tuple-element.36), channel_id=1, source_target_pairs={{0,128},{16,912},{32,160},{48,944},{64,192},{80,976},{96,224},{112... | collective-permute-start | bytes 147464 | tf_op jit(solution)/shard_map/ppermute | solution.py:159
  93.3 10.5 %collective-permute-start.7 = (bf16[16,1536]{1,0:T(8,128)(2,1)S(1)}, bf16[16,1536]{1,0:T(8,128)(2,1)S(1)}, u32[]{:S(2)}, u32[]{:S(2)}) collective-permute-start(bf16[16,1536]{1,0:T(8,128)(2,1)S(1)} %get-tuple-element.33), channel_id=1, source_target_pairs={{0,896},{16,144},{32,928},{48,176},{64,960},{80,208},{96,992},{112... | collective-permute-start | bytes 147464 | tf_op jit(solution)/shard_map/ppermute | solution.py:159
  97.7 9.9 %collective-permute-start.6 = (bf16[16,1536]{1,0:T(8,128)(2,1)S(1)}, bf16[16,1536]{1,0:T(8,128)(2,1)S(1)}, u32[]{:S(2)}, u32[]{:S(2)}) collective-permute-start(bf16[16,1536]{1,0:T(8,128)(2,1)S(1)} %get-tuple-element.34), channel_id=1, source_target_pairs={{0,128},{16,912},{32,160},{48,944},{64,192},{80,976},{96,224},{112... | collective-permute-start | bytes 147464 | tf_op jit(solution)/shard_map/ppermute | solution.py:159
  107.6 10.4 %collective-permute-start.9 = (bf16[16,1536]{1,0:T(8,128)(2,1)S(1)}, bf16[16,1536]{1,0:T(8,128)(2,1)S(1)}, u32[]{:S(2)}, u32[]{:S(2)}) collective-permute-start(bf16[16,1536]{1,0:T(8,128)(2,1)S(1)} %get-tuple-element.31), channel_id=1, source_target_pairs={{0,896},{16,144},{32,928},{48,176},{64,960},{80,208},{96,992},{112... | collective-permute-start | bytes 147464 | tf_op jit(solution)/shard_map/ppermute | solution.py:159
  113.1 9.9 %collective-permute-start.8 = (bf16[16,1536]{1,0:T(8,128)(2,1)S(1)}, bf16[16,1536]{1,0:T(8,128)(2,1)S(1)}, u32[]{:S(2)}, u32[]{:S(2)}) collective-permute-start(bf16[16,1536]{1,0:T(8,128)(2,1)S(1)} %get-tuple-element.32), channel_id=1, source_target_pairs={{0,128},{16,912},{32,160},{48,944},{64,192},{80,976},{96,224},{112... | collective-permute-start | bytes 147464 | tf_op jit(solution)/shard_map/ppermute | solution.py:159
  123.0 9.9 %collective-permute-start.10 = (bf16[16,1536]{1,0:T(8,128)(2,1)S(1)}, bf16[16,1536]{1,0:T(8,128)(2,1)S(1)}, u32[]{:S(2)}, u32[]{:S(2)}) collective-permute-start(bf16[16,1536]{1,0:T(8,128)(2,1)S(1)} %fusion), channel_id=1, source_target_pairs={{0,128},{16,912},{32,160},{48,944},{64,192},{80,976},{96,224},{112... | collective-permute-start | bytes 147464 | tf_op jit(solution)/shard_map/ppermute | solution.py:159

commit v3 on v2

--- a/solution.py
+++ b/solution.py
@@ -8,7 +8,7 @@
 from jax.sharding import PartitionSpec as P
 
 FAN = 4
-TIE = 2
+TIE = 3
 BLOCKS = 4
 
 
@@ -81,14 +81,18 @@
     out_ref[...] = contract(marks, back_ref[...], ((0,), (0,))).astype(jnp.bfloat16)
 
 
-def delta_kernel(sources, cap, tokens, arrived_ref, chosen_ref, order_ref, gate_hbm, up_hbm, grad_hbm, mine_ref, send_ref, gate_ref, up_ref, grad_ref, sems):
+def select_kernel(sources, cap, tokens, chosen_ref, order_ref, marks_ref, pick_ref):
+    marks_ref[...] = slot_marks(chosen_ref[...], sources, cap, tokens)
+    pick_ref[...] = (iota(pick_ref.shape, 0) == order_ref[...]).astype(jnp.float32).astype(jnp.bfloat16)
+
+
+def delta_kernel(arrived_ref, marks_ref, gate_hbm, up_hbm, grad_hbm, pick_hbm, mine_ref, send_ref, gate_ref, up_ref, grad_ref, pick_ref, sems):
     ff = gate_ref.shape[1]
-    width = arrived_ref.shape[1]
-    half = width // 2
-    gate_in, up_in, grad_in = fetch([(gate_hbm, gate_ref), (up_hbm, up_ref), (grad_hbm, grad_ref)], sems)
-    marks = slot_marks(chosen_ref[...], sources, cap, tokens)
-    rows = contract(marks, arrived_ref[...], ((0,), (0,))).astype(jnp.bfloat16)
-    pick = (iota((width, width), 0) == order_ref[...]).astype(jnp.float32).astype(jnp.bfloat16)
+    half = arrived_ref.shape[1] // 2
+    gate_in, up_in, grad_in, pick_in = fetch(
+        [(gate_hbm, gate_ref), (up_hbm, up_ref), (grad_hbm, grad_ref), (pick_hbm, pick_ref)], sems
+    )
+    rows = contract(marks_ref[...], arrived_ref[...], ((0,), (0,))).astype(jnp.bfloat16)
     gate_in.wait()
     gate = jnp.dot(rows, gate_ref[...], preferred_element_type=jnp.float32)
     up_in.wait()
@@ -98,21 +102,24 @@
     upstream = grad_ref[...].astype(jnp.float32)
     send_ref[:, half : half + ff] = (upstream * up * (squash * (1.0 + gate * (1.0 - squash)))).astype(jnp.bfloat16)
     send_ref[:, half + ff :] = (upstream * (gate * squash)).astype(jnp.bfloat16)
-    ordered = jnp.dot(rows, pick, preferred_element_type=jnp.float32).astype(jnp.bfloat16)
+    pick_in.wait()
+    ordered = jnp.dot(rows, pick_ref[...], preferred_element_type=jnp.float32).astype(jnp.bfloat16)
     mine_ref[...] = ordered[:, :half]
     send_ref[:, :half] = ordered[:, half:]
 
 
-def back_kernel(sources, cap, tokens, half, send_ref, chosen_ref, gate_ref, up_ref, after_ref, out_ref, stage_ref, sems):
+def back_kernel(half, send_ref, marks_ref, gate_hbm, up_hbm, out_ref, gate_ref, up_ref, stage_ref, in_sems, out_sems):
+    ff = gate_ref.shape[1]
+    gate_in, up_in = fetch([(gate_hbm, gate_ref), (up_hbm, up_ref)], in_sems)
+    gate_in.wait()
+    grad = contract(send_ref[:, half : half + ff], gate_ref[...], ((1,), (1,)))
+    up_in.wait()
+    grad = grad + contract(send_ref[:, half + ff :], up_ref[...], ((1,), (1,)))
+    marked_rows(marks_ref[...], grad.astype(jnp.bfloat16), out_ref, stage_ref, out_sems)
+
+
+def weight_kernel(mine_ref, send_ref, got_ref, after_ref, keep_ref, next_ref, past_ref, far_ref):
     del after_ref
-    ff = gate_ref.shape[1]
-    grad = contract(send_ref[:, half : half + ff], gate_ref[...], ((1,), (1,)))
-    grad = grad + contract(send_ref[:, half + ff :], up_ref[...], ((1,), (1,)))
-    marks = slot_marks(chosen_ref[...], sources, cap, tokens)
-    marked_rows(marks, grad.astype(jnp.bfloat16), out_ref, stage_ref, sems)
-
-
-def weight_kernel(mine_ref, send_ref, got_ref, keep_ref, next_ref, past_ref, far_ref):
     half = mine_ref.shape[1]
     block = half // FAN
 
@@ -158,6 +165,10 @@
         pairs = [(d, ((d // 2 + (hops if d % 2 == 0 else -hops)) % chips) * 2 + d % 2) for d in range(groups)]
         return lax.ppermute(value, "dp", pairs)
 
+    def swap(value):
+        return lax.ppermute(value, "dp", [(d, d ^ 1) for d in range(groups)])
+
+    n = chips // 2 // FAN
     routes_t = routes.T
     count = route_count[None, :]
     picked = chosen[0]
@@ -183,59 +194,63 @@
 
     m = jnp.arange(width, dtype=jnp.int32)
     block = half // FAN
-    which, q, i = m // half, (m % half) // block, (m % block) // rows
-    ahead = FAN * i + jnp.where(q == FAN - 1, -1, q)
+    which, q, i = m // half, (m % half) // block, (m % block) // (2 * rows)
     to_core = jnp.where(which == 0, core, 1 - core)
-    owner = (z + jnp.where(to_core == 0, ahead, -ahead) + 2 * chips) % chips * 2 + to_core
-    order = (owner * rows + m % rows)[None, :]
+    last = jnp.where(to_core == 0, chips // 2, 0)
+    ahead = jnp.where(q > 0, FAN * i + q, jnp.where(i == n - 1, last, FAN * (i + 1)))
+    owner = (z + jnp.where(to_core == 0, ahead, -ahead) + chips) % chips
+    order = (owner * 2 * rows + m % (2 * rows))[None, :]
+    marks, pick = call(
+        functools.partial(select_kernel, peers, cap, tok_dev),
+        [((padded, slots), bf16), ((width, width), bf16)],
+        picked, order,
+        mib=60,
+    )
 
     mine, send = call(
-        functools.partial(delta_kernel, peers, cap, tok_dev),
+        delta_kernel,
         [((slots, half), bf16), ((slots, half + 2 * ff), bf16)],
-        arrived, picked, order, gate, up, hidden_grad[0, 0],
-        ins=[None] * 3 + [hbm] * 3,
-        scratch=[vmem(gate.shape, bf16), vmem(up.shape, bf16), vmem((slots, ff), bf16), dma((3,))],
+        arrived, marks, gate, up, hidden_grad[0, 0], pick,
+        ins=[None] * 2 + [hbm] * 4,
+        scratch=[vmem(gate.shape, bf16), vmem(up.shape, bf16), vmem((slots, ff), bf16), vmem(pick.shape, bf16), dma((4,))],
         mib=50,
     )
-    got = lax.ppermute(send, "dp", [(d, d ^ 1) for d in range(groups)])
-    keep, ahead_1, past_1, ahead_2 = call(
+    got = swap(send)
+    back = call(
+        functools.partial(back_kernel, half),
+        [((padded, width), bf16)],
+        send, marks, gate, up,
+        ins=[None] * 2 + [hbm] * 2,
+        out_space=hbm,
+        scratch=[vmem(gate.shape, bf16), vmem(up.shape, bf16), vmem((padded, width), bf16), dma((2,)), dma((BLOCKS,))],
+        mib=50,
+    )
+    keep, to_1, to_past, to_2 = call(
         weight_kernel,
         [((block, 2 * ff), f32)] + [((block, 2 * ff), bf16)] * 3,
-        mine, send, got,
-    )
-    back = call(
-        functools.partial(back_kernel, peers, cap, tok_dev, half),
-        [((padded, width), bf16)],
-        send, picked, gate, up, keep,
-        ins=[None] * 4 + [pl.ANY],
-        out_space=hbm,
-        scratch=[vmem((padded, width), bf16), dma((BLOCKS,))],
+        mine, send, got, back,
+        ins=[None] * 3 + [pl.ANY],
         mib=40,
     )
-    from_2 = along(ahead_2, 2)
-    from_1 = along(ahead_1, 1)
-    from_past = along(past_1, -1)
-    returned = lax.all_to_all(
-        back.reshape(peers, cap, width), "expert", split_axis=0, concat_axis=0, tiled=True
-    )
-    part = keep + from_1.astype(f32) + from_past.astype(f32) + from_2.astype(f32)
-    part = part.reshape(chips // FAN, rows, 2 * ff)
-    n = chips // FAN
-    h = n // 2
-    right = part[h].astype(bf16)
-    left = part[n - h + 1].astype(bf16)
-    for t in range(1, h + 1):
-        right = along(right, FAN)
-        if t < h:
-            left = along(left, -FAN)
-            if t == TIE:
-                right, left, returned = lax.optimization_barrier((right, left, returned))
-            else:
-                right, left = lax.optimization_barrier((right, left))
-            right = (right.astype(f32) + part[h - t]).astype(bf16)
-            if t < h - 1:
-                left = (left.astype(f32) + part[n - h + 1 + t]).astype(bf16)
-    summed = (part[0] + right.astype(f32) + left.astype(f32)) / jnp.sqrt(f32(groups * slots))
+    from_2, from_1, from_past = [
+        v.reshape(n, 2 * rows, 2 * ff).astype(f32) for v in (along(to_2, 2), along(to_1, 1), along(to_past, -1))
+    ]
+    own = keep.reshape(n, 2 * rows, 2 * ff)
+    terms = [from_1[0] + from_2[0] + jnp.where(core == 1, own[n - 1], 0.0)]
+    terms += [own[a - 1] + from_1[a] + from_2[a] + from_past[a - 1] for a in range(1, n)]
+    total = from_past[n - 1] + jnp.where(core == 0, own[n - 1], 0.0)
+    total = total.astype(bf16)
+    total, back = lax.optimization_barrier((total, back))
+    returned = lax.all_to_all(back.reshape(peers, cap, width), "expert", split_axis=0, concat_axis=0, tiled=True)
+    for t in range(1, n + 1):
+        total = along(total, FAN)
+        if t == TIE:
+            total, returned = lax.optimization_barrier((total, returned))
+        total = total.astype(f32) + terms[n - t]
+        total = total.astype(bf16) if t < n else total
+    low, high = total[:rows], total[rows:]
+    other = swap(jnp.where(core == 0, high, low).astype(bf16))
+    summed = (jnp.where(core == 0, low, high) + other.astype(f32)) / jnp.sqrt(f32(groups * slots))
 
     token_grad = call(
         functools.partial(combine_kernel, peers, cap, slots),

time: 134 us -> 124 us (0.925)
  the two profiles are of different devices: /device:TPU:32 before, /device:TPU:97 now
where the time goes in v3:
time: 124 us; the launch traced here: 123 us
  starting transfers between devices  74.8 us (60%)
  waiting for transfers between devices  22.9 us (18%)
  Pallas kernels  15.8 us (13%)
  other arithmetic  6.82 us (6%)
  local copies, waits for them, and re-layouts  1.62 us (1%)
    ppermute x7, starting transfers between devices, along(): return lax.ppermute(value, 'dp', pairs)  49.5 us
    pallas_call x6, Pallas kernels, call(): pl.pallas_call(kernel, in_specs=[pl.BlockSpec(memory_space=s) for s in sp...  15.8 us
    ppermute x2, starting transfers between devices, swap(): return lax.ppermute(value, 'dp', [(d, d ^ 1) for d in range(groups)])  14.9 us
    all_to_all x1, waiting for transfers between devices, on_device(): lax.all_to_all(outgoing.reshape(peers, cap, width), 'expert', split_axis=...  12.1 us
    ppermute x7, waiting for transfers between devices, along(): return lax.ppermute(value, 'dp', pairs)  10.8 us
    all_to_all x1, starting transfers between devices, on_device(): lax.all_to_all(outgoing.reshape(peers, cap, width), 'expert', split_axis=...  6.77 us
    all_to_all x1, starting transfers between devices, on_device(): lax.all_to_all(back.reshape(peers, cap, width), 'expert', split_axis=0, c...  3.66 us
    convert_element_type x3, other arithmetic, on_device(): total = total.astype(bf16) if t < n else total  2.66 us
  transfers between devices with their start and end apart: 11, of which 5 were waited for; matrix products, arithmetic and copies ran while one was open for 3% of the time, Pallas kernels for 7%

profile of v3, /device:TPU:97, one launch (start us, length us, event | category | flops | bytes accessed | tf_op | source)
XLA Modules:
  0.0 122.9 jit_solution(279220006898207255)
XLA Ops:
  0.6 0.0 copy-start.2
  0.6 2.3 %shard_map.94 = bf16[512,1024]{1,0:T(8,128)(2,1)} custom-call(bf16[128,1024]{1,0:T(8,128)(2,1)} %tokens_hbm.1, s32[4,128]{1,0:T(4,128)} %bitcast.19, s32[1,128]{1,0:T(1,128)} %bitcast.21), custom_call_target="tpu_custom_call" | custom-call | tf_op jit(solution)/shard_map/pallas_call | solution.py:141
  2.9 6.8 %all-to-all-start = ((bf16[16,32,1024]{2,1,0:T(8,128)(2,1)}), bf16[16,32,1024]{2,1,0:T(8,128)(2,1)S(1)}, u32[]{:S(2)}, u32[]{:S(2)}) async-start(bf16[16,32,1024]{2,1,0:T(8,128)(2,1)} %bitcast.25), calls=%async_computation | async-start | bytes 2097152 | tf_op jit(solution)/shard_map/all_to_all | solution.py:191
  9.7 0.6 fusion.9.order_ref
  10.4 3.2 %shard_map.95 = (bf16[512,256]{1,0:T(8,128)(2,1)}, bf16[1024,1024]{1,0:T(8,128)(2,1)}) custom-call(s32[1,256]{1,0:T(1,128)} %bitcast.26, s32[1,1024]{1,0:T(1,128)} %fusion.9.order_ref), custom_call_target="tpu_custom_call" | custom-call | tf_op jit(solution)/shard_map/pallas_call | solution.py:141
  13.6 12.1 %all-to-all-done = bf16[16,32,1024]{2,1,0:T(8,128)(2,1)S(1)} async-done(((bf16[16,32,1024]{2,1,0:T(8,128)(2,1)}), bf16[16,32,1024]{2,1,0:T(8,128)(2,1)S(1)}, u32[]{:S(2)}, u32[]{:S(2)}) %all-to-all-start) | async-done | bytes 1048608 | tf_op jit(solution)/shard_map/all_to_all | solution.py:191
  25.7 0.0 copy-done.2
  25.7 0.0 copy-start.1
  25.7 0.9 copy-done.1
  26.6 4.3 %shard_map.96 = (bf16[256,512]{1,0:T(8,128)(2,1)S(1)}, bf16[256,2048]{1,0:T(8,128)(2,1)S(1)}) custom-call(bf16[512,1024]{1,0:T(8,128)(2,1)S(1)} %bitcast.17, bf16[512,256]{1,0:T(8,128)(2,1)S(1)} %copy-done.1, bf16[1024,768]{1,0:T(8,128)(2,1)} %bitcast.14, bf16[1024,768]{1,0:T(8,128)(2,1)} %bitcast.23, bf16[256,768]{1,0:T(8,128)(2,1)S(1)} %bitcast.18, ...), custom_call_target="tpu_custom_call" | custom-call | tf_op jit(solution)/shard_map/pallas_call | solution.py:141
  31.0 4.5 %collective-permute-start = (bf16[256,2048]{1,0:T(8,128)(2,1)S(1)}, bf16[256,2048]{1,0:T(8,128)(2,1)S(1)}, u32[]{:S(2)}, u32[]{:S(2)}) collective-permute-start(bf16[256,2048]{1,0:T(8,128)(2,1)S(1)} %get-tuple-element.18.send_ref), channel_id=1, source_target_pairs={{0,16},{16,0},{32,48},{48,32},{64,80},{80,64},{96,112},{112,96},{1... | collective-permute-start | bytes 3145736 | tf_op jit(solution)/shard_map/ppermute | solution.py:169
  35.5 0.0 copy-done
  35.5 3.7 %shard_map.97.after_ref = bf16[512,1024]{1,0:T(8,128)(2,1)} custom-call(bf16[256,2048]{1,0:T(8,128)(2,1)S(1)} %get-tuple-element.18.send_ref, bf16[512,256]{1,0:T(8,128)(2,1)S(1)} %copy-done.1, bf16[1024,768]{1,0:T(8,128)(2,1)S(1)} %bitcast.15, bf16[1024,768]{1,0:T(8,128)(2,1)} %bitcast.24), custom_call_target="tpu_custom_call" | custom-call | tf_op jit(solution)/shard_map/pallas_call | solution.py:141
  39.3 0.0 collective-permute-done.got_ref
  39.3 1.0 shard_map.98
  40.3 4.7 %collective-permute-start.1 = (bf16[128,1536]{1,0:T(8,128)(2,1)S(1)}, bf16[128,1536]{1,0:T(8,128)(2,1)S(1)}, u32[]{:S(2)}, u32[]{:S(2)}) collective-permute-start(bf16[128,1536]{1,0:T(8,128)(2,1)S(1)} %get-tuple-element.19), channel_id=1, source_target_pairs={{0,992},{16,48},{32,0},{48,80},{64,32},{80,112},{96,64},{112,144},... | collective-permute-start | bytes 1179656 | tf_op jit(solution)/shard_map/ppermute | solution.py:166
  45.1 1.9 %collective-permute-start.3 = (bf16[128,1536]{1,0:T(8,128)(2,1)S(1)}, bf16[128,1536]{1,0:T(8,128)(2,1)}, u32[]{:S(2)}, u32[]{:S(2)}) collective-permute-start(bf16[128,1536]{1,0:T(8,128)(2,1)S(1)} %get-tuple-element.22), channel_id=1, source_target_pairs={{0,32},{16,1008},{32,64},{48,16},{64,96},{80,48},{96,128},{112,80}... | collective-permute-start | bytes 1179656 | tf_op jit(solution)/shard_map/ppermute | solution.py:166
  47.0 3.2 %collective-permute-start.4 = (bf16[128,1536]{1,0:T(8,128)(2,1)S(1)}, bf16[128,1536]{1,0:T(8,128)(2,1)}, u32[]{:S(2)}, u32[]{:S(2)}) collective-permute-start(bf16[128,1536]{1,0:T(8,128)(2,1)S(1)} %get-tuple-element.23), channel_id=1, source_target_pairs={{0,64},{16,976},{32,96},{48,1008},{64,128},{80,16},{96,160},{112,4... | collective-permute-start | bytes 1179656 | tf_op jit(solution)/shard_map/ppermute | solution.py:166
  50.2 1.2 collective-permute-done.1
  51.4 0.1 convert_element_type.42
  51.5 15.6 %collective-permute-start.2 = (bf16[32,1536]{1,0:T(8,128)(2,1)S(1)}, bf16[32,1536]{1,0:T(8,128)(2,1)}, u32[]{:S(2)}, u32[]{:S(2)}) collective-permute-start(bf16[32,1536]{1,0:T(8,128)(2,1)S(1)} %fusion.8), channel_id=1, source_target_pairs={{0,128},{16,912},{32,160},{48,944},{64,192},{80,976},{96,224},{112... | collective-permute-start | bytes 294920 | tf_op jit(solution)/shard_map/ppermute | solution.py:166
  67.1 3.7 %all-to-all-start.1 = ((bf16[16,32,1024]{2,1,0:T(8,128)(2,1)}), bf16[16,32,1024]{2,1,0:T(8,128)(2,1)S(1)}, u32[]{:S(2)}, u32[]{:S(2)}) async-start(bf16[16,32,1024]{2,1,0:T(8,128)(2,1)} %bitcast.8), calls=%async_computation.1 | async-start | bytes 2097152 | tf_op jit(solution)/shard_map/all_to_all | solution.py:244
  70.8 0.0 collective-permute-done.3
  70.8 1.1 convert_element_type.45
  71.9 0.0 copy-start.5
  71.9 0.0 collective-permute-done.4
  71.9 1.3 %convert_element_type.46 = f32[128,1536]{1,0:T(8,128)S(1)} convert(bf16[128,1536]{1,0:T(8,128)(2,1)} %collective-permute-done.4) | non-fusion elementwise | flops 196608 | bytes 1179648 | tf_op jit(solution)/shard_map/convert_element_type | solution.py:236
  73.2 0.0 collective-permute-done.2
  73.2 1.0 fusion.7
  74.2 0.0 copy-start.3
  74.2 0.0 copy-start.4
  74.2 8.3 %collective-permute-start.5 = (bf16[32,1536]{1,0:T(8,128)(2,1)S(1)}, bf16[32,1536]{1,0:T(8,128)(2,1)S(1)}, u32[]{:S(2)}, u32[]{:S(2)}) collective-permute-start(bf16[32,1536]{1,0:T(8,128)(2,1)S(1)} %fusion.7), channel_id=1, source_target_pairs={{0,128},{16,912},{32,160},{48,944},{64,192},{80,976},{96,224},{112... | collective-permute-start | bytes 294920 | tf_op jit(solution)/shard_map/ppermute | solution.py:166
  82.6 2.8 %collective-permute-done.5 = bf16[32,1536]{1,0:T(8,128)(2,1)S(1)} collective-permute-done((bf16[32,1536]{1,0:T(8,128)(2,1)S(1)}, bf16[32,1536]{1,0:T(8,128)(2,1)S(1)}, u32[]{:S(2)}, u32[]{:S(2)}) %collective-permute-start.5) | collective-permute-done | bytes 98336 | tf_op jit(solution)/shard_map/ppermute | solution.py:166
  85.4 0.1 fusion.5
  85.5 0.0 copy-done.5
  85.5 8.9 %collective-permute-start.6 = (bf16[32,1536]{1,0:T(8,128)(2,1)S(1)}, bf16[32,1536]{1,0:T(8,128)(2,1)S(1)}, u32[]{:S(2)}, u32[]{:S(2)}) collective-permute-start(bf16[32,1536]{1,0:T(8,128)(2,1)S(1)} %fusion.5), channel_id=1, source_target_pairs={{0,128},{16,912},{32,160},{48,944},{64,192},{80,976},{96,224},{112... | collective-permute-start | bytes 294920 | tf_op jit(solution)/shard_map/ppermute | solution.py:166
  94.4 2.7 %collective-permute-done.6 = bf16[32,1536]{1,0:T(8,128)(2,1)S(1)} collective-permute-done((bf16[32,1536]{1,0:T(8,128)(2,1)S(1)}, bf16[32,1536]{1,0:T(8,128)(2,1)S(1)}, u32[]{:S(2)}, u32[]{:S(2)}) %collective-permute-start.6) | collective-permute-done | bytes 98336 | tf_op jit(solution)/shard_map/ppermute | solution.py:166
  97.1 0.0 all-to-all-done.1
  97.1 1.6 %fusion.3 = bf16[32,1536]{1,0:T(8,128)(2,1)} fusion(f32[128,1536]{1,0:T(8,128)S(1)} %convert_element_type.42, f32[128,1536]{1,0:T(8,128)S(1)} %convert_element_type.46, f32[128,1536]{1,0:T(8,128)} %copy-done.5, f32[128,1536]{1,0:T(8,128)S(1)} %get-tuple-element.20, bf16[32,1536]{1,0:T(8,128)(2,1)S(1)} %collective-permute-done.6), kind=kLoop, calls=%fused_computation.5 | loop fusion | flops 294912 | bytes 983040 | tf_op jit(solution)/shard_map/convert_element_type | solution.py:250
  98.7 6.8 %collective-permute-start.7 = (bf16[32,1536]{1,0:T(8,128)(2,1)}, bf16[32,1536]{1,0:T(8,128)(2,1)S(1)}, u32[]{:S(2)}, u32[]{:S(2)}) collective-permute-start(bf16[32,1536]{1,0:T(8,128)(2,1)} %fusion.3), channel_id=1, source_target_pairs={{0,128},{16,912},{32,160},{48,944},{64,192},{80,976},{96,224},{112... | collective-permute-start | bytes 294920 | tf_op jit(solution)/shard_map/ppermute | solution.py:166
  105.5 4.1 %collective-permute-done.7 = bf16[32,1536]{1,0:T(8,128)(2,1)S(1)} collective-permute-done((bf16[32,1536]{1,0:T(8,128)(2,1)}, bf16[32,1536]{1,0:T(8,128)(2,1)S(1)}, u32[]{:S(2)}, u32[]{:S(2)}) %collective-permute-start.7) | collective-permute-done | bytes 98336 | tf_op jit(solution)/shard_map/ppermute | solution.py:166
  109.6 1.0 fusion.1
  110.6 10.4 %collective-permute-start.8 = (bf16[16,1536]{1,0:T(8,128)(2,1)S(1)}, bf16[16,1536]{1,0:T(8,128)(2,1)S(1)}, u32[]{:S(2)}, u32[]{:S(2)}) collective-permute-start(bf16[16,1536]{1,0:T(8,128)(2,1)S(1)} %select_convert_fusion), channel_id=1, source_target_pairs={{0,16},{16,0},{32,48},{48,32},{64,80},{80,64},{96,112},{112,96},{1... | collective-permute-start | bytes 147464 | tf_op jit(solution)/shard_map/ppermute | solution.py:169
  121.0 0.0 copy-done.3
  121.0 0.0 copy-done.4
  121.0 1.2 shard_map.99
  122.2 0.0 collective-permute-done.8
  122.2 0.6 slice_bitcast_fusion
  (4 shorter events, 0.1 us)
Async XLA Ops:
  0.6 25.1 %copy-start.2 = (bf16[1,1,256,768]{3,2,1,0:T(8,128)(2,1)S(1)}, bf16[1,1,256,768]{3,2,1,0:T(8,128)(2,1)}, u32[]{:S(2)}) copy-start(bf16[1,1,256,768]{3,2,1,0:T(8,128)(2,1)} %param.10) | copy-start | bytes 1179652
  2.9 22.8 %all-to-all-start = ((bf16[16,32,1024]{2,1,0:T(8,128)(2,1)}), bf16[16,32,1024]{2,1,0:T(8,128)(2,1)S(1)}, u32[]{:S(2)}, u32[]{:S(2)}) async-start(bf16[16,32,1024]{2,1,0:T(8,128)(2,1)} %bitcast.25), calls=%async_computation | async-start | bytes 2097152 | tf_op jit(solution)/shard_map/all_to_all | solution.py:191
  25.7 1.0 copy-start.1
  26.6 8.9 %copy-start = (bf16[1,1024,768]{2,1,0:T(8,128)(2,1)S(1)}, bf16[1,1024,768]{2,1,0:T(8,128)(2,1)}, u32[]{:S(2)}) copy-start(bf16[1,1024,768]{2,1,0:T(8,128)(2,1)} %param.8) | copy-start | bytes 4718596
  31.0 8.3 %collective-permute-start = (bf16[256,2048]{1,0:T(8,128)(2,1)S(1)}, bf16[256,2048]{1,0:T(8,128)(2,1)S(1)}, u32[]{:S(2)}, u32[]{:S(2)}) collective-permute-start(bf16[256,2048]{1,0:T(8,128)(2,1)S(1)} %get-tuple-element.18.send_ref), channel_id=1, source_target_pairs={{0,16},{16,0},{32,48},{48,32},{64,80},{80,64},{96,112},{112,96},{1... | collective-permute-start | bytes 3145736 | tf_op jit(solution)/shard_map/ppermute | solution.py:169
  40.3 11.1 %collective-permute-start.1 = (bf16[128,1536]{1,0:T(8,128)(2,1)S(1)}, bf16[128,1536]{1,0:T(8,128)(2,1)S(1)}, u32[]{:S(2)}, u32[]{:S(2)}) collective-permute-start(bf16[128,1536]{1,0:T(8,128)(2,1)S(1)} %get-tuple-element.19), channel_id=1, source_target_pairs={{0,992},{16,48},{32,0},{48,80},{64,32},{80,112},{96,64},{112,144},... | collective-permute-start | bytes 1179656 | tf_op jit(solution)/shard_map/ppermute | solution.py:166
  45.1 25.7 %collective-permute-start.3 = (bf16[128,1536]{1,0:T(8,128)(2,1)S(1)}, bf16[128,1536]{1,0:T(8,128)(2,1)}, u32[]{:S(2)}, u32[]{:S(2)}) collective-permute-start(bf16[128,1536]{1,0:T(8,128)(2,1)S(1)} %get-tuple-element.22), channel_id=1, source_target_pairs={{0,32},{16,1008},{32,64},{48,16},{64,96},{80,48},{96,128},{112,80}... | collective-permute-start | bytes 1179656 | tf_op jit(solution)/shard_map/ppermute | solution.py:166
  47.0 24.9 %collective-permute-start.4 = (bf16[128,1536]{1,0:T(8,128)(2,1)S(1)}, bf16[128,1536]{1,0:T(8,128)(2,1)}, u32[]{:S(2)}, u32[]{:S(2)}) collective-permute-start(bf16[128,1536]{1,0:T(8,128)(2,1)S(1)} %get-tuple-element.23), channel_id=1, source_target_pairs={{0,64},{16,976},{32,96},{48,1008},{64,128},{80,16},{96,160},{112,4... | collective-permute-start | bytes 1179656 | tf_op jit(solution)/shard_map/ppermute | solution.py:166
  51.5 21.7 %collective-permute-start.2 = (bf16[32,1536]{1,0:T(8,128)(2,1)S(1)}, bf16[32,1536]{1,0:T(8,128)(2,1)}, u32[]{:S(2)}, u32[]{:S(2)}) collective-permute-start(bf16[32,1536]{1,0:T(8,128)(2,1)S(1)} %fusion.8), channel_id=1, source_target_pairs={{0,128},{16,912},{32,160},{48,944},{64,192},{80,976},{96,224},{112... | collective-permute-start | bytes 294920 | tf_op jit(solution)/shard_map/ppermute | solution.py:166
  67.1 30.0 %all-to-all-start.1 = ((bf16[16,32,1024]{2,1,0:T(8,128)(2,1)}), bf16[16,32,1024]{2,1,0:T(8,128)(2,1)S(1)}, u32[]{:S(2)}, u32[]{:S(2)}) async-start(bf16[16,32,1024]{2,1,0:T(8,128)(2,1)} %bitcast.8), calls=%async_computation.1 | async-start | bytes 2097152 | tf_op jit(solution)/shard_map/all_to_all | solution.py:244
  71.9 13.7 %copy-start.5 = (f32[128,1536]{1,0:T(8,128)}, f32[128,1536]{1,0:T(8,128)S(1)}, u32[]{:S(2)}) copy-start(f32[128,1536]{1,0:T(8,128)S(1)} %convert_element_type.45) | copy-start | bytes 2359300
  74.2 46.8 %copy-start.3 = (s32[128,4]{0,1:T(4,128)S(1)}, s32[128,4]{0,1:T(4,128)}, u32[]{:S(2)}) copy-start(s32[128,4]{0,1:T(4,128)} %param.12) | copy-start | bytes 6148
  74.2 46.8 %copy-start.4 = (s32[128]{0:T(128)S(1)}, s32[128]{0:T(128)}, u32[]{:S(2)}) copy-start(s32[128]{0:T(128)} %param.13) | copy-start | bytes 1540
  74.2 11.2 %collective-permute-start.5 = (bf16[32,1536]{1,0:T(8,128)(2,1)S(1)}, bf16[32,1536]{1,0:T(8,128)(2,1)S(1)}, u32[]{:S(2)}, u32[]{:S(2)}) collective-permute-start(bf16[32,1536]{1,0:T(8,128)(2,1)S(1)} %fusion.7), channel_id=1, source_target_pairs={{0,128},{16,912},{32,160},{48,944},{64,192},{80,976},{96,224},{112... | collective-permute-start | bytes 294920 | tf_op jit(solution)/shard_map/ppermute | solution.py:166
  85.5 11.6 %collective-permute-start.6 = (bf16[32,1536]{1,0:T(8,128)(2,1)S(1)}, bf16[32,1536]{1,0:T(8,128)(2,1)S(1)}, u32[]{:S(2)}, u32[]{:S(2)}) collective-permute-start(bf16[32,1536]{1,0:T(8,128)(2,1)S(1)} %fusion.5), channel_id=1, source_target_pairs={{0,128},{16,912},{32,160},{48,944},{64,192},{80,976},{96,224},{112... | collective-permute-start | bytes 294920 | tf_op jit(solution)/shard_map/ppermute | solution.py:166
  98.7 10.9 %collective-permute-start.7 = (bf16[32,1536]{1,0:T(8,128)(2,1)}, bf16[32,1536]{1,0:T(8,128)(2,1)S(1)}, u32[]{:S(2)}, u32[]{:S(2)}) collective-permute-start(bf16[32,1536]{1,0:T(8,128)(2,1)} %fusion.3), channel_id=1, source_target_pairs={{0,128},{16,912},{32,160},{48,944},{64,192},{80,976},{96,224},{112... | collective-permute-start | bytes 294920 | tf_op jit(solution)/shard_map/ppermute | solution.py:166
  110.6 11.6 %collective-permute-start.8 = (bf16[16,1536]{1,0:T(8,128)(2,1)S(1)}, bf16[16,1536]{1,0:T(8,128)(2,1)S(1)}, u32[]{:S(2)}, u32[]{:S(2)}) collective-permute-start(bf16[16,1536]{1,0:T(8,128)(2,1)S(1)} %select_convert_fusion), channel_id=1, source_target_pairs={{0,16},{16,0},{32,48},{48,32},{64,80},{80,64},{96,112},{112,96},{1... | collective-permute-start | bytes 147464 | tf_op jit(solution)/shard_map/ppermute | solution.py:169

commit v4 on v3

--- a/solution.py
+++ b/solution.py
@@ -81,18 +81,17 @@
     out_ref[...] = contract(marks, back_ref[...], ((0,), (0,))).astype(jnp.bfloat16)
 
 
-def select_kernel(sources, cap, tokens, chosen_ref, order_ref, marks_ref, pick_ref):
-    marks_ref[...] = slot_marks(chosen_ref[...], sources, cap, tokens)
-    pick_ref[...] = (iota(pick_ref.shape, 0) == order_ref[...]).astype(jnp.float32).astype(jnp.bfloat16)
-
-
-def delta_kernel(arrived_ref, marks_ref, gate_hbm, up_hbm, grad_hbm, pick_hbm, mine_ref, send_ref, gate_ref, up_ref, grad_ref, pick_ref, sems):
+def delta_kernel(sources, cap, tokens, arrived_ref, chosen_ref, order_ref, gate_hbm, up_hbm, grad_hbm, mine_ref, send_ref, gate_ref, up_ref, grad_ref, sems):
     ff = gate_ref.shape[1]
-    half = arrived_ref.shape[1] // 2
-    gate_in, up_in, grad_in, pick_in = fetch(
-        [(gate_hbm, gate_ref), (up_hbm, up_ref), (grad_hbm, grad_ref), (pick_hbm, pick_ref)], sems
-    )
-    rows = contract(marks_ref[...], arrived_ref[...], ((0,), (0,))).astype(jnp.bfloat16)
+    width = arrived_ref.shape[1]
+    half = width // 2
+    gate_in, up_in, grad_in = fetch([(gate_hbm, gate_ref), (up_hbm, up_ref), (grad_hbm, grad_ref)], sems)
+    marks = slot_marks(chosen_ref[...], sources, cap, tokens)
+    rows = contract(marks, arrived_ref[...], ((0,), (0,))).astype(jnp.bfloat16)
+    pick = (iota((width, width), 0) == order_ref[...]).astype(jnp.float32).astype(jnp.bfloat16)
+    ordered = jnp.dot(rows, pick, preferred_element_type=jnp.float32).astype(jnp.bfloat16)
+    mine_ref[...] = ordered[:, :half]
+    send_ref[:, :half] = ordered[:, half:]
     gate_in.wait()
     gate = jnp.dot(rows, gate_ref[...], preferred_element_type=jnp.float32)
     up_in.wait()
@@ -102,20 +101,22 @@
     upstream = grad_ref[...].astype(jnp.float32)
     send_ref[:, half : half + ff] = (upstream * up * (squash * (1.0 + gate * (1.0 - squash)))).astype(jnp.bfloat16)
     send_ref[:, half + ff :] = (upstream * (gate * squash)).astype(jnp.bfloat16)
-    pick_in.wait()
-    ordered = jnp.dot(rows, pick_ref[...], preferred_element_type=jnp.float32).astype(jnp.bfloat16)
-    mine_ref[...] = ordered[:, :half]
-    send_ref[:, :half] = ordered[:, half:]
-
-
-def back_kernel(half, send_ref, marks_ref, gate_hbm, up_hbm, out_ref, gate_ref, up_ref, stage_ref, in_sems, out_sems):
+
+
+def slot_grad_kernel(half, send_ref, gate_hbm, up_hbm, out_ref, gate_ref, up_ref, sems):
     ff = gate_ref.shape[1]
-    gate_in, up_in = fetch([(gate_hbm, gate_ref), (up_hbm, up_ref)], in_sems)
+    gate_in, up_in = fetch([(gate_hbm, gate_ref), (up_hbm, up_ref)], sems)
     gate_in.wait()
     grad = contract(send_ref[:, half : half + ff], gate_ref[...], ((1,), (1,)))
     up_in.wait()
     grad = grad + contract(send_ref[:, half + ff :], up_ref[...], ((1,), (1,)))
-    marked_rows(marks_ref[...], grad.astype(jnp.bfloat16), out_ref, stage_ref, out_sems)
+    out_ref[...] = grad.astype(jnp.bfloat16)
+
+
+def back_kernel(sources, cap, tokens, chosen_ref, grad_ref, after_ref, out_ref, stage_ref, sems):
+    del after_ref
+    marks = slot_marks(chosen_ref[...], sources, cap, tokens)
+    marked_rows(marks, grad_ref[...], out_ref, stage_ref, sems)
 
 
 def weight_kernel(mine_ref, send_ref, got_ref, after_ref, keep_ref, next_ref, past_ref, far_ref):
@@ -132,6 +133,20 @@
     next_ref[...] = part(1).astype(jnp.bfloat16)
     past_ref[...] = part(3).astype(jnp.bfloat16)
     keep_ref[...] = part(0)
+
+
+def fold_kernel(rows, core_ref, keep_ref, next_hbm, far_hbm, past_hbm, out_ref, next_ref, far_ref, past_ref, sems):
+    for copy in fetch([(next_hbm, next_ref), (far_hbm, far_ref), (past_hbm, past_ref)], sems):
+        copy.wait()
+    n = keep_ref.shape[0] // rows
+    for a in range(n):
+        here, before = pl.ds(a * rows, rows), pl.ds((a - 1 if a else n - 1) * rows, rows)
+        total = next_ref[here].astype(jnp.float32) + far_ref[here].astype(jnp.float32)
+        if a:
+            total = total + keep_ref[before] + past_ref[before].astype(jnp.float32)
+        else:
+            total = total + jnp.where(core_ref[0] == 1, keep_ref[before], 0.0)
+        out_ref[here] = total
 
 
 def call(kernel, outs, *args, ins=None, out_space=None, scratch=(), mib=40):
@@ -200,47 +215,49 @@
     ahead = jnp.where(q > 0, FAN * i + q, jnp.where(i == n - 1, last, FAN * (i + 1)))
     owner = (z + jnp.where(to_core == 0, ahead, -ahead) + chips) % chips
     order = (owner * 2 * rows + m % (2 * rows))[None, :]
-    marks, pick = call(
-        functools.partial(select_kernel, peers, cap, tok_dev),
-        [((padded, slots), bf16), ((width, width), bf16)],
-        picked, order,
-        mib=60,
-    )
-
     mine, send = call(
-        delta_kernel,
+        functools.partial(delta_kernel, peers, cap, tok_dev),
         [((slots, half), bf16), ((slots, half + 2 * ff), bf16)],
-        arrived, marks, gate, up, hidden_grad[0, 0], pick,
-        ins=[None] * 2 + [hbm] * 4,
-        scratch=[vmem(gate.shape, bf16), vmem(up.shape, bf16), vmem((slots, ff), bf16), vmem(pick.shape, bf16), dma((4,))],
+        arrived, picked, order, gate, up, hidden_grad[0, 0],
+        ins=[None] * 3 + [hbm] * 3,
+        scratch=[vmem(a.shape, bf16) for a in (gate, up, hidden_grad[0, 0])] + [dma((3,))],
         mib=50,
     )
     got = swap(send)
-    back = call(
-        functools.partial(back_kernel, half),
-        [((padded, width), bf16)],
-        send, marks, gate, up,
-        ins=[None] * 2 + [hbm] * 2,
-        out_space=hbm,
-        scratch=[vmem(gate.shape, bf16), vmem(up.shape, bf16), vmem((padded, width), bf16), dma((2,)), dma((BLOCKS,))],
+    slot_grad = call(
+        functools.partial(slot_grad_kernel, half),
+        [((slots, width), bf16)],
+        send, gate, up,
+        ins=[None] + [hbm] * 2,
+        scratch=[vmem(gate.shape, bf16), vmem(up.shape, bf16), dma((2,))],
         mib=50,
     )
     keep, to_1, to_past, to_2 = call(
         weight_kernel,
         [((block, 2 * ff), f32)] + [((block, 2 * ff), bf16)] * 3,
-        mine, send, got, back,
+        mine, send, got, slot_grad,
         ins=[None] * 3 + [pl.ANY],
         mib=40,
     )
-    from_2, from_1, from_past = [
-        v.reshape(n, 2 * rows, 2 * ff).astype(f32) for v in (along(to_2, 2), along(to_1, 1), along(to_past, -1))
-    ]
-    own = keep.reshape(n, 2 * rows, 2 * ff)
-    terms = [from_1[0] + from_2[0] + jnp.where(core == 1, own[n - 1], 0.0)]
-    terms += [own[a - 1] + from_1[a] + from_2[a] + from_past[a - 1] for a in range(1, n)]
-    total = from_past[n - 1] + jnp.where(core == 0, own[n - 1], 0.0)
-    total = total.astype(bf16)
-    total, back = lax.optimization_barrier((total, back))
+    from_past, from_1, from_2 = along(to_past, -1), along(to_1, 1), along(to_2, 2)
+    end = slice(block - 2 * rows, block)
+    total = (from_past[end].astype(f32) + jnp.where(core == 0, keep[end], 0.0)).astype(bf16)
+    terms = call(
+        functools.partial(fold_kernel, 2 * rows),
+        [((block, 2 * ff), f32)],
+        core[None], keep, from_1, from_2, from_past,
+        ins=[pltpu.SMEM, None] + [hbm] * 3,
+        scratch=[vmem((block, 2 * ff), bf16)] * 3 + [dma((3,))],
+        mib=56,
+    ).reshape(n, 2 * rows, 2 * ff)
+    back = call(
+        functools.partial(back_kernel, peers, cap, tok_dev),
+        [((padded, width), bf16)],
+        picked, slot_grad, total,
+        ins=[None] * 2 + [pl.ANY],
+        out_space=hbm,
+        scratch=[vmem((padded, width), bf16), dma((BLOCKS,))],
+    )
     returned = lax.all_to_all(back.reshape(peers, cap, width), "expert", split_axis=0, concat_axis=0, tiled=True)
     for t in range(1, n + 1):
         total = along(total, FAN)

time: 124 us -> 121 us (0.976)
  the two profiles are of different devices: /device:TPU:97 before, /device:TPU:1 now
where the time goes in v4:
time: 121 us; the launch traced here: 120 us
  starting transfers between devices  63.8 us (53%)
  waiting for transfers between devices  34.8 us (29%)
  Pallas kernels  15.4 us (13%)
  other arithmetic  3.97 us (3%)
    ppermute x7, starting transfers between devices, along(): return lax.ppermute(value, 'dp', pairs)  37.4 us
    ppermute x7, waiting for transfers between devices, along(): return lax.ppermute(value, 'dp', pairs)  22.7 us
    pallas_call x7, Pallas kernels, call(): pl.pallas_call(kernel, in_specs=[pl.BlockSpec(memory_space=s) for s in sp...  15.4 us
    ppermute x2, starting transfers between devices, swap(): return lax.ppermute(value, 'dp', [(d, d ^ 1) for d in range(groups)])  15.2 us
    all_to_all x1, waiting for transfers between devices, on_device(): lax.all_to_all(outgoing.reshape(peers, cap, width), 'expert', split_axis=...  12.1 us
    all_to_all x1, starting transfers between devices, on_device(): lax.all_to_all(outgoing.reshape(peers, cap, width), 'expert', split_axis=...  7.6 us
    all_to_all x1, starting transfers between devices, on_device(): lax.all_to_all(back.reshape(peers, cap, width), 'expert', split_axis=0, c...  3.66 us
    convert_element_type x3, other arithmetic, on_device(): total = total.astype(bf16) if t < n else total  2.92 us
  transfers between devices with their start and end apart: 11, of which 5 were waited for; matrix products, arithmetic and copies ran while one was open for 2% of the time, Pallas kernels for 7%

profile of v4, /device:TPU:1, one launch (start us, length us, event | category | flops | bytes accessed | tf_op | source)
XLA Modules:
  0.0 119.7 jit_solution(6474408438783859581)
XLA Ops:
  0.6 0.0 copy-start.2
  0.6 0.0 copy-start.4
  0.7 2.3 %shard_map.94 = bf16[512,1024]{1,0:T(8,128)(2,1)} custom-call(bf16[128,1024]{1,0:T(8,128)(2,1)} %tokens_hbm.1, s32[4,128]{1,0:T(4,128)} %bitcast.20, s32[1,128]{1,0:T(1,128)} %bitcast.24), custom_call_target="tpu_custom_call" | custom-call | tf_op jit(solution)/shard_map/pallas_call | solution.py:156
  2.9 7.6 %all-to-all-start = ((bf16[16,32,1024]{2,1,0:T(8,128)(2,1)}), bf16[16,32,1024]{2,1,0:T(8,128)(2,1)S(1)}, u32[]{:S(2)}, u32[]{:S(2)}) async-start(bf16[16,32,1024]{2,1,0:T(8,128)(2,1)} %bitcast.28), calls=%async_computation | async-start | bytes 2097152 | tf_op jit(solution)/shard_map/all_to_all | solution.py:206
  10.6 0.1 fusion.3.order_ref
  10.6 12.1 %all-to-all-done = bf16[16,32,1024]{2,1,0:T(8,128)(2,1)S(1)} async-done(((bf16[16,32,1024]{2,1,0:T(8,128)(2,1)}), bf16[16,32,1024]{2,1,0:T(8,128)(2,1)S(1)}, u32[]{:S(2)}, u32[]{:S(2)}) %all-to-all-start) | async-done | bytes 1048608 | tf_op jit(solution)/shard_map/all_to_all | solution.py:206
  22.7 0.0 copy-done.2
  22.7 0.0 copy-done.4
  22.7 3.6 %shard_map.95 = (bf16[256,512]{1,0:T(8,128)(2,1)S(1)}, bf16[256,2048]{1,0:T(8,128)(2,1)S(1)}) custom-call(bf16[512,1024]{1,0:T(8,128)(2,1)S(1)} %bitcast.18, s32[1,256]{1,0:T(1,128)S(1)} %bitcast.22, s32[1,1024]{1,0:T(1,128)S(1)} %fusion.3.order_ref, bf16[1024,768]{1,0:T(8,128)(2,1)} %bitcast.15, bf16[1024,768]{1,0:T(8,128)(2,1)} %bitcast.26, ...), custom_call_target="tpu_custom_call" | custom-call | tf_op jit(solution)/shard_map/pallas_call | solution.py:156
  26.4 13.2 %collective-permute-start = (bf16[256,2048]{1,0:T(8,128)(2,1)S(1)}, bf16[256,2048]{1,0:T(8,128)(2,1)S(1)}, u32[]{:S(2)}, u32[]{:S(2)}) collective-permute-start(bf16[256,2048]{1,0:T(8,128)(2,1)S(1)} %get-tuple-element.12.send_ref), channel_id=1, source_target_pairs={{0,16},{16,0},{32,48},{48,32},{64,80},{80,64},{96,112},{112,96},{1... | collective-permute-start | bytes 3145736 | tf_op jit(solution)/shard_map/ppermute | solution.py:184
  39.6 0.0 copy-done
  39.6 2.5 %shard_map.96.after_ref.grad_ref = bf16[256,1024]{1,0:T(8,128)(2,1)S(1)} custom-call(bf16[256,2048]{1,0:T(8,128)(2,1)S(1)} %get-tuple-element.12.send_ref, bf16[1024,768]{1,0:T(8,128)(2,1)S(1)} %bitcast.16, bf16[1024,768]{1,0:T(8,128)(2,1)} %bitcast.27), custom_call_target="tpu_custom_call" | custom-call | tf_op jit(solution)/shard_map/pallas_call | solution.py:156
  42.2 0.0 collective-permute-done.got_ref
  42.2 1.0 shard_map.97
  43.2 0.0 copy-start.1
  43.2 1.9 %collective-permute-start.1 = (bf16[128,1536]{1,0:T(8,128)(2,1)S(1)}, bf16[128,1536]{1,0:T(8,128)(2,1)S(1)}, u32[]{:S(2)}, u32[]{:S(2)}) collective-permute-start(bf16[128,1536]{1,0:T(8,128)(2,1)S(1)} %get-tuple-element.13), channel_id=1, source_target_pairs={{0,992},{16,48},{32,0},{48,80},{64,32},{80,112},{96,64},{112,144},... | collective-permute-start | bytes 1179656 | tf_op jit(solution)/shard_map/ppermute | solution.py:181
  45.1 13.5 %collective-permute-start.3 = (bf16[128,1536]{1,0:T(8,128)(2,1)S(1)}, bf16[128,1536]{1,0:T(8,128)(2,1)S(1)}, u32[]{:S(2)}, u32[]{:S(2)}) collective-permute-start(bf16[128,1536]{1,0:T(8,128)(2,1)S(1)} %get-tuple-element.15), channel_id=1, source_target_pairs={{0,32},{16,1008},{32,64},{48,16},{64,96},{80,48},{96,128},{112,80}... | collective-permute-start | bytes 1179656 | tf_op jit(solution)/shard_map/ppermute | solution.py:181
  58.6 3.8 %collective-permute-start.4 = (bf16[128,1536]{1,0:T(8,128)(2,1)S(1)}, bf16[128,1536]{1,0:T(8,128)(2,1)}, u32[]{:S(2)}, u32[]{:S(2)}) collective-permute-start(bf16[128,1536]{1,0:T(8,128)(2,1)S(1)} %get-tuple-element.16), channel_id=1, source_target_pairs={{0,64},{16,976},{32,96},{48,1008},{64,128},{80,16},{96,160},{112,4... | collective-permute-start | bytes 1179656 | tf_op jit(solution)/shard_map/ppermute | solution.py:181
  62.4 0.0 collective-permute-done.1.past_hbm
  62.4 0.0 copy-start.6
  62.5 5.3 %collective-permute-start.2 = (bf16[32,1536]{1,0:T(8,128)(2,1)S(1)}, bf16[32,1536]{1,0:T(8,128)(2,1)}, u32[]{:S(2)}, u32[]{:S(2)}) collective-permute-start(bf16[32,1536]{1,0:T(8,128)(2,1)S(1)} %add_convert_fusion.after_ref), channel_id=1, source_target_pairs={{0,128},{16,912},{32,160},{48,944},{64,192},{80,976},{96,224},{112... | collective-permute-start | bytes 294920 | tf_op jit(solution)/shard_map/ppermute | solution.py:181
  67.8 1.4 %shard_map.99 = bf16[512,1024]{1,0:T(8,128)(2,1)} custom-call(s32[1,256]{1,0:T(1,128)S(1)} %bitcast.23, bf16[256,1024]{1,0:T(8,128)(2,1)S(1)} %shard_map.96.after_ref.grad_ref, bf16[32,1536]{1,0:T(8,128)(2,1)S(1)} %add_convert_fusion.after_ref), custom_call_target="tpu_custom_call" | custom-call | tf_op jit(solution)/shard_map/pallas_call | solution.py:156
  69.2 0.0 copy-done.1
  69.2 0.0 copy-done.6
  69.2 3.7 %all-to-all-start.1 = ((bf16[16,32,1024]{2,1,0:T(8,128)(2,1)}), bf16[16,32,1024]{2,1,0:T(8,128)(2,1)S(1)}, u32[]{:S(2)}, u32[]{:S(2)}) async-start(bf16[16,32,1024]{2,1,0:T(8,128)(2,1)} %bitcast.9), calls=%async_computation.1 | async-start | bytes 2097152 | tf_op jit(solution)/shard_map/all_to_all | solution.py:261
  72.9 0.0 collective-permute-done.3.next_hbm
  72.9 0.0 copy-start.7
  72.9 4.8 %collective-permute-done.4.far_hbm = bf16[128,1536]{1,0:T(8,128)(2,1)} collective-permute-done((bf16[128,1536]{1,0:T(8,128)(2,1)S(1)}, bf16[128,1536]{1,0:T(8,128)(2,1)}, u32[]{:S(2)}, u32[]{:S(2)}) %collective-permute-start.4) | collective-permute-done | bytes 393248 | tf_op jit(solution)/shard_map/ppermute | solution.py:181
  77.7 0.0 copy-done.7
  77.7 3.4 %shard_map.98 = f32[128,1536]{1,0:T(8,128)} custom-call(s32[1]{0:T(128)} %bitcast.8.core_ref, f32[128,1536]{1,0:T(8,128)} %copy-done.1, bf16[128,1536]{1,0:T(8,128)(2,1)} %copy-done.7, bf16[128,1536]{1,0:T(8,128)(2,1)} %collective-permute-done.4.far_hbm, bf16[128,1536]{1,0:T(8,128)(2,1)} %copy-done.6), custom_call_target="tpu_custom_call" | custom-call | tf_op jit(solution)/shard_map/pallas_call | solution.py:156
  81.1 0.0 copy-start.3
  81.1 0.0 copy-start.5
  81.1 0.0 collective-permute-done.2
  81.2 1.0 fusion.2
  82.2 5.4 %collective-permute-start.5 = (bf16[32,1536]{1,0:T(8,128)(2,1)S(1)}, bf16[32,1536]{1,0:T(8,128)(2,1)S(1)}, u32[]{:S(2)}, u32[]{:S(2)}) collective-permute-start(bf16[32,1536]{1,0:T(8,128)(2,1)S(1)} %fusion.2), channel_id=1, source_target_pairs={{0,128},{16,912},{32,160},{48,944},{64,192},{80,976},{96,224},{112... | collective-permute-start | bytes 294920 | tf_op jit(solution)/shard_map/ppermute | solution.py:181
  87.6 4.5 %collective-permute-done.5 = bf16[32,1536]{1,0:T(8,128)(2,1)S(1)} collective-permute-done((bf16[32,1536]{1,0:T(8,128)(2,1)S(1)}, bf16[32,1536]{1,0:T(8,128)(2,1)S(1)}, u32[]{:S(2)}, u32[]{:S(2)}) %collective-permute-start.5) | collective-permute-done | bytes 98336 | tf_op jit(solution)/shard_map/ppermute | solution.py:181
  92.1 1.0 fusion.1
  93.1 4.8 %collective-permute-start.6 = (bf16[32,1536]{1,0:T(8,128)(2,1)S(1)}, bf16[32,1536]{1,0:T(8,128)(2,1)S(1)}, u32[]{:S(2)}, u32[]{:S(2)}) collective-permute-start(bf16[32,1536]{1,0:T(8,128)(2,1)S(1)} %fusion.1), channel_id=1, source_target_pairs={{0,128},{16,912},{32,160},{48,944},{64,192},{80,976},{96,224},{112... | collective-permute-start | bytes 294920 | tf_op jit(solution)/shard_map/ppermute | solution.py:181
  97.8 6.5 %collective-permute-done.6 = bf16[32,1536]{1,0:T(8,128)(2,1)S(1)} collective-permute-done((bf16[32,1536]{1,0:T(8,128)(2,1)S(1)}, bf16[32,1536]{1,0:T(8,128)(2,1)S(1)}, u32[]{:S(2)}, u32[]{:S(2)}) %collective-permute-start.6) | collective-permute-done | bytes 98336 | tf_op jit(solution)/shard_map/ppermute | solution.py:181
  104.4 0.0 all-to-all-done.1
  104.4 1.0 fusion
  105.3 2.7 %collective-permute-start.7 = (bf16[32,1536]{1,0:T(8,128)(2,1)S(1)}, bf16[32,1536]{1,0:T(8,128)(2,1)S(1)}, u32[]{:S(2)}, u32[]{:S(2)}) collective-permute-start(bf16[32,1536]{1,0:T(8,128)(2,1)S(1)} %fusion), channel_id=1, source_target_pairs={{0,128},{16,912},{32,160},{48,944},{64,192},{80,976},{96,224},{112... | collective-permute-start | bytes 294920 | tf_op jit(solution)/shard_map/ppermute | solution.py:181
  108.1 6.9 %collective-permute-done.7 = bf16[32,1536]{1,0:T(8,128)(2,1)S(1)} collective-permute-done((bf16[32,1536]{1,0:T(8,128)(2,1)S(1)}, bf16[32,1536]{1,0:T(8,128)(2,1)S(1)}, u32[]{:S(2)}, u32[]{:S(2)}) %collective-permute-start.7) | collective-permute-done | bytes 98336 | tf_op jit(solution)/shard_map/ppermute | solution.py:181
  114.9 0.9 slice_add_fusion
  115.9 1.9 %collective-permute-start.8 = (bf16[16,1536]{1,0:T(8,128)(2,1)S(1)}, bf16[16,1536]{1,0:T(8,128)(2,1)S(1)}, u32[]{:S(2)}, u32[]{:S(2)}) collective-permute-start(bf16[16,1536]{1,0:T(8,128)(2,1)S(1)} %select_convert_fusion), channel_id=1, source_target_pairs={{0,16},{16,0},{32,48},{48,32},{64,80},{80,64},{96,112},{112,96},{1... | collective-permute-start | bytes 147464 | tf_op jit(solution)/shard_map/ppermute | solution.py:184
  117.8 1.2 shard_map.100
  119.0 0.0 collective-permute-done.8
  119.1 0.6 slice_bitcast_fusion
  (6 shorter events, 0.1 us)
Async XLA Ops:
  0.6 22.1 %copy-start.2 = (bf16[1,1,256,768]{3,2,1,0:T(8,128)(2,1)S(1)}, bf16[1,1,256,768]{3,2,1,0:T(8,128)(2,1)}, u32[]{:S(2)}) copy-start(bf16[1,1,256,768]{3,2,1,0:T(8,128)(2,1)} %param.10) | copy-start | bytes 1179652
  0.6 22.1 %copy-start.4 = (s32[1,1,256]{2,1,0:T(1,128)S(1)}, s32[1,1,256]{2,1,0:T(1,128)}, u32[]{:S(2)}) copy-start(s32[1,1,256]{2,1,0:T(1,128)} %param.11) | copy-start | bytes 3076
  2.9 19.8 %all-to-all-start = ((bf16[16,32,1024]{2,1,0:T(8,128)(2,1)}), bf16[16,32,1024]{2,1,0:T(8,128)(2,1)S(1)}, u32[]{:S(2)}, u32[]{:S(2)}) async-start(bf16[16,32,1024]{2,1,0:T(8,128)(2,1)} %bitcast.28), calls=%async_computation | async-start | bytes 2097152 | tf_op jit(solution)/shard_map/all_to_all | solution.py:206
  22.7 16.9 %copy-start = (bf16[1,1024,768]{2,1,0:T(8,128)(2,1)S(1)}, bf16[1,1024,768]{2,1,0:T(8,128)(2,1)}, u32[]{:S(2)}) copy-start(bf16[1,1024,768]{2,1,0:T(8,128)(2,1)} %param.8) | copy-start | bytes 4718596
  26.4 15.8 %collective-permute-start = (bf16[256,2048]{1,0:T(8,128)(2,1)S(1)}, bf16[256,2048]{1,0:T(8,128)(2,1)S(1)}, u32[]{:S(2)}, u32[]{:S(2)}) collective-permute-start(bf16[256,2048]{1,0:T(8,128)(2,1)S(1)} %get-tuple-element.12.send_ref), channel_id=1, source_target_pairs={{0,16},{16,0},{32,48},{48,32},{64,80},{80,64},{96,112},{112,96},{1... | collective-permute-start | bytes 3145736 | tf_op jit(solution)/shard_map/ppermute | solution.py:184
  43.2 26.0 %copy-start.1 = (f32[128,1536]{1,0:T(8,128)}, f32[128,1536]{1,0:T(8,128)S(1)}, u32[]{:S(2)}) copy-start(f32[128,1536]{1,0:T(8,128)S(1)} %get-tuple-element.14.keep_ref) | copy-start | bytes 2359300
  43.2 19.2 %collective-permute-start.1 = (bf16[128,1536]{1,0:T(8,128)(2,1)S(1)}, bf16[128,1536]{1,0:T(8,128)(2,1)S(1)}, u32[]{:S(2)}, u32[]{:S(2)}) collective-permute-start(bf16[128,1536]{1,0:T(8,128)(2,1)S(1)} %get-tuple-element.13), channel_id=1, source_target_pairs={{0,992},{16,48},{32,0},{48,80},{64,32},{80,112},{96,64},{112,144},... | collective-permute-start | bytes 1179656 | tf_op jit(solution)/shard_map/ppermute | solution.py:181
  45.1 27.7 %collective-permute-start.3 = (bf16[128,1536]{1,0:T(8,128)(2,1)S(1)}, bf16[128,1536]{1,0:T(8,128)(2,1)S(1)}, u32[]{:S(2)}, u32[]{:S(2)}) collective-permute-start(bf16[128,1536]{1,0:T(8,128)(2,1)S(1)} %get-tuple-element.15), channel_id=1, source_target_pairs={{0,32},{16,1008},{32,64},{48,16},{64,96},{80,48},{96,128},{112,80}... | collective-permute-start | bytes 1179656 | tf_op jit(solution)/shard_map/ppermute | solution.py:181
  58.6 19.1 %collective-permute-start.4 = (bf16[128,1536]{1,0:T(8,128)(2,1)S(1)}, bf16[128,1536]{1,0:T(8,128)(2,1)}, u32[]{:S(2)}, u32[]{:S(2)}) collective-permute-start(bf16[128,1536]{1,0:T(8,128)(2,1)S(1)} %get-tuple-element.16), channel_id=1, source_target_pairs={{0,64},{16,976},{32,96},{48,1008},{64,128},{80,16},{96,160},{112,4... | collective-permute-start | bytes 1179656 | tf_op jit(solution)/shard_map/ppermute | solution.py:181
  62.4 6.8 %copy-start.6 = (bf16[128,1536]{1,0:T(8,128)(2,1)}, bf16[128,1536]{1,0:T(8,128)(2,1)S(1)}, u32[]{:S(2)}) copy-start(bf16[128,1536]{1,0:T(8,128)(2,1)S(1)} %collective-permute-done.1.past_hbm) | copy-start | bytes 1179652
  62.5 18.7 %collective-permute-start.2 = (bf16[32,1536]{1,0:T(8,128)(2,1)S(1)}, bf16[32,1536]{1,0:T(8,128)(2,1)}, u32[]{:S(2)}, u32[]{:S(2)}) collective-permute-start(bf16[32,1536]{1,0:T(8,128)(2,1)S(1)} %add_convert_fusion.after_ref), channel_id=1, source_target_pairs={{0,128},{16,912},{32,160},{48,944},{64,192},{80,976},{96,224},{112... | collective-permute-start | bytes 294920 | tf_op jit(solution)/shard_map/ppermute | solution.py:181
  69.2 35.2 %all-to-all-start.1 = ((bf16[16,32,1024]{2,1,0:T(8,128)(2,1)}), bf16[16,32,1024]{2,1,0:T(8,128)(2,1)S(1)}, u32[]{:S(2)}, u32[]{:S(2)}) async-start(bf16[16,32,1024]{2,1,0:T(8,128)(2,1)} %bitcast.9), calls=%async_computation.1 | async-start | bytes 2097152 | tf_op jit(solution)/shard_map/all_to_all | solution.py:261
  72.9 4.8 %copy-start.7 = (bf16[128,1536]{1,0:T(8,128)(2,1)}, bf16[128,1536]{1,0:T(8,128)(2,1)S(1)}, u32[]{:S(2)}) copy-start(bf16[128,1536]{1,0:T(8,128)(2,1)S(1)} %collective-permute-done.3.next_hbm) | copy-start | bytes 1179652
  81.1 36.7 %copy-start.3 = (s32[128,4]{0,1:T(4,128)S(1)}, s32[128,4]{0,1:T(4,128)}, u32[]{:S(2)}) copy-start(s32[128,4]{0,1:T(4,128)} %param.12) | copy-start | bytes 6148
  81.1 36.7 %copy-start.5 = (s32[128]{0:T(128)S(1)}, s32[128]{0:T(128)}, u32[]{:S(2)}) copy-start(s32[128]{0:T(128)} %param.13) | copy-start | bytes 1540
  82.2 9.9 %collective-permute-start.5 = (bf16[32,1536]{1,0:T(8,128)(2,1)S(1)}, bf16[32,1536]{1,0:T(8,128)(2,1)S(1)}, u32[]{:S(2)}, u32[]{:S(2)}) collective-permute-start(bf16[32,1536]{1,0:T(8,128)(2,1)S(1)} %fusion.2), channel_id=1, source_target_pairs={{0,128},{16,912},{32,160},{48,944},{64,192},{80,976},{96,224},{112... | collective-permute-start | bytes 294920 | tf_op jit(solution)/shard_map/ppermute | solution.py:181
  93.1 11.3 %collective-permute-start.6 = (bf16[32,1536]{1,0:T(8,128)(2,1)S(1)}, bf16[32,1536]{1,0:T(8,128)(2,1)S(1)}, u32[]{:S(2)}, u32[]{:S(2)}) collective-permute-start(bf16[32,1536]{1,0:T(8,128)(2,1)S(1)} %fusion.1), channel_id=1, source_target_pairs={{0,128},{16,912},{32,160},{48,944},{64,192},{80,976},{96,224},{112... | collective-permute-start | bytes 294920 | tf_op jit(solution)/shard_map/ppermute | solution.py:181
  105.3 9.6 %collective-permute-start.7 = (bf16[32,1536]{1,0:T(8,128)(2,1)S(1)}, bf16[32,1536]{1,0:T(8,128)(2,1)S(1)}, u32[]{:S(2)}, u32[]{:S(2)}) collective-permute-start(bf16[32,1536]{1,0:T(8,128)(2,1)S(1)} %fusion), channel_id=1, source_target_pairs={{0,128},{16,912},{32,160},{48,944},{64,192},{80,976},{96,224},{112... | collective-permute-start | bytes 294920 | tf_op jit(solution)/shard_map/ppermute | solution.py:181
  115.9 3.1 %collective-permute-start.8 = (bf16[16,1536]{1,0:T(8,128)(2,1)S(1)}, bf16[16,1536]{1,0:T(8,128)(2,1)S(1)}, u32[]{:S(2)}, u32[]{:S(2)}) collective-permute-start(bf16[16,1536]{1,0:T(8,128)(2,1)S(1)} %select_convert_fusion), channel_id=1, source_target_pairs={{0,16},{16,0},{32,48},{48,32},{64,80},{80,64},{96,112},{112,96},{1... | collective-permute-start | bytes 147464 | tf_op jit(solution)/shard_map/ppermute | solution.py:184

commit v5 on v4

--- a/solution.py
+++ b/solution.py
@@ -135,20 +135,6 @@
     keep_ref[...] = part(0)
 
 
-def fold_kernel(rows, core_ref, keep_ref, next_hbm, far_hbm, past_hbm, out_ref, next_ref, far_ref, past_ref, sems):
-    for copy in fetch([(next_hbm, next_ref), (far_hbm, far_ref), (past_hbm, past_ref)], sems):
-        copy.wait()
-    n = keep_ref.shape[0] // rows
-    for a in range(n):
-        here, before = pl.ds(a * rows, rows), pl.ds((a - 1 if a else n - 1) * rows, rows)
-        total = next_ref[here].astype(jnp.float32) + far_ref[here].astype(jnp.float32)
-        if a:
-            total = total + keep_ref[before] + past_ref[before].astype(jnp.float32)
-        else:
-            total = total + jnp.where(core_ref[0] == 1, keep_ref[before], 0.0)
-        out_ref[here] = total
-
-
 def call(kernel, outs, *args, ins=None, out_space=None, scratch=(), mib=40):
     shapes = [jax.ShapeDtypeStruct(*o) for o in outs]
     spaces = [s or pltpu.VMEM for s in (ins or [None] * len(args))]
@@ -242,14 +228,11 @@
     from_past, from_1, from_2 = along(to_past, -1), along(to_1, 1), along(to_2, 2)
     end = slice(block - 2 * rows, block)
     total = (from_past[end].astype(f32) + jnp.where(core == 0, keep[end], 0.0)).astype(bf16)
-    terms = call(
-        functools.partial(fold_kernel, 2 * rows),
-        [((block, 2 * ff), f32)],
-        core[None], keep, from_1, from_2, from_past,
-        ins=[pltpu.SMEM, None] + [hbm] * 3,
-        scratch=[vmem((block, 2 * ff), bf16)] * 3 + [dma((3,))],
-        mib=56,
-    ).reshape(n, 2 * rows, 2 * ff)
+    before = [keep[a * 2 * rows : (a + 1) * 2 * rows] for a in range(n)]
+    terms = jnp.concatenate([jnp.where(core == 1, before[-1], 0.0)] + before[:-1])
+    behind = jnp.concatenate([jnp.zeros_like(from_past[: 2 * rows]), from_past[: block - 2 * rows]])
+    terms = terms + from_1.astype(f32) + from_2.astype(f32) + behind.astype(f32)
+    terms = lax.optimization_barrier(terms).reshape(n, 2 * rows, 2 * ff)
     back = call(
         functools.partial(back_kernel, peers, cap, tok_dev),
         [((padded, width), bf16)],

time: 121 us -> 121 us (level)
  starting transfers between devices: 63.8 us -> 80.6 us
  waiting for transfers between devices: 34.8 us -> 22 us
  Pallas kernels: 15.4 us -> 12 us
    ppermute x7, waiting for transfers between devices: 22.7 us -> 9.87 us  [along(): return lax.ppermute(value, 'dp', pairs)]
    ppermute x7, starting transfers between devices: 37.4 us -> 48.3 us  [along(): return lax.ppermute(value, 'dp', pairs)]
    ppermute x2, starting transfers between devices: 15.2 us -> 21 us  [swap(): return lax.ppermute(value, 'dp', [(d, d ^ 1) for d in range(groups)])]
    pallas_call x7 -> x6, Pallas kernels: 15.4 us -> 12 us  [call(): pl.pallas_call(kernel, in_specs=[pl.BlockSpec(memory_space=s) for s in sp...]
    convert_element_type x3, other arithmetic: 2.92 us -> 0.96 us  [on_device(): total = total.astype(bf16) if t < n else total]
    add x0 -> x1, other arithmetic: none -> 1.26 us  [on_device(): terms = terms + from_1.astype(f32) + from_2.astype(f32) + behind.astype(f32)]
  transfers between devices with their start and end apart: 11 -> 11, of which waited for: 5 -> 5; matrix products, arithmetic and copies ran while one was open for 2% -> 3% of each run, Pallas kernels for 7% -> 4%
where the time goes in v5:
time: 121 us; the launch traced here: 120 us
  starting transfers between devices  80.6 us (67%)
  waiting for transfers between devices  22 us (18%)
  Pallas kernels  12 us (10%)
  other arithmetic  3.25 us (3%)
  local copies, waits for them, and re-layouts  1.69 us (1%)
    ppermute x7, starting transfers between devices, along(): return lax.ppermute(value, 'dp', pairs)  48.3 us
    ppermute x2, starting transfers between devices, swap(): return lax.ppermute(value, 'dp', [(d, d ^ 1) for d in range(groups)])  21 us
    all_to_all x1, waiting for transfers between devices, on_device(): lax.all_to_all(outgoing.reshape(peers, cap, width), 'expert', split_axis=...  12.1 us
    pallas_call x6, Pallas kernels, call(): pl.pallas_call(kernel, in_specs=[pl.BlockSpec(memory_space=s) for s in sp...  12 us
    ppermute x7, waiting for transfers between devices, along(): return lax.ppermute(value, 'dp', pairs)  9.87 us
    all_to_all x1, starting transfers between devices, on_device(): lax.all_to_all(outgoing.reshape(peers, cap, width), 'expert', split_axis=...  7.6 us
    all_to_all x1, starting transfers between devices, on_device(): lax.all_to_all(back.reshape(peers, cap, width), 'expert', split_axis=0, c...  3.66 us
  transfers between devices with their start and end apart: 11, of which 5 were waited for; matrix products, arithmetic and copies ran while one was open for 3% of the time, Pallas kernels for 4%

profile of v5, /device:TPU:1, one launch (start us, length us, event | category | flops | bytes accessed | tf_op | source)
XLA Modules:
  0.0 120.4 jit_solution(1806400074834835958)
XLA Ops:
  0.6 0.0 copy-start.1
  0.6 0.0 copy-start.3
  0.7 2.3 %shard_map.94 = bf16[512,1024]{1,0:T(8,128)(2,1)} custom-call(bf16[128,1024]{1,0:T(8,128)(2,1)} %tokens_hbm.1, s32[4,128]{1,0:T(4,128)} %bitcast.19, s32[1,128]{1,0:T(1,128)} %bitcast.23), custom_call_target="tpu_custom_call" | custom-call | tf_op jit(solution)/shard_map/pallas_call | solution.py:142
  2.9 7.6 %all-to-all-start = ((bf16[16,32,1024]{2,1,0:T(8,128)(2,1)}), bf16[16,32,1024]{2,1,0:T(8,128)(2,1)S(1)}, u32[]{:S(2)}, u32[]{:S(2)}) async-start(bf16[16,32,1024]{2,1,0:T(8,128)(2,1)} %bitcast.27), calls=%async_computation | async-start | bytes 2097152 | tf_op jit(solution)/shard_map/all_to_all | solution.py:192
  10.6 0.1 fusion.5.order_ref
  10.6 12.1 %all-to-all-done = bf16[16,32,1024]{2,1,0:T(8,128)(2,1)S(1)} async-done(((bf16[16,32,1024]{2,1,0:T(8,128)(2,1)}), bf16[16,32,1024]{2,1,0:T(8,128)(2,1)S(1)}, u32[]{:S(2)}, u32[]{:S(2)}) %all-to-all-start) | async-done | bytes 1048608 | tf_op jit(solution)/shard_map/all_to_all | solution.py:192
  22.7 0.0 copy-done.1
  22.7 0.0 copy-done.3
  22.7 0.0 copy-start
  22.7 3.6 %shard_map.95 = (bf16[256,512]{1,0:T(8,128)(2,1)S(1)}, bf16[256,2048]{1,0:T(8,128)(2,1)S(1)}) custom-call(bf16[512,1024]{1,0:T(8,128)(2,1)S(1)} %bitcast.17, s32[1,256]{1,0:T(1,128)S(1)} %bitcast.21, s32[1,1024]{1,0:T(1,128)S(1)} %fusion.5.order_ref, bf16[1024,768]{1,0:T(8,128)(2,1)} %bitcast.14, bf16[1024,768]{1,0:T(8,128)(2,1)} %bitcast.25, ...), custom_call_target="tpu_custom_call" | custom-call | tf_op jit(solution)/shard_map/pallas_call | solution.py:142
  26.3 13.2 %collective-permute-start = (bf16[256,2048]{1,0:T(8,128)(2,1)S(1)}, bf16[256,2048]{1,0:T(8,128)(2,1)S(1)}, u32[]{:S(2)}, u32[]{:S(2)}) collective-permute-start(bf16[256,2048]{1,0:T(8,128)(2,1)S(1)} %get-tuple-element.12.send_ref), channel_id=1, source_target_pairs={{0,16},{16,0},{32,48},{48,32},{64,80},{80,64},{96,112},{112,96},{1... | collective-permute-start | bytes 3145736 | tf_op jit(solution)/shard_map/ppermute | solution.py:170
  39.6 0.0 copy-done
  39.6 2.5 %shard_map.96.after_ref.grad_ref = bf16[256,1024]{1,0:T(8,128)(2,1)S(1)} custom-call(bf16[256,2048]{1,0:T(8,128)(2,1)S(1)} %get-tuple-element.12.send_ref, bf16[1024,768]{1,0:T(8,128)(2,1)S(1)} %bitcast.15, bf16[1024,768]{1,0:T(8,128)(2,1)} %bitcast.26), custom_call_target="tpu_custom_call" | custom-call | tf_op jit(solution)/shard_map/pallas_call | solution.py:142
  42.2 0.0 collective-permute-done.got_ref
  42.2 1.0 shard_map.97
  43.2 1.9 %collective-permute-start.1 = (bf16[128,1536]{1,0:T(8,128)(2,1)S(1)}, bf16[128,1536]{1,0:T(8,128)(2,1)}, u32[]{:S(2)}, u32[]{:S(2)}) collective-permute-start(bf16[128,1536]{1,0:T(8,128)(2,1)S(1)} %get-tuple-element.13), channel_id=1, source_target_pairs={{0,992},{16,48},{32,0},{48,80},{64,32},{80,112},{96,64},{112,144},... | collective-permute-start | bytes 1179656 | tf_op jit(solution)/shard_map/ppermute | solution.py:167
  45.2 13.5 %collective-permute-start.3 = (bf16[128,1536]{1,0:T(8,128)(2,1)S(1)}, bf16[128,1536]{1,0:T(8,128)(2,1)}, u32[]{:S(2)}, u32[]{:S(2)}) collective-permute-start(bf16[128,1536]{1,0:T(8,128)(2,1)S(1)} %get-tuple-element.15), channel_id=1, source_target_pairs={{0,32},{16,1008},{32,64},{48,16},{64,96},{80,48},{96,128},{112,80}... | collective-permute-start | bytes 1179656 | tf_op jit(solution)/shard_map/ppermute | solution.py:167
  58.6 3.8 %collective-permute-start.4 = (bf16[128,1536]{1,0:T(8,128)(2,1)S(1)}, bf16[128,1536]{1,0:T(8,128)(2,1)}, u32[]{:S(2)}, u32[]{:S(2)}) collective-permute-start(bf16[128,1536]{1,0:T(8,128)(2,1)S(1)} %get-tuple-element.16), channel_id=1, source_target_pairs={{0,64},{16,976},{32,96},{48,1008},{64,128},{80,16},{96,160},{112,4... | collective-permute-start | bytes 1179656 | tf_op jit(solution)/shard_map/ppermute | solution.py:167
  62.5 0.0 collective-permute-done.1
  62.5 0.9 add_convert_fusion
  63.4 1.4 %shard_map.98 = bf16[512,1024]{1,0:T(8,128)(2,1)} custom-call(s32[1,256]{1,0:T(1,128)S(1)} %bitcast.22, bf16[256,1024]{1,0:T(8,128)(2,1)S(1)} %shard_map.96.after_ref.grad_ref, bf16[32,1536]{1,0:T(8,128)(2,1)S(1)} %get-tuple-element.19.after_ref), custom_call_target="tpu_custom_call" | custom-call | tf_op jit(solution)/shard_map/pallas_call | solution.py:142
  64.8 5.4 %collective-permute-start.2 = (bf16[32,1536]{1,0:T(8,128)(2,1)S(1)}, bf16[32,1536]{1,0:T(8,128)(2,1)}, u32[]{:S(2)}, u32[]{:S(2)}) collective-permute-start(bf16[32,1536]{1,0:T(8,128)(2,1)S(1)} %get-tuple-element.19.after_ref), channel_id=1, source_target_pairs={{0,128},{16,912},{32,160},{48,944},{64,192},{80,976},{96,224},{112... | collective-permute-start | bytes 294920 | tf_op jit(solution)/shard_map/ppermute | solution.py:167
  70.2 3.7 %all-to-all-start.1 = ((bf16[16,32,1024]{2,1,0:T(8,128)(2,1)}), bf16[16,32,1024]{2,1,0:T(8,128)(2,1)S(1)}, u32[]{:S(2)}, u32[]{:S(2)}) async-start(bf16[16,32,1024]{2,1,0:T(8,128)(2,1)} %bitcast.8), calls=%async_computation.1 | async-start | bytes 2097152 | tf_op jit(solution)/shard_map/all_to_all | solution.py:244
  73.8 1.0 slice.57
  74.8 0.0 collective-permute-done.3
  74.8 2.8 %collective-permute-done.4 = bf16[128,1536]{1,0:T(8,128)(2,1)} collective-permute-done((bf16[128,1536]{1,0:T(8,128)(2,1)S(1)}, bf16[128,1536]{1,0:T(8,128)(2,1)}, u32[]{:S(2)}, u32[]{:S(2)}) %collective-permute-start.4) | collective-permute-done | bytes 393248 | tf_op jit(solution)/shard_map/ppermute | solution.py:167
  77.7 1.3 %fusion.1 = f32[128,1536]{1,0:T(8,128)S(1)} fusion(f32[96,1536]{1,0:T(8,128)S(1)} %slice.46, f32[32,1536]{1,0:T(8,128)S(1)} %get-tuple-element.20, bf16[128,1536]{1,0:T(8,128)(2,1)} %collective-permute-done.4, bf16[128,1536]{1,0:T(8,128)(2,1)} %collective-permute-done.3, bf16[96,1536]{1,0:T(8,128)(2,1)S(1)} %slice.57), kind=kLoop, calls=%fused_computation.2 | loop fusion | flops 1376256 | bytes 2654208 | tf_op jit(solution)/shard_map/add | solution.py:234
  78.9 0.0 copy-start.2
  79.0 0.0 copy-start.4
  79.0 0.0 collective-permute-done.2
  79.0 0.9 fusion.4
  79.9 7.9 %collective-permute-start.5 = (bf16[32,1536]{1,0:T(8,128)(2,1)S(1)}, bf16[32,1536]{1,0:T(8,128)(2,1)S(1)}, u32[]{:S(2)}, u32[]{:S(2)}) collective-permute-start(bf16[32,1536]{1,0:T(8,128)(2,1)S(1)} %fusion.4), channel_id=1, source_target_pairs={{0,128},{16,912},{32,160},{48,944},{64,192},{80,976},{96,224},{112... | collective-permute-start | bytes 294920 | tf_op jit(solution)/shard_map/ppermute | solution.py:167
  87.8 2.1 %collective-permute-done.5 = bf16[32,1536]{1,0:T(8,128)(2,1)S(1)} collective-permute-done((bf16[32,1536]{1,0:T(8,128)(2,1)S(1)}, bf16[32,1536]{1,0:T(8,128)(2,1)S(1)}, u32[]{:S(2)}, u32[]{:S(2)}) %collective-permute-start.5) | collective-permute-done | bytes 98336 | tf_op jit(solution)/shard_map/ppermute | solution.py:167
  89.9 8.2 %collective-permute-start.6 = (bf16[32,1536]{1,0:T(8,128)(2,1)S(1)}, bf16[32,1536]{1,0:T(8,128)(2,1)S(1)}, u32[]{:S(2)}, u32[]{:S(2)}) collective-permute-start(bf16[32,1536]{1,0:T(8,128)(2,1)S(1)} %fusion.3), channel_id=1, source_target_pairs={{0,128},{16,912},{32,160},{48,944},{64,192},{80,976},{96,224},{112... | collective-permute-start | bytes 294920 | tf_op jit(solution)/shard_map/ppermute | solution.py:167
  98.1 2.6 %collective-permute-done.6 = bf16[32,1536]{1,0:T(8,128)(2,1)S(1)} collective-permute-done((bf16[32,1536]{1,0:T(8,128)(2,1)S(1)}, bf16[32,1536]{1,0:T(8,128)(2,1)S(1)}, u32[]{:S(2)}, u32[]{:S(2)}) %collective-permute-start.6) | collective-permute-done | bytes 98336 | tf_op jit(solution)/shard_map/ppermute | solution.py:167
  100.7 0.0 all-to-all-done.1
  100.8 7.6 %collective-permute-start.7 = (bf16[32,1536]{1,0:T(8,128)(2,1)S(1)}, bf16[32,1536]{1,0:T(8,128)(2,1)S(1)}, u32[]{:S(2)}, u32[]{:S(2)}) collective-permute-start(bf16[32,1536]{1,0:T(8,128)(2,1)S(1)} %fusion.2), channel_id=1, source_target_pairs={{0,128},{16,912},{32,160},{48,944},{64,192},{80,976},{96,224},{112... | collective-permute-start | bytes 294920 | tf_op jit(solution)/shard_map/ppermute | solution.py:167
  108.4 2.3 %collective-permute-done.7 = bf16[32,1536]{1,0:T(8,128)(2,1)S(1)} collective-permute-done((bf16[32,1536]{1,0:T(8,128)(2,1)S(1)}, bf16[32,1536]{1,0:T(8,128)(2,1)S(1)}, u32[]{:S(2)}, u32[]{:S(2)}) %collective-permute-start.7) | collective-permute-done | bytes 98336 | tf_op jit(solution)/shard_map/ppermute | solution.py:167
  110.7 7.8 %collective-permute-start.8 = (bf16[16,1536]{1,0:T(8,128)(2,1)S(1)}, bf16[16,1536]{1,0:T(8,128)(2,1)S(1)}, u32[]{:S(2)}, u32[]{:S(2)}) collective-permute-start(bf16[16,1536]{1,0:T(8,128)(2,1)S(1)} %select_convert_fusion), channel_id=1, source_target_pairs={{0,16},{16,0},{32,48},{48,32},{64,80},{80,64},{96,112},{112,96},{1... | collective-permute-start | bytes 147464 | tf_op jit(solution)/shard_map/ppermute | solution.py:170
  118.5 0.0 copy-done.2
  118.6 0.0 copy-done.4
  118.6 1.2 shard_map.99
  119.8 0.0 collective-permute-done.8
  119.8 0.6 slice_bitcast_fusion
  (6 shorter events, 0.1 us)
Async XLA Ops:
  0.6 22.1 %copy-start.1 = (bf16[1,1,256,768]{3,2,1,0:T(8,128)(2,1)S(1)}, bf16[1,1,256,768]{3,2,1,0:T(8,128)(2,1)}, u32[]{:S(2)}) copy-start(bf16[1,1,256,768]{3,2,1,0:T(8,128)(2,1)} %param.10) | copy-start | bytes 1179652
  0.6 22.1 %copy-start.3 = (s32[1,1,256]{2,1,0:T(1,128)S(1)}, s32[1,1,256]{2,1,0:T(1,128)}, u32[]{:S(2)}) copy-start(s32[1,1,256]{2,1,0:T(1,128)} %param.11) | copy-start | bytes 3076
  2.9 19.8 %all-to-all-start = ((bf16[16,32,1024]{2,1,0:T(8,128)(2,1)}), bf16[16,32,1024]{2,1,0:T(8,128)(2,1)S(1)}, u32[]{:S(2)}, u32[]{:S(2)}) async-start(bf16[16,32,1024]{2,1,0:T(8,128)(2,1)} %bitcast.27), calls=%async_computation | async-start | bytes 2097152 | tf_op jit(solution)/shard_map/all_to_all | solution.py:192
  22.7 16.9 %copy-start = (bf16[1,1024,768]{2,1,0:T(8,128)(2,1)S(1)}, bf16[1,1024,768]{2,1,0:T(8,128)(2,1)}, u32[]{:S(2)}) copy-start(bf16[1,1024,768]{2,1,0:T(8,128)(2,1)} %param.8) | copy-start | bytes 4718596
  26.3 15.8 %collective-permute-start = (bf16[256,2048]{1,0:T(8,128)(2,1)S(1)}, bf16[256,2048]{1,0:T(8,128)(2,1)S(1)}, u32[]{:S(2)}, u32[]{:S(2)}) collective-permute-start(bf16[256,2048]{1,0:T(8,128)(2,1)S(1)} %get-tuple-element.12.send_ref), channel_id=1, source_target_pairs={{0,16},{16,0},{32,48},{48,32},{64,80},{80,64},{96,112},{112,96},{1... | collective-permute-start | bytes 3145736 | tf_op jit(solution)/shard_map/ppermute | solution.py:170
  43.2 19.3 %collective-permute-start.1 = (bf16[128,1536]{1,0:T(8,128)(2,1)S(1)}, bf16[128,1536]{1,0:T(8,128)(2,1)}, u32[]{:S(2)}, u32[]{:S(2)}) collective-permute-start(bf16[128,1536]{1,0:T(8,128)(2,1)S(1)} %get-tuple-element.13), channel_id=1, source_target_pairs={{0,992},{16,48},{32,0},{48,80},{64,32},{80,112},{96,64},{112,144},... | collective-permute-start | bytes 1179656 | tf_op jit(solution)/shard_map/ppermute | solution.py:167
  45.2 29.7 %collective-permute-start.3 = (bf16[128,1536]{1,0:T(8,128)(2,1)S(1)}, bf16[128,1536]{1,0:T(8,128)(2,1)}, u32[]{:S(2)}, u32[]{:S(2)}) collective-permute-start(bf16[128,1536]{1,0:T(8,128)(2,1)S(1)} %get-tuple-element.15), channel_id=1, source_target_pairs={{0,32},{16,1008},{32,64},{48,16},{64,96},{80,48},{96,128},{112,80}... | collective-permute-start | bytes 1179656 | tf_op jit(solution)/shard_map/ppermute | solution.py:167
  58.6 19.0 %collective-permute-start.4 = (bf16[128,1536]{1,0:T(8,128)(2,1)S(1)}, bf16[128,1536]{1,0:T(8,128)(2,1)}, u32[]{:S(2)}, u32[]{:S(2)}) collective-permute-start(bf16[128,1536]{1,0:T(8,128)(2,1)S(1)} %get-tuple-element.16), channel_id=1, source_target_pairs={{0,64},{16,976},{32,96},{48,1008},{64,128},{80,16},{96,160},{112,4... | collective-permute-start | bytes 1179656 | tf_op jit(solution)/shard_map/ppermute | solution.py:167
  64.8 14.2 %collective-permute-start.2 = (bf16[32,1536]{1,0:T(8,128)(2,1)S(1)}, bf16[32,1536]{1,0:T(8,128)(2,1)}, u32[]{:S(2)}, u32[]{:S(2)}) collective-permute-start(bf16[32,1536]{1,0:T(8,128)(2,1)S(1)} %get-tuple-element.19.after_ref), channel_id=1, source_target_pairs={{0,128},{16,912},{32,160},{48,944},{64,192},{80,976},{96,224},{112... | collective-permute-start | bytes 294920 | tf_op jit(solution)/shard_map/ppermute | solution.py:167
  70.2 30.6 %all-to-all-start.1 = ((bf16[16,32,1024]{2,1,0:T(8,128)(2,1)}), bf16[16,32,1024]{2,1,0:T(8,128)(2,1)S(1)}, u32[]{:S(2)}, u32[]{:S(2)}) async-start(bf16[16,32,1024]{2,1,0:T(8,128)(2,1)} %bitcast.8), calls=%async_computation.1 | async-start | bytes 2097152 | tf_op jit(solution)/shard_map/all_to_all | solution.py:244
  78.9 39.6 %copy-start.2 = (s32[128,4]{0,1:T(4,128)S(1)}, s32[128,4]{0,1:T(4,128)}, u32[]{:S(2)}) copy-start(s32[128,4]{0,1:T(4,128)} %param.12) | copy-start | bytes 6148
  79.0 39.6 %copy-start.4 = (s32[128]{0:T(128)S(1)}, s32[128]{0:T(128)}, u32[]{:S(2)}) copy-start(s32[128]{0:T(128)} %param.13) | copy-start | bytes 1540
  79.9 10.0 %collective-permute-start.5 = (bf16[32,1536]{1,0:T(8,128)(2,1)S(1)}, bf16[32,1536]{1,0:T(8,128)(2,1)S(1)}, u32[]{:S(2)}, u32[]{:S(2)}) collective-permute-start(bf16[32,1536]{1,0:T(8,128)(2,1)S(1)} %fusion.4), channel_id=1, source_target_pairs={{0,128},{16,912},{32,160},{48,944},{64,192},{80,976},{96,224},{112... | collective-permute-start | bytes 294920 | tf_op jit(solution)/shard_map/ppermute | solution.py:167
  89.9 10.8 %collective-permute-start.6 = (bf16[32,1536]{1,0:T(8,128)(2,1)S(1)}, bf16[32,1536]{1,0:T(8,128)(2,1)S(1)}, u32[]{:S(2)}, u32[]{:S(2)}) collective-permute-start(bf16[32,1536]{1,0:T(8,128)(2,1)S(1)} %fusion.3), channel_id=1, source_target_pairs={{0,128},{16,912},{32,160},{48,944},{64,192},{80,976},{96,224},{112... | collective-permute-start | bytes 294920 | tf_op jit(solution)/shard_map/ppermute | solution.py:167
  100.8 9.9 %collective-permute-start.7 = (bf16[32,1536]{1,0:T(8,128)(2,1)S(1)}, bf16[32,1536]{1,0:T(8,128)(2,1)S(1)}, u32[]{:S(2)}, u32[]{:S(2)}) collective-permute-start(bf16[32,1536]{1,0:T(8,128)(2,1)S(1)} %fusion.2), channel_id=1, source_target_pairs={{0,128},{16,912},{32,160},{48,944},{64,192},{80,976},{96,224},{112... | collective-permute-start | bytes 294920 | tf_op jit(solution)/shard_map/ppermute | solution.py:167
  110.7 9.0 %collective-permute-start.8 = (bf16[16,1536]{1,0:T(8,128)(2,1)S(1)}, bf16[16,1536]{1,0:T(8,128)(2,1)S(1)}, u32[]{:S(2)}, u32[]{:S(2)}) collective-permute-start(bf16[16,1536]{1,0:T(8,128)(2,1)S(1)} %select_convert_fusion), channel_id=1, source_target_pairs={{0,16},{16,0},{32,48},{48,32},{64,80},{80,64},{96,112},{112,96},{1... | collective-permute-start | bytes 147464 | tf_op jit(solution)/shard_map/ppermute | solution.py:170

commit v6 on v5

--- a/solution.py
+++ b/solution.py
@@ -197,8 +197,8 @@
     block = half // FAN
     which, q, i = m // half, (m % half) // block, (m % block) // (2 * rows)
     to_core = jnp.where(which == 0, core, 1 - core)
-    last = jnp.where(to_core == 0, chips // 2, 0)
-    ahead = jnp.where(q > 0, FAN * i + q, jnp.where(i == n - 1, last, FAN * (i + 1)))
+    first = jnp.where(q == 0, jnp.where(to_core == 0, chips // 2, 0), chips // 2 - 1)
+    ahead = jnp.where((q == 1) | (q == 2), FAN * i + q, jnp.where(i == 0, first, FAN * i - jnp.where(q == 0, 0, 1)))
     owner = (z + jnp.where(to_core == 0, ahead, -ahead) + chips) % chips
     order = (owner * 2 * rows + m % (2 * rows))[None, :]
     mine, send = call(
@@ -226,13 +226,12 @@
         mib=40,
     )
     from_past, from_1, from_2 = along(to_past, -1), along(to_1, 1), along(to_2, 2)
-    end = slice(block - 2 * rows, block)
-    total = (from_past[end].astype(f32) + jnp.where(core == 0, keep[end], 0.0)).astype(bf16)
-    before = [keep[a * 2 * rows : (a + 1) * 2 * rows] for a in range(n)]
-    terms = jnp.concatenate([jnp.where(core == 1, before[-1], 0.0)] + before[:-1])
-    behind = jnp.concatenate([jnp.zeros_like(from_past[: 2 * rows]), from_past[: block - 2 * rows]])
-    terms = terms + from_1.astype(f32) + from_2.astype(f32) + behind.astype(f32)
-    terms = lax.optimization_barrier(terms).reshape(n, 2 * rows, 2 * ff)
+    piece = 2 * rows
+    total = (from_past[:piece].astype(f32) + jnp.where(core == 0, keep[:piece], 0.0)).astype(bf16)
+    inner = jnp.arange(block)[:, None] >= piece
+    terms = jnp.where(inner, keep + from_past.astype(f32), jnp.where(core == 1, keep, 0.0))
+    terms = terms + from_1.astype(f32) + from_2.astype(f32)
+    terms = lax.optimization_barrier(terms).reshape(n, piece, 2 * ff)
     back = call(
         functools.partial(back_kernel, peers, cap, tok_dev),
         [((padded, width), bf16)],

time: 121 us -> 118 us (0.975)
  starting transfers between devices: 80.6 us -> 73.9 us
  waiting for transfers between devices: 22 us -> 26 us
    ppermute x2, starting transfers between devices: 21 us -> 15.2 us  [swap(): return lax.ppermute(value, 'dp', [(d, d ^ 1) for d in range(groups)])]
    ppermute x7, waiting for transfers between devices: 9.87 us -> 13.9 us  [along(): return lax.ppermute(value, 'dp', pairs)]
  transfers between devices with their start and end apart: 11 -> 11, of which waited for: 5 -> 5; matrix products, arithmetic and copies ran while one was open for 3% -> 1% of each run, Pallas kernels for 4% -> 4%
where the time goes in v6:
time: 118 us; the launch traced here: 117 us
  starting transfers between devices  73.9 us (63%)
  waiting for transfers between devices  26 us (22%)
  Pallas kernels  12 us (10%)
  other arithmetic  3.52 us (3%)
    ppermute x7, starting transfers between devices, along(): return lax.ppermute(value, 'dp', pairs)  47.5 us
    ppermute x2, starting transfers between devices, swap(): return lax.ppermute(value, 'dp', [(d, d ^ 1) for d in range(groups)])  15.2 us
    ppermute x7, waiting for transfers between devices, along(): return lax.ppermute(value, 'dp', pairs)  13.9 us
    all_to_all x1, waiting for transfers between devices, on_device(): lax.all_to_all(outgoing.reshape(peers, cap, width), 'expert', split_axis=...  12.1 us
    pallas_call x6, Pallas kernels, call(): pl.pallas_call(kernel, in_specs=[pl.BlockSpec(memory_space=s) for s in sp...  12 us
    all_to_all x1, starting transfers between devices, on_device(): lax.all_to_all(outgoing.reshape(peers, cap, width), 'expert', split_axis=...  7.6 us
    all_to_all x1, starting transfers between devices, on_device(): lax.all_to_all(back.reshape(peers, cap, width), 'expert', split_axis=0, c...  3.66 us
  transfers between devices with their start and end apart: 11, of which 5 were waited for; matrix products, arithmetic and copies ran while one was open for 1% of the time, Pallas kernels for 4%

profile of v6, /device:TPU:1, one launch (start us, length us, event | category | flops | bytes accessed | tf_op | source)
XLA Modules:
  0.0 117.1 jit_solution(17946541895752828020)
XLA Ops:
  0.6 0.0 copy-start.1
  0.6 0.0 copy-start.3
  0.7 2.3 %shard_map.94 = bf16[512,1024]{1,0:T(8,128)(2,1)} custom-call(bf16[128,1024]{1,0:T(8,128)(2,1)} %tokens_hbm.1, s32[4,128]{1,0:T(4,128)} %bitcast.19, s32[1,128]{1,0:T(1,128)} %bitcast.23), custom_call_target="tpu_custom_call" | custom-call | tf_op jit(solution)/shard_map/pallas_call | solution.py:142
  2.9 7.6 %all-to-all-start = ((bf16[16,32,1024]{2,1,0:T(8,128)(2,1)}), bf16[16,32,1024]{2,1,0:T(8,128)(2,1)S(1)}, u32[]{:S(2)}, u32[]{:S(2)}) async-start(bf16[16,32,1024]{2,1,0:T(8,128)(2,1)} %bitcast.27), calls=%async_computation | async-start | bytes 2097152 | tf_op jit(solution)/shard_map/all_to_all | solution.py:192
  10.6 0.1 fusion.3.order_ref
  10.6 12.1 %all-to-all-done = bf16[16,32,1024]{2,1,0:T(8,128)(2,1)S(1)} async-done(((bf16[16,32,1024]{2,1,0:T(8,128)(2,1)}), bf16[16,32,1024]{2,1,0:T(8,128)(2,1)S(1)}, u32[]{:S(2)}, u32[]{:S(2)}) %all-to-all-start) | async-done | bytes 1048608 | tf_op jit(solution)/shard_map/all_to_all | solution.py:192
  22.7 0.0 copy-done.1
  22.7 0.0 copy-done.3
  22.7 0.0 copy-start
  22.7 3.6 %shard_map.95 = (bf16[256,512]{1,0:T(8,128)(2,1)S(1)}, bf16[256,2048]{1,0:T(8,128)(2,1)S(1)}) custom-call(bf16[512,1024]{1,0:T(8,128)(2,1)S(1)} %bitcast.17, s32[1,256]{1,0:T(1,128)S(1)} %bitcast.21, s32[1,1024]{1,0:T(1,128)S(1)} %fusion.3.order_ref, bf16[1024,768]{1,0:T(8,128)(2,1)} %bitcast.14, bf16[1024,768]{1,0:T(8,128)(2,1)} %bitcast.25, ...), custom_call_target="tpu_custom_call" | custom-call | tf_op jit(solution)/shard_map/pallas_call | solution.py:142
  26.3 13.2 %collective-permute-start = (bf16[256,2048]{1,0:T(8,128)(2,1)S(1)}, bf16[256,2048]{1,0:T(8,128)(2,1)S(1)}, u32[]{:S(2)}, u32[]{:S(2)}) collective-permute-start(bf16[256,2048]{1,0:T(8,128)(2,1)S(1)} %get-tuple-element.12.send_ref), channel_id=1, source_target_pairs={{0,16},{16,0},{32,48},{48,32},{64,80},{80,64},{96,112},{112,96},{1... | collective-permute-start | bytes 3145736 | tf_op jit(solution)/shard_map/ppermute | solution.py:170
  39.6 0.0 copy-done
  39.6 2.5 %shard_map.96.after_ref.grad_ref = bf16[256,1024]{1,0:T(8,128)(2,1)S(1)} custom-call(bf16[256,2048]{1,0:T(8,128)(2,1)S(1)} %get-tuple-element.12.send_ref, bf16[1024,768]{1,0:T(8,128)(2,1)S(1)} %bitcast.15, bf16[1024,768]{1,0:T(8,128)(2,1)} %bitcast.26), custom_call_target="tpu_custom_call" | custom-call | tf_op jit(solution)/shard_map/pallas_call | solution.py:142
  42.2 0.0 collective-permute-done.got_ref
  42.2 1.0 shard_map.97
  43.2 1.9 %collective-permute-start.1 = (bf16[128,1536]{1,0:T(8,128)(2,1)S(1)}, bf16[128,1536]{1,0:T(8,128)(2,1)S(1)}, u32[]{:S(2)}, u32[]{:S(2)}) collective-permute-start(bf16[128,1536]{1,0:T(8,128)(2,1)S(1)} %get-tuple-element.13), channel_id=1, source_target_pairs={{0,992},{16,48},{32,0},{48,80},{64,32},{80,112},{96,64},{112,144},... | collective-permute-start | bytes 1179656 | tf_op jit(solution)/shard_map/ppermute | solution.py:167
  45.1 13.5 %collective-permute-start.3 = (bf16[128,1536]{1,0:T(8,128)(2,1)S(1)}, bf16[128,1536]{1,0:T(8,128)(2,1)}, u32[]{:S(2)}, u32[]{:S(2)}) collective-permute-start(bf16[128,1536]{1,0:T(8,128)(2,1)S(1)} %get-tuple-element.15), channel_id=1, source_target_pairs={{0,32},{16,1008},{32,64},{48,16},{64,96},{80,48},{96,128},{112,80}... | collective-permute-start | bytes 1179656 | tf_op jit(solution)/shard_map/ppermute | solution.py:167
  58.6 3.8 %collective-permute-start.4 = (bf16[128,1536]{1,0:T(8,128)(2,1)S(1)}, bf16[128,1536]{1,0:T(8,128)(2,1)}, u32[]{:S(2)}, u32[]{:S(2)}) collective-permute-start(bf16[128,1536]{1,0:T(8,128)(2,1)S(1)} %get-tuple-element.16), channel_id=1, source_target_pairs={{0,64},{16,976},{32,96},{48,1008},{64,128},{80,16},{96,160},{112,4... | collective-permute-start | bytes 1179656 | tf_op jit(solution)/shard_map/ppermute | solution.py:167
  62.4 0.0 collective-permute-done.1
  62.5 1.4 %shard_map.98 = bf16[512,1024]{1,0:T(8,128)(2,1)} custom-call(s32[1,256]{1,0:T(1,128)S(1)} %bitcast.22, bf16[256,1024]{1,0:T(8,128)(2,1)S(1)} %shard_map.96.after_ref.grad_ref, bf16[32,1536]{1,0:T(8,128)(2,1)S(1)} %add_convert_fusion.after_ref), custom_call_target="tpu_custom_call" | custom-call | tf_op jit(solution)/shard_map/pallas_call | solution.py:142
  63.9 5.3 %collective-permute-start.2 = (bf16[32,1536]{1,0:T(8,128)(2,1)S(1)}, bf16[32,1536]{1,0:T(8,128)(2,1)S(1)}, u32[]{:S(2)}, u32[]{:S(2)}) collective-permute-start(bf16[32,1536]{1,0:T(8,128)(2,1)S(1)} %add_convert_fusion.after_ref), channel_id=1, source_target_pairs={{0,128},{16,912},{32,160},{48,944},{64,192},{80,976},{96,224},{112... | collective-permute-start | bytes 294920 | tf_op jit(solution)/shard_map/ppermute | solution.py:167
  69.2 3.7 %all-to-all-start.1 = ((bf16[16,32,1024]{2,1,0:T(8,128)(2,1)}), bf16[16,32,1024]{2,1,0:T(8,128)(2,1)S(1)}, u32[]{:S(2)}, u32[]{:S(2)}) async-start(bf16[16,32,1024]{2,1,0:T(8,128)(2,1)} %bitcast.8), calls=%async_computation.1 | async-start | bytes 2097152 | tf_op jit(solution)/shard_map/all_to_all | solution.py:243
  72.8 0.0 collective-permute-done.3
  72.8 4.8 %collective-permute-done.4 = bf16[128,1536]{1,0:T(8,128)(2,1)} collective-permute-done((bf16[128,1536]{1,0:T(8,128)(2,1)S(1)}, bf16[128,1536]{1,0:T(8,128)(2,1)}, u32[]{:S(2)}, u32[]{:S(2)}) %collective-permute-start.4) | collective-permute-done | bytes 393248 | tf_op jit(solution)/shard_map/ppermute | solution.py:167
  77.7 1.4 %convert_add_fusion = f32[128,1536]{1,0:T(8,128)S(1)} fusion(bf16[128,1536]{1,0:T(8,128)(2,1)} %collective-permute-done.4, bf16[128,1536]{1,0:T(8,128)(2,1)} %collective-permute-done.3, f32[128,1536]{1,0:T(8,128)S(1)} %get-tuple-element.14, bf16[128,1536]{1,0:T(8,128)(2,1)S(1)} %collective-permute-done.1, pred[128]{0:T(512)(128)(4,1)S(1)} %iota_compare_fusion, ...), kind=kLoop, calls=%fused_computation | loop fusion | flops 1572864 | bytes 2752641 | tf_op jit(solution)/shard_map/add | solution.py:233
  79.1 0.0 copy-start.5
  79.1 0.0 copy-start.2
  79.2 0.0 copy-start.4
  79.2 0.0 collective-permute-done.2
  79.2 7.6 %collective-permute-start.5 = (bf16[32,1536]{1,0:T(8,128)(2,1)S(1)}, bf16[32,1536]{1,0:T(8,128)(2,1)S(1)}, u32[]{:S(2)}, u32[]{:S(2)}) collective-permute-start(bf16[32,1536]{1,0:T(8,128)(2,1)S(1)} %fusion.2), channel_id=1, source_target_pairs={{0,128},{16,912},{32,160},{48,944},{64,192},{80,976},{96,224},{112... | collective-permute-start | bytes 294920 | tf_op jit(solution)/shard_map/ppermute | solution.py:167
  86.8 2.6 %collective-permute-done.5 = bf16[32,1536]{1,0:T(8,128)(2,1)S(1)} collective-permute-done((bf16[32,1536]{1,0:T(8,128)(2,1)S(1)}, bf16[32,1536]{1,0:T(8,128)(2,1)S(1)}, u32[]{:S(2)}, u32[]{:S(2)}) %collective-permute-start.5) | collective-permute-done | bytes 98336 | tf_op jit(solution)/shard_map/ppermute | solution.py:167
  89.4 7.7 %collective-permute-start.6 = (bf16[32,1536]{1,0:T(8,128)(2,1)S(1)}, bf16[32,1536]{1,0:T(8,128)(2,1)S(1)}, u32[]{:S(2)}, u32[]{:S(2)}) collective-permute-start(bf16[32,1536]{1,0:T(8,128)(2,1)S(1)} %fusion.1), channel_id=1, source_target_pairs={{0,128},{16,912},{32,160},{48,944},{64,192},{80,976},{96,224},{112... | collective-permute-start | bytes 294920 | tf_op jit(solution)/shard_map/ppermute | solution.py:167
  97.1 0.0 copy-done.5
  97.1 2.9 %collective-permute-done.6 = bf16[32,1536]{1,0:T(8,128)(2,1)S(1)} collective-permute-done((bf16[32,1536]{1,0:T(8,128)(2,1)S(1)}, bf16[32,1536]{1,0:T(8,128)(2,1)S(1)}, u32[]{:S(2)}, u32[]{:S(2)}) %collective-permute-start.6) | collective-permute-done | bytes 98336 | tf_op jit(solution)/shard_map/ppermute | solution.py:167
  100.0 0.0 all-to-all-done.1
  100.0 1.0 fusion
  101.0 7.7 %collective-permute-start.7 = (bf16[32,1536]{1,0:T(8,128)(2,1)S(1)}, bf16[32,1536]{1,0:T(8,128)(2,1)S(1)}, u32[]{:S(2)}, u32[]{:S(2)}) collective-permute-start(bf16[32,1536]{1,0:T(8,128)(2,1)S(1)} %fusion), channel_id=1, source_target_pairs={{0,128},{16,912},{32,160},{48,944},{64,192},{80,976},{96,224},{112... | collective-permute-start | bytes 294920 | tf_op jit(solution)/shard_map/ppermute | solution.py:167
  108.7 3.6 %collective-permute-done.7 = bf16[32,1536]{1,0:T(8,128)(2,1)S(1)} collective-permute-done((bf16[32,1536]{1,0:T(8,128)(2,1)S(1)}, bf16[32,1536]{1,0:T(8,128)(2,1)S(1)}, u32[]{:S(2)}, u32[]{:S(2)}) %collective-permute-start.7) | collective-permute-done | bytes 98336 | tf_op jit(solution)/shard_map/ppermute | solution.py:167
  112.3 0.9 slice_add_fusion
  113.3 1.9 %collective-permute-start.8 = (bf16[16,1536]{1,0:T(8,128)(2,1)S(1)}, bf16[16,1536]{1,0:T(8,128)(2,1)S(1)}, u32[]{:S(2)}, u32[]{:S(2)}) collective-permute-start(bf16[16,1536]{1,0:T(8,128)(2,1)S(1)} %select_convert_fusion), channel_id=1, source_target_pairs={{0,16},{16,0},{32,48},{48,32},{64,80},{80,64},{96,112},{112,96},{1... | collective-permute-start | bytes 147464 | tf_op jit(solution)/shard_map/ppermute | solution.py:170
  115.2 0.0 copy-done.2
  115.2 0.0 copy-done.4
  115.2 1.2 %shard_map.99 = bf16[128,1024]{1,0:T(8,128)(2,1)} custom-call(bf16[512,1024]{1,0:T(8,128)(2,1)S(1)} %bitcast.16, s32[4,128]{1,0:T(4,128)S(1)} %bitcast.20, s32[1,128]{1,0:T(1,128)S(1)} %bitcast.24), custom_call_target="tpu_custom_call" | custom-call | tf_op jit(solution)/shard_map/pallas_call | solution.py:142
  116.4 0.0 collective-permute-done.8
  116.4 0.6 slice_bitcast_fusion
  (6 shorter events, 0.1 us)
Async XLA Ops:
  0.6 22.1 %copy-start.1 = (bf16[1,1,256,768]{3,2,1,0:T(8,128)(2,1)S(1)}, bf16[1,1,256,768]{3,2,1,0:T(8,128)(2,1)}, u32[]{:S(2)}) copy-start(bf16[1,1,256,768]{3,2,1,0:T(8,128)(2,1)} %param.10) | copy-start | bytes 1179652
  0.6 22.1 %copy-start.3 = (s32[1,1,256]{2,1,0:T(1,128)S(1)}, s32[1,1,256]{2,1,0:T(1,128)}, u32[]{:S(2)}) copy-start(s32[1,1,256]{2,1,0:T(1,128)} %param.11) | copy-start | bytes 3076
  2.9 19.8 %all-to-all-start = ((bf16[16,32,1024]{2,1,0:T(8,128)(2,1)}), bf16[16,32,1024]{2,1,0:T(8,128)(2,1)S(1)}, u32[]{:S(2)}, u32[]{:S(2)}) async-start(bf16[16,32,1024]{2,1,0:T(8,128)(2,1)} %bitcast.27), calls=%async_computation | async-start | bytes 2097152 | tf_op jit(solution)/shard_map/all_to_all | solution.py:192
  22.7 16.9 %copy-start = (bf16[1,1024,768]{2,1,0:T(8,128)(2,1)S(1)}, bf16[1,1024,768]{2,1,0:T(8,128)(2,1)}, u32[]{:S(2)}) copy-start(bf16[1,1024,768]{2,1,0:T(8,128)(2,1)} %param.8) | copy-start | bytes 4718596
  26.3 15.8 %collective-permute-start = (bf16[256,2048]{1,0:T(8,128)(2,1)S(1)}, bf16[256,2048]{1,0:T(8,128)(2,1)S(1)}, u32[]{:S(2)}, u32[]{:S(2)}) collective-permute-start(bf16[256,2048]{1,0:T(8,128)(2,1)S(1)} %get-tuple-element.12.send_ref), channel_id=1, source_target_pairs={{0,16},{16,0},{32,48},{48,32},{64,80},{80,64},{96,112},{112,96},{1... | collective-permute-start | bytes 3145736 | tf_op jit(solution)/shard_map/ppermute | solution.py:170
  43.2 19.2 %collective-permute-start.1 = (bf16[128,1536]{1,0:T(8,128)(2,1)S(1)}, bf16[128,1536]{1,0:T(8,128)(2,1)S(1)}, u32[]{:S(2)}, u32[]{:S(2)}) collective-permute-start(bf16[128,1536]{1,0:T(8,128)(2,1)S(1)} %get-tuple-element.13), channel_id=1, source_target_pairs={{0,992},{16,48},{32,0},{48,80},{64,32},{80,112},{96,64},{112,144},... | collective-permute-start | bytes 1179656 | tf_op jit(solution)/shard_map/ppermute | solution.py:167
  45.1 27.7 %collective-permute-start.3 = (bf16[128,1536]{1,0:T(8,128)(2,1)S(1)}, bf16[128,1536]{1,0:T(8,128)(2,1)}, u32[]{:S(2)}, u32[]{:S(2)}) collective-permute-start(bf16[128,1536]{1,0:T(8,128)(2,1)S(1)} %get-tuple-element.15), channel_id=1, source_target_pairs={{0,32},{16,1008},{32,64},{48,16},{64,96},{80,48},{96,128},{112,80}... | collective-permute-start | bytes 1179656 | tf_op jit(solution)/shard_map/ppermute | solution.py:167
  58.6 19.1 %collective-permute-start.4 = (bf16[128,1536]{1,0:T(8,128)(2,1)S(1)}, bf16[128,1536]{1,0:T(8,128)(2,1)}, u32[]{:S(2)}, u32[]{:S(2)}) collective-permute-start(bf16[128,1536]{1,0:T(8,128)(2,1)S(1)} %get-tuple-element.16), channel_id=1, source_target_pairs={{0,64},{16,976},{32,96},{48,1008},{64,128},{80,16},{96,160},{112,4... | collective-permute-start | bytes 1179656 | tf_op jit(solution)/shard_map/ppermute | solution.py:167
  63.9 15.3 %collective-permute-start.2 = (bf16[32,1536]{1,0:T(8,128)(2,1)S(1)}, bf16[32,1536]{1,0:T(8,128)(2,1)S(1)}, u32[]{:S(2)}, u32[]{:S(2)}) collective-permute-start(bf16[32,1536]{1,0:T(8,128)(2,1)S(1)} %add_convert_fusion.after_ref), channel_id=1, source_target_pairs={{0,128},{16,912},{32,160},{48,944},{64,192},{80,976},{96,224},{112... | collective-permute-start | bytes 294920 | tf_op jit(solution)/shard_map/ppermute | solution.py:167
  69.2 30.9 %all-to-all-start.1 = ((bf16[16,32,1024]{2,1,0:T(8,128)(2,1)}), bf16[16,32,1024]{2,1,0:T(8,128)(2,1)S(1)}, u32[]{:S(2)}, u32[]{:S(2)}) async-start(bf16[16,32,1024]{2,1,0:T(8,128)(2,1)} %bitcast.8), calls=%async_computation.1 | async-start | bytes 2097152 | tf_op jit(solution)/shard_map/all_to_all | solution.py:243
  79.1 18.0 %copy-start.5 = (f32[128,1536]{1,0:T(8,128)}, f32[128,1536]{1,0:T(8,128)S(1)}, u32[]{:S(2)}) copy-start(f32[128,1536]{1,0:T(8,128)S(1)} %convert_add_fusion) | copy-start | bytes 2359300
  79.1 36.1 %copy-start.2 = (s32[128,4]{0,1:T(4,128)S(1)}, s32[128,4]{0,1:T(4,128)}, u32[]{:S(2)}) copy-start(s32[128,4]{0,1:T(4,128)} %param.12) | copy-start | bytes 6148
  79.2 36.1 %copy-start.4 = (s32[128]{0:T(128)S(1)}, s32[128]{0:T(128)}, u32[]{:S(2)}) copy-start(s32[128]{0:T(128)} %param.13) | copy-start | bytes 1540
  79.2 10.2 %collective-permute-start.5 = (bf16[32,1536]{1,0:T(8,128)(2,1)S(1)}, bf16[32,1536]{1,0:T(8,128)(2,1)S(1)}, u32[]{:S(2)}, u32[]{:S(2)}) collective-permute-start(bf16[32,1536]{1,0:T(8,128)(2,1)S(1)} %fusion.2), channel_id=1, source_target_pairs={{0,128},{16,912},{32,160},{48,944},{64,192},{80,976},{96,224},{112... | collective-permute-start | bytes 294920 | tf_op jit(solution)/shard_map/ppermute | solution.py:167
  89.4 10.6 %collective-permute-start.6 = (bf16[32,1536]{1,0:T(8,128)(2,1)S(1)}, bf16[32,1536]{1,0:T(8,128)(2,1)S(1)}, u32[]{:S(2)}, u32[]{:S(2)}) collective-permute-start(bf16[32,1536]{1,0:T(8,128)(2,1)S(1)} %fusion.1), channel_id=1, source_target_pairs={{0,128},{16,912},{32,160},{48,944},{64,192},{80,976},{96,224},{112... | collective-permute-start | bytes 294920 | tf_op jit(solution)/shard_map/ppermute | solution.py:167
  101.0 11.3 %collective-permute-start.7 = (bf16[32,1536]{1,0:T(8,128)(2,1)S(1)}, bf16[32,1536]{1,0:T(8,128)(2,1)S(1)}, u32[]{:S(2)}, u32[]{:S(2)}) collective-permute-start(bf16[32,1536]{1,0:T(8,128)(2,1)S(1)} %fusion), channel_id=1, source_target_pairs={{0,128},{16,912},{32,160},{48,944},{64,192},{80,976},{96,224},{112... | collective-permute-start | bytes 294920 | tf_op jit(solution)/shard_map/ppermute | solution.py:167
  113.3 3.1 %collective-permute-start.8 = (bf16[16,1536]{1,0:T(8,128)(2,1)S(1)}, bf16[16,1536]{1,0:T(8,128)(2,1)S(1)}, u32[]{:S(2)}, u32[]{:S(2)}) collective-permute-start(bf16[16,1536]{1,0:T(8,128)(2,1)S(1)} %select_convert_fusion), channel_id=1, source_target_pairs={{0,16},{16,0},{32,48},{48,32},{64,80},{80,64},{96,112},{112,96},{1... | collective-permute-start | bytes 147464 | tf_op jit(solution)/shard_map/ppermute | solution.py:170

commit v7 on v6

--- a/solution.py
+++ b/solution.py
@@ -8,7 +8,7 @@
 from jax.sharding import PartitionSpec as P
 
 FAN = 4
-TIE = 3
+TIE = 4
 BLOCKS = 4
 
 

time: 118 us -> 117 us (level)
  waiting for transfers between devices: 26 us -> 33.5 us
  starting transfers between devices: 73.9 us -> 68.8 us
  other arithmetic: 3.52 us -> 0.55 us
    ppermute x7, waiting for transfers between devices: 13.9 us -> 21.4 us  [along(): return lax.ppermute(value, 'dp', pairs)]
    ppermute x7, starting transfers between devices: 47.5 us -> 42.4 us  [along(): return lax.ppermute(value, 'dp', pairs)]
  transfers between devices with their start and end apart: 11 -> 11, of which waited for: 5 -> 5; matrix products, arithmetic and copies ran while one was open for 1% -> 0% of each run, Pallas kernels for 4% -> 4%
where the time goes in v7:
time: 117 us; the launch traced here: 116 us
  starting transfers between devices  68.8 us (59%)
  waiting for transfers between devices  33.5 us (29%)
  Pallas kernels  12 us (10%)
    ppermute x7, starting transfers between devices, along(): return lax.ppermute(value, 'dp', pairs)  42.4 us
    ppermute x7, waiting for transfers between devices, along(): return lax.ppermute(value, 'dp', pairs)  21.4 us
    ppermute x2, starting transfers between devices, swap(): return lax.ppermute(value, 'dp', [(d, d ^ 1) for d in range(groups)])  15.2 us
    all_to_all x1, waiting for transfers between devices, on_device(): lax.all_to_all(outgoing.reshape(peers, cap, width), 'expert', split_axis=...  12.1 us
    pallas_call x6, Pallas kernels, call(): pl.pallas_call(kernel, in_specs=[pl.BlockSpec(memory_space=s) for s in sp...  12 us
    all_to_all x1, starting transfers between devices, on_device(): lax.all_to_all(outgoing.reshape(peers, cap, width), 'expert', split_axis=...  7.6 us
    all_to_all x1, starting transfers between devices, on_device(): lax.all_to_all(back.reshape(peers, cap, width), 'expert', split_axis=0, c...  3.66 us
  transfers between devices with their start and end apart: 11, of which 5 were waited for; matrix products, arithmetic and copies ran while one was open for 0% of the time, Pallas kernels for 4%

profile of v7, /device:TPU:1, one launch (start us, length us, event | category | flops | bytes accessed | tf_op | source)
XLA Modules:
  0.0 116.5 jit_solution(4193635529695703230)
XLA Ops:
  0.6 0.0 copy-start.1
  0.6 0.0 copy-start.3
  0.7 2.3 %shard_map.94 = bf16[512,1024]{1,0:T(8,128)(2,1)} custom-call(bf16[128,1024]{1,0:T(8,128)(2,1)} %tokens_hbm.1, s32[4,128]{1,0:T(4,128)} %bitcast.19, s32[1,128]{1,0:T(1,128)} %bitcast.23), custom_call_target="tpu_custom_call" | custom-call | tf_op jit(solution)/shard_map/pallas_call | solution.py:142
  2.9 7.6 %all-to-all-start = ((bf16[16,32,1024]{2,1,0:T(8,128)(2,1)}), bf16[16,32,1024]{2,1,0:T(8,128)(2,1)S(1)}, u32[]{:S(2)}, u32[]{:S(2)}) async-start(bf16[16,32,1024]{2,1,0:T(8,128)(2,1)} %bitcast.27), calls=%async_computation | async-start | bytes 2097152 | tf_op jit(solution)/shard_map/all_to_all | solution.py:192
  10.6 0.1 fusion.3.order_ref
  10.6 12.1 %all-to-all-done = bf16[16,32,1024]{2,1,0:T(8,128)(2,1)S(1)} async-done(((bf16[16,32,1024]{2,1,0:T(8,128)(2,1)}), bf16[16,32,1024]{2,1,0:T(8,128)(2,1)S(1)}, u32[]{:S(2)}, u32[]{:S(2)}) %all-to-all-start) | async-done | bytes 1048608 | tf_op jit(solution)/shard_map/all_to_all | solution.py:192
  22.7 0.0 copy-done.1
  22.7 0.0 copy-done.3
  22.7 0.0 copy-start
  22.7 3.6 %shard_map.95 = (bf16[256,512]{1,0:T(8,128)(2,1)S(1)}, bf16[256,2048]{1,0:T(8,128)(2,1)S(1)}) custom-call(bf16[512,1024]{1,0:T(8,128)(2,1)S(1)} %bitcast.17, s32[1,256]{1,0:T(1,128)S(1)} %bitcast.21, s32[1,1024]{1,0:T(1,128)S(1)} %fusion.3.order_ref, bf16[1024,768]{1,0:T(8,128)(2,1)} %bitcast.14, bf16[1024,768]{1,0:T(8,128)(2,1)} %bitcast.25, ...), custom_call_target="tpu_custom_call" | custom-call | tf_op jit(solution)/shard_map/pallas_call | solution.py:142
  26.4 13.2 %collective-permute-start = (bf16[256,2048]{1,0:T(8,128)(2,1)S(1)}, bf16[256,2048]{1,0:T(8,128)(2,1)S(1)}, u32[]{:S(2)}, u32[]{:S(2)}) collective-permute-start(bf16[256,2048]{1,0:T(8,128)(2,1)S(1)} %get-tuple-element.12.send_ref), channel_id=1, source_target_pairs={{0,16},{16,0},{32,48},{48,32},{64,80},{80,64},{96,112},{112,96},{1... | collective-permute-start | bytes 3145736 | tf_op jit(solution)/shard_map/ppermute | solution.py:170
  39.6 0.0 copy-done
  39.6 2.5 %shard_map.96.after_ref.grad_ref = bf16[256,1024]{1,0:T(8,128)(2,1)S(1)} custom-call(bf16[256,2048]{1,0:T(8,128)(2,1)S(1)} %get-tuple-element.12.send_ref, bf16[1024,768]{1,0:T(8,128)(2,1)S(1)} %bitcast.15, bf16[1024,768]{1,0:T(8,128)(2,1)} %bitcast.26), custom_call_target="tpu_custom_call" | custom-call | tf_op jit(solution)/shard_map/pallas_call | solution.py:142
  42.2 0.0 collective-permute-done.got_ref
  42.2 1.0 shard_map.97
  43.2 1.9 %collective-permute-start.1 = (bf16[128,1536]{1,0:T(8,128)(2,1)S(1)}, bf16[128,1536]{1,0:T(8,128)(2,1)S(1)}, u32[]{:S(2)}, u32[]{:S(2)}) collective-permute-start(bf16[128,1536]{1,0:T(8,128)(2,1)S(1)} %get-tuple-element.13), channel_id=1, source_target_pairs={{0,992},{16,48},{32,0},{48,80},{64,32},{80,112},{96,64},{112,144},... | collective-permute-start | bytes 1179656 | tf_op jit(solution)/shard_map/ppermute | solution.py:167
  45.1 13.5 %collective-permute-start.3 = (bf16[128,1536]{1,0:T(8,128)(2,1)S(1)}, bf16[128,1536]{1,0:T(8,128)(2,1)S(1)}, u32[]{:S(2)}, u32[]{:S(2)}) collective-permute-start(bf16[128,1536]{1,0:T(8,128)(2,1)S(1)} %get-tuple-element.15), channel_id=1, source_target_pairs={{0,32},{16,1008},{32,64},{48,16},{64,96},{80,48},{96,128},{112,80}... | collective-permute-start | bytes 1179656 | tf_op jit(solution)/shard_map/ppermute | solution.py:167
  58.6 3.8 %collective-permute-start.4 = (bf16[128,1536]{1,0:T(8,128)(2,1)S(1)}, bf16[128,1536]{1,0:T(8,128)(2,1)S(1)}, u32[]{:S(2)}, u32[]{:S(2)}) collective-permute-start(bf16[128,1536]{1,0:T(8,128)(2,1)S(1)} %get-tuple-element.16), channel_id=1, source_target_pairs={{0,64},{16,976},{32,96},{48,1008},{64,128},{80,16},{96,160},{112,4... | collective-permute-start | bytes 1179656 | tf_op jit(solution)/shard_map/ppermute | solution.py:167
  62.4 0.0 collective-permute-done.1
  62.5 5.3 %collective-permute-start.2 = (bf16[32,1536]{1,0:T(8,128)(2,1)S(1)}, bf16[32,1536]{1,0:T(8,128)(2,1)S(1)}, u32[]{:S(2)}, u32[]{:S(2)}) collective-permute-start(bf16[32,1536]{1,0:T(8,128)(2,1)S(1)} %add_convert_fusion.after_ref), channel_id=1, source_target_pairs={{0,128},{16,912},{32,160},{48,944},{64,192},{80,976},{96,224},{112... | collective-permute-start | bytes 294920 | tf_op jit(solution)/shard_map/ppermute | solution.py:167
  67.8 0.0 collective-permute-done.3
  67.8 9.9 %collective-permute-done.4 = bf16[128,1536]{1,0:T(8,128)(2,1)S(1)} collective-permute-done((bf16[128,1536]{1,0:T(8,128)(2,1)S(1)}, bf16[128,1536]{1,0:T(8,128)(2,1)S(1)}, u32[]{:S(2)}, u32[]{:S(2)}) %collective-permute-start.4) | collective-permute-done | bytes 393248 | tf_op jit(solution)/shard_map/ppermute | solution.py:167
  77.7 0.3 convert_add_fusion
  78.0 0.7 collective-permute-done.2
  78.8 7.7 %collective-permute-start.5 = (bf16[32,1536]{1,0:T(8,128)(2,1)S(1)}, bf16[32,1536]{1,0:T(8,128)(2,1)S(1)}, u32[]{:S(2)}, u32[]{:S(2)}) collective-permute-start(bf16[32,1536]{1,0:T(8,128)(2,1)S(1)} %fusion.2), channel_id=1, source_target_pairs={{0,128},{16,912},{32,160},{48,944},{64,192},{80,976},{96,224},{112... | collective-permute-start | bytes 294920 | tf_op jit(solution)/shard_map/ppermute | solution.py:167
  86.5 1.4 %shard_map.98 = bf16[512,1024]{1,0:T(8,128)(2,1)} custom-call(s32[1,256]{1,0:T(1,128)S(1)} %bitcast.22, bf16[256,1024]{1,0:T(8,128)(2,1)S(1)} %shard_map.96.after_ref.grad_ref, bf16[32,1536]{1,0:T(8,128)(2,1)S(1)} %add_convert_fusion.after_ref), custom_call_target="tpu_custom_call" | custom-call | tf_op jit(solution)/shard_map/pallas_call | solution.py:142
  87.9 0.0 copy-start.2
  87.9 0.0 copy-start.4
  87.9 3.7 %all-to-all-start.1 = ((bf16[16,32,1024]{2,1,0:T(8,128)(2,1)}), bf16[16,32,1024]{2,1,0:T(8,128)(2,1)S(1)}, u32[]{:S(2)}, u32[]{:S(2)}) async-start(bf16[16,32,1024]{2,1,0:T(8,128)(2,1)} %bitcast.8), calls=%async_computation.1 | async-start | bytes 2097152 | tf_op jit(solution)/shard_map/all_to_all | solution.py:243
  91.6 0.0 collective-permute-done.5
  91.6 5.2 %collective-permute-start.6 = (bf16[32,1536]{1,0:T(8,128)(2,1)S(1)}, bf16[32,1536]{1,0:T(8,128)(2,1)S(1)}, u32[]{:S(2)}, u32[]{:S(2)}) collective-permute-start(bf16[32,1536]{1,0:T(8,128)(2,1)S(1)} %fusion.1), channel_id=1, source_target_pairs={{0,128},{16,912},{32,160},{48,944},{64,192},{80,976},{96,224},{112... | collective-permute-start | bytes 294920 | tf_op jit(solution)/shard_map/ppermute | solution.py:167
  96.8 5.2 %collective-permute-done.6 = bf16[32,1536]{1,0:T(8,128)(2,1)S(1)} collective-permute-done((bf16[32,1536]{1,0:T(8,128)(2,1)S(1)}, bf16[32,1536]{1,0:T(8,128)(2,1)S(1)}, u32[]{:S(2)}, u32[]{:S(2)}) %collective-permute-start.6) | collective-permute-done | bytes 98336 | tf_op jit(solution)/shard_map/ppermute | solution.py:167
  102.0 5.0 %collective-permute-start.7 = (bf16[32,1536]{1,0:T(8,128)(2,1)S(1)}, bf16[32,1536]{1,0:T(8,128)(2,1)S(1)}, u32[]{:S(2)}, u32[]{:S(2)}) collective-permute-start(bf16[32,1536]{1,0:T(8,128)(2,1)S(1)} %fusion), channel_id=1, source_target_pairs={{0,128},{16,912},{32,160},{48,944},{64,192},{80,976},{96,224},{112... | collective-permute-start | bytes 294920 | tf_op jit(solution)/shard_map/ppermute | solution.py:167
  107.0 5.6 %collective-permute-done.7 = bf16[32,1536]{1,0:T(8,128)(2,1)S(1)} collective-permute-done((bf16[32,1536]{1,0:T(8,128)(2,1)S(1)}, bf16[32,1536]{1,0:T(8,128)(2,1)S(1)}, u32[]{:S(2)}, u32[]{:S(2)}) %collective-permute-start.7) | collective-permute-done | bytes 98336 | tf_op jit(solution)/shard_map/ppermute | solution.py:167
  112.6 0.0 all-to-all-done.1
  112.7 1.9 %collective-permute-start.8 = (bf16[16,1536]{1,0:T(8,128)(2,1)S(1)}, bf16[16,1536]{1,0:T(8,128)(2,1)S(1)}, u32[]{:S(2)}, u32[]{:S(2)}) collective-permute-start(bf16[16,1536]{1,0:T(8,128)(2,1)S(1)} %select_convert_fusion), channel_id=1, source_target_pairs={{0,16},{16,0},{32,48},{48,32},{64,80},{80,64},{96,112},{112,96},{1... | collective-permute-start | bytes 147464 | tf_op jit(solution)/shard_map/ppermute | solution.py:170
  114.6 0.0 copy-done.2
  114.6 0.0 copy-done.4
  114.6 1.2 %shard_map.99 = bf16[128,1024]{1,0:T(8,128)(2,1)} custom-call(bf16[512,1024]{1,0:T(8,128)(2,1)S(1)} %bitcast.16, s32[4,128]{1,0:T(4,128)S(1)} %bitcast.20, s32[1,128]{1,0:T(1,128)S(1)} %bitcast.24), custom_call_target="tpu_custom_call" | custom-call | tf_op jit(solution)/shard_map/pallas_call | solution.py:142
  115.8 0.0 collective-permute-done.8
  115.8 0.6 slice_bitcast_fusion
  (8 shorter events, 0.2 us)
Async XLA Ops:
  0.6 22.1 %copy-start.1 = (bf16[1,1,256,768]{3,2,1,0:T(8,128)(2,1)S(1)}, bf16[1,1,256,768]{3,2,1,0:T(8,128)(2,1)}, u32[]{:S(2)}) copy-start(bf16[1,1,256,768]{3,2,1,0:T(8,128)(2,1)} %param.10) | copy-start | bytes 1179652
  0.6 22.1 %copy-start.3 = (s32[1,1,256]{2,1,0:T(1,128)S(1)}, s32[1,1,256]{2,1,0:T(1,128)}, u32[]{:S(2)}) copy-start(s32[1,1,256]{2,1,0:T(1,128)} %param.11) | copy-start | bytes 3076
  2.9 19.8 %all-to-all-start = ((bf16[16,32,1024]{2,1,0:T(8,128)(2,1)}), bf16[16,32,1024]{2,1,0:T(8,128)(2,1)S(1)}, u32[]{:S(2)}, u32[]{:S(2)}) async-start(bf16[16,32,1024]{2,1,0:T(8,128)(2,1)} %bitcast.27), calls=%async_computation | async-start | bytes 2097152 | tf_op jit(solution)/shard_map/all_to_all | solution.py:192
  22.7 16.9 %copy-start = (bf16[1,1024,768]{2,1,0:T(8,128)(2,1)S(1)}, bf16[1,1024,768]{2,1,0:T(8,128)(2,1)}, u32[]{:S(2)}) copy-start(bf16[1,1024,768]{2,1,0:T(8,128)(2,1)} %param.8) | copy-start | bytes 4718596
  26.4 15.8 %collective-permute-start = (bf16[256,2048]{1,0:T(8,128)(2,1)S(1)}, bf16[256,2048]{1,0:T(8,128)(2,1)S(1)}, u32[]{:S(2)}, u32[]{:S(2)}) collective-permute-start(bf16[256,2048]{1,0:T(8,128)(2,1)S(1)} %get-tuple-element.12.send_ref), channel_id=1, source_target_pairs={{0,16},{16,0},{32,48},{48,32},{64,80},{80,64},{96,112},{112,96},{1... | collective-permute-start | bytes 3145736 | tf_op jit(solution)/shard_map/ppermute | solution.py:170
  43.2 19.2 %collective-permute-start.1 = (bf16[128,1536]{1,0:T(8,128)(2,1)S(1)}, bf16[128,1536]{1,0:T(8,128)(2,1)S(1)}, u32[]{:S(2)}, u32[]{:S(2)}) collective-permute-start(bf16[128,1536]{1,0:T(8,128)(2,1)S(1)} %get-tuple-element.13), channel_id=1, source_target_pairs={{0,992},{16,48},{32,0},{48,80},{64,32},{80,112},{96,64},{112,144},... | collective-permute-start | bytes 1179656 | tf_op jit(solution)/shard_map/ppermute | solution.py:167
  45.1 22.6 %collective-permute-start.3 = (bf16[128,1536]{1,0:T(8,128)(2,1)S(1)}, bf16[128,1536]{1,0:T(8,128)(2,1)S(1)}, u32[]{:S(2)}, u32[]{:S(2)}) collective-permute-start(bf16[128,1536]{1,0:T(8,128)(2,1)S(1)} %get-tuple-element.15), channel_id=1, source_target_pairs={{0,32},{16,1008},{32,64},{48,16},{64,96},{80,48},{96,128},{112,80}... | collective-permute-start | bytes 1179656 | tf_op jit(solution)/shard_map/ppermute | solution.py:167
  58.6 19.1 %collective-permute-start.4 = (bf16[128,1536]{1,0:T(8,128)(2,1)S(1)}, bf16[128,1536]{1,0:T(8,128)(2,1)S(1)}, u32[]{:S(2)}, u32[]{:S(2)}) collective-permute-start(bf16[128,1536]{1,0:T(8,128)(2,1)S(1)} %get-tuple-element.16), channel_id=1, source_target_pairs={{0,64},{16,976},{32,96},{48,1008},{64,128},{80,16},{96,160},{112,4... | collective-permute-start | bytes 1179656 | tf_op jit(solution)/shard_map/ppermute | solution.py:167
  62.5 16.3 %collective-permute-start.2 = (bf16[32,1536]{1,0:T(8,128)(2,1)S(1)}, bf16[32,1536]{1,0:T(8,128)(2,1)S(1)}, u32[]{:S(2)}, u32[]{:S(2)}) collective-permute-start(bf16[32,1536]{1,0:T(8,128)(2,1)S(1)} %add_convert_fusion.after_ref), channel_id=1, source_target_pairs={{0,128},{16,912},{32,160},{48,944},{64,192},{80,976},{96,224},{112... | collective-permute-start | bytes 294920 | tf_op jit(solution)/shard_map/ppermute | solution.py:167
  78.8 12.8 %collective-permute-start.5 = (bf16[32,1536]{1,0:T(8,128)(2,1)S(1)}, bf16[32,1536]{1,0:T(8,128)(2,1)S(1)}, u32[]{:S(2)}, u32[]{:S(2)}) collective-permute-start(bf16[32,1536]{1,0:T(8,128)(2,1)S(1)} %fusion.2), channel_id=1, source_target_pairs={{0,128},{16,912},{32,160},{48,944},{64,192},{80,976},{96,224},{112... | collective-permute-start | bytes 294920 | tf_op jit(solution)/shard_map/ppermute | solution.py:167
  87.9 26.7 %copy-start.2 = (s32[128,4]{0,1:T(4,128)S(1)}, s32[128,4]{0,1:T(4,128)}, u32[]{:S(2)}) copy-start(s32[128,4]{0,1:T(4,128)} %param.12) | copy-start | bytes 6148
  87.9 26.7 %copy-start.4 = (s32[128]{0:T(128)S(1)}, s32[128]{0:T(128)}, u32[]{:S(2)}) copy-start(s32[128]{0:T(128)} %param.13) | copy-start | bytes 1540
  87.9 24.7 %all-to-all-start.1 = ((bf16[16,32,1024]{2,1,0:T(8,128)(2,1)}), bf16[16,32,1024]{2,1,0:T(8,128)(2,1)S(1)}, u32[]{:S(2)}, u32[]{:S(2)}) async-start(bf16[16,32,1024]{2,1,0:T(8,128)(2,1)} %bitcast.8), calls=%async_computation.1 | async-start | bytes 2097152 | tf_op jit(solution)/shard_map/all_to_all | solution.py:243
  91.6 10.4 %collective-permute-start.6 = (bf16[32,1536]{1,0:T(8,128)(2,1)S(1)}, bf16[32,1536]{1,0:T(8,128)(2,1)S(1)}, u32[]{:S(2)}, u32[]{:S(2)}) collective-permute-start(bf16[32,1536]{1,0:T(8,128)(2,1)S(1)} %fusion.1), channel_id=1, source_target_pairs={{0,128},{16,912},{32,160},{48,944},{64,192},{80,976},{96,224},{112... | collective-permute-start | bytes 294920 | tf_op jit(solution)/shard_map/ppermute | solution.py:167
  102.0 10.6 %collective-permute-start.7 = (bf16[32,1536]{1,0:T(8,128)(2,1)S(1)}, bf16[32,1536]{1,0:T(8,128)(2,1)S(1)}, u32[]{:S(2)}, u32[]{:S(2)}) collective-permute-start(bf16[32,1536]{1,0:T(8,128)(2,1)S(1)} %fusion), channel_id=1, source_target_pairs={{0,128},{16,912},{32,160},{48,944},{64,192},{80,976},{96,224},{112... | collective-permute-start | bytes 294920 | tf_op jit(solution)/shard_map/ppermute | solution.py:167
  112.7 3.1 %collective-permute-start.8 = (bf16[16,1536]{1,0:T(8,128)(2,1)S(1)}, bf16[16,1536]{1,0:T(8,128)(2,1)S(1)}, u32[]{:S(2)}, u32[]{:S(2)}) collective-permute-start(bf16[16,1536]{1,0:T(8,128)(2,1)S(1)} %select_convert_fusion), channel_id=1, source_target_pairs={{0,16},{16,0},{32,48},{48,32},{64,80},{80,64},{96,112},{112,96},{1... | collective-permute-start | bytes 147464 | tf_op jit(solution)/shard_map/ppermute | solution.py:170

commit v8 on v7

--- a/solution.py
+++ b/solution.py
@@ -9,7 +9,7 @@
 
 FAN = 4
 TIE = 4
-BLOCKS = 4
+BLOCKS = 8
 
 
 def iota(shape, dim):
@@ -85,7 +85,12 @@
     ff = gate_ref.shape[1]
     width = arrived_ref.shape[1]
     half = width // 2
-    gate_in, up_in, grad_in = fetch([(gate_hbm, gate_ref), (up_hbm, up_ref), (grad_hbm, grad_ref)], sems)
+    top, low = pl.ds(0, half), pl.ds(half, half)
+    gate_in, gate_too, up_in, up_too, grad_in = fetch(
+        [(w.at[part], v.at[part]) for w, v in ((gate_hbm, gate_ref), (up_hbm, up_ref)) for part in (top, low)]
+        + [(grad_hbm, grad_ref)],
+        sems,
+    )
     marks = slot_marks(chosen_ref[...], sources, cap, tokens)
     rows = contract(marks, arrived_ref[...], ((0,), (0,))).astype(jnp.bfloat16)
     pick = (iota((width, width), 0) == order_ref[...]).astype(jnp.float32).astype(jnp.bfloat16)
@@ -93,8 +98,10 @@
     mine_ref[...] = ordered[:, :half]
     send_ref[:, :half] = ordered[:, half:]
     gate_in.wait()
+    gate_too.wait()
     gate = jnp.dot(rows, gate_ref[...], preferred_element_type=jnp.float32)
     up_in.wait()
+    up_too.wait()
     up = jnp.dot(rows, up_ref[...], preferred_element_type=jnp.float32)
     squash = jax.nn.sigmoid(gate)
     grad_in.wait()
@@ -206,7 +213,7 @@
         [((slots, half), bf16), ((slots, half + 2 * ff), bf16)],
         arrived, picked, order, gate, up, hidden_grad[0, 0],
         ins=[None] * 3 + [hbm] * 3,
-        scratch=[vmem(a.shape, bf16) for a in (gate, up, hidden_grad[0, 0])] + [dma((3,))],
+        scratch=[vmem(a.shape, bf16) for a in (gate, up, hidden_grad[0, 0])] + [dma((5,))],
         mib=50,
     )
     got = swap(send)

time: 117 us -> 117 us (level)
  transfers between devices with their start and end apart: 11 -> 11, of which waited for: 5 -> 5; matrix products, arithmetic and copies ran while one was open for 0% -> 0% of each run, Pallas kernels for 4% -> 5%
where the time goes in v8:
time: 117 us
  starting transfers between devices  68.9 us (59%)
  waiting for transfers between devices  33.6 us (29%)
  Pallas kernels  12.1 us (10%)
    ppermute x7, starting transfers between devices, along(): return lax.ppermute(value, 'dp', pairs)  42.5 us
    ppermute x7, waiting for transfers between devices, along(): return lax.ppermute(value, 'dp', pairs)  21.5 us
    ppermute x2, starting transfers between devices, swap(): return lax.ppermute(value, 'dp', [(d, d ^ 1) for d in range(groups)])  15.2 us
    all_to_all x1, waiting for transfers between devices, on_device(): lax.all_to_all(outgoing.reshape(peers, cap, width), 'expert', split_axis=...  12.1 us
    pallas_call x6, Pallas kernels, call(): pl.pallas_call(kernel, in_specs=[pl.BlockSpec(memory_space=s) for s in sp...  12.1 us
    all_to_all x1, starting transfers between devices, on_device(): lax.all_to_all(outgoing.reshape(peers, cap, width), 'expert', split_axis=...  7.6 us
    all_to_all x1, starting transfers between devices, on_device(): lax.all_to_all(back.reshape(peers, cap, width), 'expert', split_axis=0, c...  3.66 us
  transfers between devices with their start and end apart: 11, of which 5 were waited for; matrix products, arithmetic and copies ran while one was open for 0% of the time, Pallas kernels for 5%

profile of v8, /device:TPU:1, one launch (start us, length us, event | category | flops | bytes accessed | tf_op | source)
XLA Modules:
  0.0 116.7 jit_solution(6811807942512168711)
XLA Ops:
  0.6 0.0 copy-start.1
  0.6 0.0 copy-start.3
  0.7 2.3 %shard_map.94 = bf16[512,1024]{1,0:T(8,128)(2,1)} custom-call(bf16[128,1024]{1,0:T(8,128)(2,1)} %tokens_hbm.1, s32[4,128]{1,0:T(4,128)} %bitcast.19, s32[1,128]{1,0:T(1,128)} %bitcast.23), custom_call_target="tpu_custom_call" | custom-call | tf_op jit(solution)/shard_map/pallas_call | solution.py:149
  2.9 7.6 %all-to-all-start = ((bf16[16,32,1024]{2,1,0:T(8,128)(2,1)}), bf16[16,32,1024]{2,1,0:T(8,128)(2,1)S(1)}, u32[]{:S(2)}, u32[]{:S(2)}) async-start(bf16[16,32,1024]{2,1,0:T(8,128)(2,1)} %bitcast.27), calls=%async_computation | async-start | bytes 2097152 | tf_op jit(solution)/shard_map/all_to_all | solution.py:199
  10.6 0.1 fusion.3.order_ref
  10.6 12.1 %all-to-all-done = bf16[16,32,1024]{2,1,0:T(8,128)(2,1)S(1)} async-done(((bf16[16,32,1024]{2,1,0:T(8,128)(2,1)}), bf16[16,32,1024]{2,1,0:T(8,128)(2,1)S(1)}, u32[]{:S(2)}, u32[]{:S(2)}) %all-to-all-start) | async-done | bytes 1048608 | tf_op jit(solution)/shard_map/all_to_all | solution.py:199
  22.7 0.0 copy-done.1
  22.7 0.0 copy-done.3
  22.7 0.0 copy-start
  22.7 3.3 %shard_map.95 = (bf16[256,512]{1,0:T(8,128)(2,1)S(1)}, bf16[256,2048]{1,0:T(8,128)(2,1)S(1)}) custom-call(bf16[512,1024]{1,0:T(8,128)(2,1)S(1)} %bitcast.17, s32[1,256]{1,0:T(1,128)S(1)} %bitcast.21, s32[1,1024]{1,0:T(1,128)S(1)} %fusion.3.order_ref, bf16[1024,768]{1,0:T(8,128)(2,1)} %bitcast.14, bf16[1024,768]{1,0:T(8,128)(2,1)} %bitcast.25, ...), custom_call_target="tpu_custom_call" | custom-call | tf_op jit(solution)/shard_map/pallas_call | solution.py:149
  26.1 13.2 %collective-permute-start = (bf16[256,2048]{1,0:T(8,128)(2,1)S(1)}, bf16[256,2048]{1,0:T(8,128)(2,1)S(1)}, u32[]{:S(2)}, u32[]{:S(2)}) collective-permute-start(bf16[256,2048]{1,0:T(8,128)(2,1)S(1)} %get-tuple-element.12.send_ref), channel_id=1, source_target_pairs={{0,16},{16,0},{32,48},{48,32},{64,80},{80,64},{96,112},{112,96},{1... | collective-permute-start | bytes 3145736 | tf_op jit(solution)/shard_map/ppermute | solution.py:177
  39.3 0.0 copy-done
  39.3 2.5 %shard_map.96.after_ref.grad_ref = bf16[256,1024]{1,0:T(8,128)(2,1)S(1)} custom-call(bf16[256,2048]{1,0:T(8,128)(2,1)S(1)} %get-tuple-element.12.send_ref, bf16[1024,768]{1,0:T(8,128)(2,1)S(1)} %bitcast.15, bf16[1024,768]{1,0:T(8,128)(2,1)} %bitcast.26), custom_call_target="tpu_custom_call" | custom-call | tf_op jit(solution)/shard_map/pallas_call | solution.py:149
  41.9 0.0 collective-permute-done.got_ref
  41.9 1.0 shard_map.97
  42.9 1.9 %collective-permute-start.1 = (bf16[128,1536]{1,0:T(8,128)(2,1)S(1)}, bf16[128,1536]{1,0:T(8,128)(2,1)S(1)}, u32[]{:S(2)}, u32[]{:S(2)}) collective-permute-start(bf16[128,1536]{1,0:T(8,128)(2,1)S(1)} %get-tuple-element.13), channel_id=1, source_target_pairs={{0,992},{16,48},{32,0},{48,80},{64,32},{80,112},{96,64},{112,144},... | collective-permute-start | bytes 1179656 | tf_op jit(solution)/shard_map/ppermute | solution.py:174
  44.9 13.5 %collective-permute-start.3 = (bf16[128,1536]{1,0:T(8,128)(2,1)S(1)}, bf16[128,1536]{1,0:T(8,128)(2,1)S(1)}, u32[]{:S(2)}, u32[]{:S(2)}) collective-permute-start(bf16[128,1536]{1,0:T(8,128)(2,1)S(1)} %get-tuple-element.15), channel_id=1, source_target_pairs={{0,32},{16,1008},{32,64},{48,16},{64,96},{80,48},{96,128},{112,80}... | collective-permute-start | bytes 1179656 | tf_op jit(solution)/shard_map/ppermute | solution.py:174
  58.3 3.8 %collective-permute-start.4 = (bf16[128,1536]{1,0:T(8,128)(2,1)S(1)}, bf16[128,1536]{1,0:T(8,128)(2,1)S(1)}, u32[]{:S(2)}, u32[]{:S(2)}) collective-permute-start(bf16[128,1536]{1,0:T(8,128)(2,1)S(1)} %get-tuple-element.16), channel_id=1, source_target_pairs={{0,64},{16,976},{32,96},{48,1008},{64,128},{80,16},{96,160},{112,4... | collective-permute-start | bytes 1179656 | tf_op jit(solution)/shard_map/ppermute | solution.py:174
  62.2 0.0 collective-permute-done.1
  62.2 5.3 %collective-permute-start.2 = (bf16[32,1536]{1,0:T(8,128)(2,1)S(1)}, bf16[32,1536]{1,0:T(8,128)(2,1)S(1)}, u32[]{:S(2)}, u32[]{:S(2)}) collective-permute-start(bf16[32,1536]{1,0:T(8,128)(2,1)S(1)} %add_convert_fusion.after_ref), channel_id=1, source_target_pairs={{0,128},{16,912},{32,160},{48,944},{64,192},{80,976},{96,224},{112... | collective-permute-start | bytes 294920 | tf_op jit(solution)/shard_map/ppermute | solution.py:174
  67.5 0.0 collective-permute-done.3
  67.5 9.9 %collective-permute-done.4 = bf16[128,1536]{1,0:T(8,128)(2,1)S(1)} collective-permute-done((bf16[128,1536]{1,0:T(8,128)(2,1)S(1)}, bf16[128,1536]{1,0:T(8,128)(2,1)S(1)}, u32[]{:S(2)}, u32[]{:S(2)}) %collective-permute-start.4) | collective-permute-done | bytes 393248 | tf_op jit(solution)/shard_map/ppermute | solution.py:174
  77.4 0.3 convert_add_fusion
  77.7 0.7 collective-permute-done.2
  78.5 7.7 %collective-permute-start.5 = (bf16[32,1536]{1,0:T(8,128)(2,1)S(1)}, bf16[32,1536]{1,0:T(8,128)(2,1)S(1)}, u32[]{:S(2)}, u32[]{:S(2)}) collective-permute-start(bf16[32,1536]{1,0:T(8,128)(2,1)S(1)} %fusion.2), channel_id=1, source_target_pairs={{0,128},{16,912},{32,160},{48,944},{64,192},{80,976},{96,224},{112... | collective-permute-start | bytes 294920 | tf_op jit(solution)/shard_map/ppermute | solution.py:174
  86.2 1.7 %shard_map.98 = bf16[512,1024]{1,0:T(8,128)(2,1)} custom-call(s32[1,256]{1,0:T(1,128)S(1)} %bitcast.22, bf16[256,1024]{1,0:T(8,128)(2,1)S(1)} %shard_map.96.after_ref.grad_ref, bf16[32,1536]{1,0:T(8,128)(2,1)S(1)} %add_convert_fusion.after_ref), custom_call_target="tpu_custom_call" | custom-call | tf_op jit(solution)/shard_map/pallas_call | solution.py:149
  88.0 0.0 copy-start.2
  88.0 0.0 copy-start.4
  88.0 3.7 %all-to-all-start.1 = ((bf16[16,32,1024]{2,1,0:T(8,128)(2,1)}), bf16[16,32,1024]{2,1,0:T(8,128)(2,1)S(1)}, u32[]{:S(2)}, u32[]{:S(2)}) async-start(bf16[16,32,1024]{2,1,0:T(8,128)(2,1)} %bitcast.8), calls=%async_computation.1 | async-start | bytes 2097152 | tf_op jit(solution)/shard_map/all_to_all | solution.py:250
  91.7 0.0 collective-permute-done.5
  91.7 5.2 %collective-permute-start.6 = (bf16[32,1536]{1,0:T(8,128)(2,1)S(1)}, bf16[32,1536]{1,0:T(8,128)(2,1)S(1)}, u32[]{:S(2)}, u32[]{:S(2)}) collective-permute-start(bf16[32,1536]{1,0:T(8,128)(2,1)S(1)} %fusion.1), channel_id=1, source_target_pairs={{0,128},{16,912},{32,160},{48,944},{64,192},{80,976},{96,224},{112... | collective-permute-start | bytes 294920 | tf_op jit(solution)/shard_map/ppermute | solution.py:174
  96.9 5.2 %collective-permute-done.6 = bf16[32,1536]{1,0:T(8,128)(2,1)S(1)} collective-permute-done((bf16[32,1536]{1,0:T(8,128)(2,1)S(1)}, bf16[32,1536]{1,0:T(8,128)(2,1)S(1)}, u32[]{:S(2)}, u32[]{:S(2)}) %collective-permute-start.6) | collective-permute-done | bytes 98336 | tf_op jit(solution)/shard_map/ppermute | solution.py:174
  102.1 5.1 %collective-permute-start.7 = (bf16[32,1536]{1,0:T(8,128)(2,1)S(1)}, bf16[32,1536]{1,0:T(8,128)(2,1)S(1)}, u32[]{:S(2)}, u32[]{:S(2)}) collective-permute-start(bf16[32,1536]{1,0:T(8,128)(2,1)S(1)} %fusion), channel_id=1, source_target_pairs={{0,128},{16,912},{32,160},{48,944},{64,192},{80,976},{96,224},{112... | collective-permute-start | bytes 294920 | tf_op jit(solution)/shard_map/ppermute | solution.py:174
  107.2 5.7 %collective-permute-done.7 = bf16[32,1536]{1,0:T(8,128)(2,1)S(1)} collective-permute-done((bf16[32,1536]{1,0:T(8,128)(2,1)S(1)}, bf16[32,1536]{1,0:T(8,128)(2,1)S(1)}, u32[]{:S(2)}, u32[]{:S(2)}) %collective-permute-start.7) | collective-permute-done | bytes 98336 | tf_op jit(solution)/shard_map/ppermute | solution.py:174
  112.9 0.0 all-to-all-done.1
  112.9 1.9 %collective-permute-start.8 = (bf16[16,1536]{1,0:T(8,128)(2,1)S(1)}, bf16[16,1536]{1,0:T(8,128)(2,1)S(1)}, u32[]{:S(2)}, u32[]{:S(2)}) collective-permute-start(bf16[16,1536]{1,0:T(8,128)(2,1)S(1)} %select_convert_fusion), channel_id=1, source_target_pairs={{0,16},{16,0},{32,48},{48,32},{64,80},{80,64},{96,112},{112,96},{1... | collective-permute-start | bytes 147464 | tf_op jit(solution)/shard_map/ppermute | solution.py:177
  114.8 0.0 copy-done.2
  114.9 0.0 copy-done.4
  114.9 1.2 %shard_map.99 = bf16[128,1024]{1,0:T(8,128)(2,1)} custom-call(bf16[512,1024]{1,0:T(8,128)(2,1)S(1)} %bitcast.16, s32[4,128]{1,0:T(4,128)S(1)} %bitcast.20, s32[1,128]{1,0:T(1,128)S(1)} %bitcast.24), custom_call_target="tpu_custom_call" | custom-call | tf_op jit(solution)/shard_map/pallas_call | solution.py:149
  116.1 0.0 collective-permute-done.8
  116.1 0.6 slice_bitcast_fusion
  (8 shorter events, 0.2 us)
Async XLA Ops:
  0.6 22.1 %copy-start.1 = (bf16[1,1,256,768]{3,2,1,0:T(8,128)(2,1)S(1)}, bf16[1,1,256,768]{3,2,1,0:T(8,128)(2,1)}, u32[]{:S(2)}) copy-start(bf16[1,1,256,768]{3,2,1,0:T(8,128)(2,1)} %param.10) | copy-start | bytes 1179652
  0.6 22.1 %copy-start.3 = (s32[1,1,256]{2,1,0:T(1,128)S(1)}, s32[1,1,256]{2,1,0:T(1,128)}, u32[]{:S(2)}) copy-start(s32[1,1,256]{2,1,0:T(1,128)} %param.11) | copy-start | bytes 3076
  2.9 19.8 %all-to-all-start = ((bf16[16,32,1024]{2,1,0:T(8,128)(2,1)}), bf16[16,32,1024]{2,1,0:T(8,128)(2,1)S(1)}, u32[]{:S(2)}, u32[]{:S(2)}) async-start(bf16[16,32,1024]{2,1,0:T(8,128)(2,1)} %bitcast.27), calls=%async_computation | async-start | bytes 2097152 | tf_op jit(solution)/shard_map/all_to_all | solution.py:199
  22.7 16.6 %copy-start = (bf16[1,1024,768]{2,1,0:T(8,128)(2,1)S(1)}, bf16[1,1024,768]{2,1,0:T(8,128)(2,1)}, u32[]{:S(2)}) copy-start(bf16[1,1024,768]{2,1,0:T(8,128)(2,1)} %param.8) | copy-start | bytes 4718596
  26.1 15.8 %collective-permute-start = (bf16[256,2048]{1,0:T(8,128)(2,1)S(1)}, bf16[256,2048]{1,0:T(8,128)(2,1)S(1)}, u32[]{:S(2)}, u32[]{:S(2)}) collective-permute-start(bf16[256,2048]{1,0:T(8,128)(2,1)S(1)} %get-tuple-element.12.send_ref), channel_id=1, source_target_pairs={{0,16},{16,0},{32,48},{48,32},{64,80},{80,64},{96,112},{112,96},{1... | collective-permute-start | bytes 3145736 | tf_op jit(solution)/shard_map/ppermute | solution.py:177
  42.9 19.2 %collective-permute-start.1 = (bf16[128,1536]{1,0:T(8,128)(2,1)S(1)}, bf16[128,1536]{1,0:T(8,128)(2,1)S(1)}, u32[]{:S(2)}, u32[]{:S(2)}) collective-permute-start(bf16[128,1536]{1,0:T(8,128)(2,1)S(1)} %get-tuple-element.13), channel_id=1, source_target_pairs={{0,992},{16,48},{32,0},{48,80},{64,32},{80,112},{96,64},{112,144},... | collective-permute-start | bytes 1179656 | tf_op jit(solution)/shard_map/ppermute | solution.py:174
  44.9 22.6 %collective-permute-start.3 = (bf16[128,1536]{1,0:T(8,128)(2,1)S(1)}, bf16[128,1536]{1,0:T(8,128)(2,1)S(1)}, u32[]{:S(2)}, u32[]{:S(2)}) collective-permute-start(bf16[128,1536]{1,0:T(8,128)(2,1)S(1)} %get-tuple-element.15), channel_id=1, source_target_pairs={{0,32},{16,1008},{32,64},{48,16},{64,96},{80,48},{96,128},{112,80}... | collective-permute-start | bytes 1179656 | tf_op jit(solution)/shard_map/ppermute | solution.py:174
  58.3 19.1 %collective-permute-start.4 = (bf16[128,1536]{1,0:T(8,128)(2,1)S(1)}, bf16[128,1536]{1,0:T(8,128)(2,1)S(1)}, u32[]{:S(2)}, u32[]{:S(2)}) collective-permute-start(bf16[128,1536]{1,0:T(8,128)(2,1)S(1)} %get-tuple-element.16), channel_id=1, source_target_pairs={{0,64},{16,976},{32,96},{48,1008},{64,128},{80,16},{96,160},{112,4... | collective-permute-start | bytes 1179656 | tf_op jit(solution)/shard_map/ppermute | solution.py:174
  62.2 16.3 %collective-permute-start.2 = (bf16[32,1536]{1,0:T(8,128)(2,1)S(1)}, bf16[32,1536]{1,0:T(8,128)(2,1)S(1)}, u32[]{:S(2)}, u32[]{:S(2)}) collective-permute-start(bf16[32,1536]{1,0:T(8,128)(2,1)S(1)} %add_convert_fusion.after_ref), channel_id=1, source_target_pairs={{0,128},{16,912},{32,160},{48,944},{64,192},{80,976},{96,224},{112... | collective-permute-start | bytes 294920 | tf_op jit(solution)/shard_map/ppermute | solution.py:174
  78.5 13.2 %collective-permute-start.5 = (bf16[32,1536]{1,0:T(8,128)(2,1)S(1)}, bf16[32,1536]{1,0:T(8,128)(2,1)S(1)}, u32[]{:S(2)}, u32[]{:S(2)}) collective-permute-start(bf16[32,1536]{1,0:T(8,128)(2,1)S(1)} %fusion.2), channel_id=1, source_target_pairs={{0,128},{16,912},{32,160},{48,944},{64,192},{80,976},{96,224},{112... | collective-permute-start | bytes 294920 | tf_op jit(solution)/shard_map/ppermute | solution.py:174
  88.0 26.9 %copy-start.2 = (s32[128,4]{0,1:T(4,128)S(1)}, s32[128,4]{0,1:T(4,128)}, u32[]{:S(2)}) copy-start(s32[128,4]{0,1:T(4,128)} %param.12) | copy-start | bytes 6148
  88.0 26.9 %copy-start.4 = (s32[128]{0:T(128)S(1)}, s32[128]{0:T(128)}, u32[]{:S(2)}) copy-start(s32[128]{0:T(128)} %param.13) | copy-start | bytes 1540
  88.0 24.9 %all-to-all-start.1 = ((bf16[16,32,1024]{2,1,0:T(8,128)(2,1)}), bf16[16,32,1024]{2,1,0:T(8,128)(2,1)S(1)}, u32[]{:S(2)}, u32[]{:S(2)}) async-start(bf16[16,32,1024]{2,1,0:T(8,128)(2,1)} %bitcast.8), calls=%async_computation.1 | async-start | bytes 2097152 | tf_op jit(solution)/shard_map/all_to_all | solution.py:250
  91.7 10.4 %collective-permute-start.6 = (bf16[32,1536]{1,0:T(8,128)(2,1)S(1)}, bf16[32,1536]{1,0:T(8,128)(2,1)S(1)}, u32[]{:S(2)}, u32[]{:S(2)}) collective-permute-start(bf16[32,1536]{1,0:T(8,128)(2,1)S(1)} %fusion.1), channel_id=1, source_target_pairs={{0,128},{16,912},{32,160},{48,944},{64,192},{80,976},{96,224},{112... | collective-permute-start | bytes 294920 | tf_op jit(solution)/shard_map/ppermute | solution.py:174
  102.1 10.8 %collective-permute-start.7 = (bf16[32,1536]{1,0:T(8,128)(2,1)S(1)}, bf16[32,1536]{1,0:T(8,128)(2,1)S(1)}, u32[]{:S(2)}, u32[]{:S(2)}) collective-permute-start(bf16[32,1536]{1,0:T(8,128)(2,1)S(1)} %fusion), channel_id=1, source_target_pairs={{0,128},{16,912},{32,160},{48,944},{64,192},{80,976},{96,224},{112... | collective-permute-start | bytes 294920 | tf_op jit(solution)/shard_map/ppermute | solution.py:174
  112.9 3.1 %collective-permute-start.8 = (bf16[16,1536]{1,0:T(8,128)(2,1)S(1)}, bf16[16,1536]{1,0:T(8,128)(2,1)S(1)}, u32[]{:S(2)}, u32[]{:S(2)}) collective-permute-start(bf16[16,1536]{1,0:T(8,128)(2,1)S(1)} %select_convert_fusion), channel_id=1, source_target_pairs={{0,16},{16,0},{32,48},{48,32},{64,80},{80,64},{96,112},{112,96},{1... | collective-permute-start | bytes 147464 | tf_op jit(solution)/shard_map/ppermute | solution.py:177
